TPU v7x, 32 devices: a whole 2x2x4 slice. The times are simulated.
32 devices in a mesh: groups: 2 (over x), render: 4 (over y, core), view: 4 (over z).
Axes of the slice: x: 2, y: 2, z: 4, core: 2. Of those that a mesh axis runs over, the one named last changes fastest.
Arguments:
- params: float32 [59, 32768], P(None, ('groups', 'render')), parts along dimension 1, may hold values from -6 to 1.5, as said below
- cameras: float32 [32, 7], P(('groups', 'view')), parts along dimension 0, may hold values from -0.2 to 170, as said below
- send_index: int32 [8, 4, 4, 512], P(('groups', 'render'), 'view'), parts along dimension 0, may hold values from 0 to 4095, as said below
- tile_id: int32 [8, 4, 8], P(('groups', 'render'), 'view'), parts along dimension 0, may hold values from 0 to 15
- tile_count: int32 [8, 4, 8], P(('groups', 'render'), 'view'), parts along dimension 0, may hold values from 1 to 512, as said below
- tile_slot: int32 [8, 4, 8, 512], P(('groups', 'render'), 'view'), parts along dimension 0, may hold values from 0 to 2047, as said below
- targets: float32 [8, 4, 8, 3, 256], P(('groups', 'render'), 'view'), parts along dimension 0, may hold values from 0 to 1
Outputs:
- image: float32 [8, 4, 8, 3, 256], P(('groups', 'render'), 'view'), parts along dimension 0
- gradients: float32 [59, 32768], P(None, ('groups', 'render', 'view')), parts along dimension 1
There are 2 independent parts, one for each index of `groups`. A program takes and returns all parts, laid end to end along the dimension named above; each array names one. Nothing has to cross between parts.
Inputs may be any that keep to these rules, and one draw needn't show every extreme that they name: `params`: row ranges: 0-2 in -0.1 to 0.1, 3-5 in log 0.2 to log 0.6, 6 in 0.5 to 1.5, 7-9 in -1 to 1, 10 in -6 to -4, colour rows of basis index 0 in -1 to 1, the others in -0.5 to 0.5. `cameras`: columns 0-2 in -0.2 to 0.2, 3-4 in -0.05 to 0.05, 5 in 3.5 to 4.5, 6 in 130 to 170. `send_index`: the 512 rows of one slab, view column and renderer are distinct. `tile_count`: every device has a tile with exactly 512 live entries. `tile_slot`: the 512 entries of one tile are distinct.
All inputs are finite; a program needn't handle non-finite values.
Results may differ from a plain program's by a relative error of at most 0.0003.
Values sent between devices are 32-bit elements; how exact they have to be, the bound alone decides.
No kernel may reach another device: no remote copies, remote signals or barrier semaphores. Data moves between devices by JAX's collectives and lax.ppermute only.
A program may use at most 64 MiB of HBM per device.

v0:
```python
from functools import partial

import jax
import jax.numpy as jnp
from jax import lax
from jax.sharding import PartitionSpec as P

CROP = 2


dilation = 0.3
backdrop = 1.0
band_zero = 0.28209479177387814
band_one = 0.4886025119029199
band_two = [
    1.0925484305920792,
    -1.0925484305920792,
    0.31539156525252005,
    -1.0925484305920792,
    0.5462742152960396,
]
band_three = [
    -0.5900435899266435,
    2.890611442640554,
    -0.4570457994644658,
    0.3731763325901154,
    -0.4570457994644658,
    1.445305721320277,
    -0.5900435899266435,
]


def harmonic_basis(direction):
    along_x, along_y, along_z = (direction[0], direction[1], direction[2])
    square_x = along_x * along_x
    square_y = along_y * along_y
    square_z = along_z * along_z
    constant = band_zero + 0.0 * along_x
    return [
        constant,
        -band_one * along_y,
        band_one * along_z,
        -band_one * along_x,
        band_two[0] * along_x * along_y,
        band_two[1] * along_y * along_z,
        band_two[2] * (2.0 * square_z - square_x - square_y),
        band_two[3] * along_x * along_z,
        band_two[4] * (square_x - square_y),
        band_three[0] * along_y * (3.0 * square_x - square_y),
        band_three[1] * along_x * along_y * along_z,
        band_three[2] * along_y * (4.0 * square_z - square_x - square_y),
        band_three[3] * along_z * (2.0 * square_z - 3.0 * square_x - 3.0 * square_y),
        band_three[4] * along_x * (4.0 * square_z - square_x - square_y),
        band_three[5] * along_z * (square_x - square_y),
        band_three[6] * along_x * (square_x - 3.0 * square_y),
    ]


def project(raw_rows, frame):
    position = [raw_rows[0], raw_rows[1], raw_rows[2]]
    extent = [jnp.exp(raw_rows[3]), jnp.exp(raw_rows[4]), jnp.exp(raw_rows[5])]
    quat_raw = [raw_rows[6], raw_rows[7], raw_rows[8], raw_rows[9]]
    quat_norm = jnp.sqrt(sum((member * member for member in quat_raw)))
    quat = [member / quat_norm for member in quat_raw]
    opacity = jax.nn.sigmoid(raw_rows[10])
    cosine = [jnp.cos(frame[0]), jnp.cos(frame[1]), jnp.cos(frame[2])]
    sine = [jnp.sin(frame[0]), jnp.sin(frame[1]), jnp.sin(frame[2])]
    rotation = [
        [
            cosine[1] * cosine[2],
            sine[0] * sine[1] * cosine[2] - cosine[0] * sine[2],
            cosine[0] * sine[1] * cosine[2] + sine[0] * sine[2],
        ],
        [
            cosine[1] * sine[2],
            sine[0] * sine[1] * sine[2] + cosine[0] * cosine[2],
            cosine[0] * sine[1] * sine[2] - sine[0] * cosine[2],
        ],
        [-sine[1], sine[0] * cosine[1], cosine[0] * cosine[1]],
    ]
    camera_pt = [
        rotation[across][0] * position[0]
        + rotation[across][1] * position[1]
        + rotation[across][2] * position[2]
        + frame[3 + across]
        for across in range(3)
    ]
    inv_depth = 1.0 / camera_pt[2]
    focal = frame[6]
    centre = CROP * 8.0
    screen_u = focal * camera_pt[0] * inv_depth + centre
    screen_v = focal * camera_pt[1] * inv_depth + centre
    quat_rot = [
        [
            1.0 - 2.0 * (quat[2] * quat[2] + quat[3] * quat[3]),
            2.0 * (quat[1] * quat[2] - quat[0] * quat[3]),
            2.0 * (quat[1] * quat[3] + quat[0] * quat[2]),
        ],
        [
            2.0 * (quat[1] * quat[2] + quat[0] * quat[3]),
            1.0 - 2.0 * (quat[1] * quat[1] + quat[3] * quat[3]),
            2.0 * (quat[2] * quat[3] - quat[0] * quat[1]),
        ],
        [
            2.0 * (quat[1] * quat[3] - quat[0] * quat[2]),
            2.0 * (quat[2] * quat[3] + quat[0] * quat[1]),
            1.0 - 2.0 * (quat[1] * quat[1] + quat[2] * quat[2]),
        ],
    ]
    spread = [
        [quat_rot[across][within] * extent[within] for within in range(3)] for across in range(3)
    ]
    depth_term = [
        focal * camera_pt[0] * inv_depth * inv_depth,
        focal * camera_pt[1] * inv_depth * inv_depth,
    ]
    screen_rot = [
        [
            focal * inv_depth * rotation[across][within] - depth_term[across] * rotation[2][within]
            for within in range(3)
        ]
        for across in range(2)
    ]
    footprint = [
        [
            sum((screen_rot[across][middle] * spread[middle][within] for middle in range(3)))
            for within in range(3)
        ]
        for across in range(2)
    ]
    cov_a = sum((footprint[0][within] * footprint[0][within] for within in range(3))) + dilation
    cov_b = sum((footprint[0][within] * footprint[1][within] for within in range(3)))
    cov_c = sum((footprint[1][within] * footprint[1][within] for within in range(3))) + dilation
    determinant = cov_a * cov_c - cov_b * cov_b
    conic_a = cov_c / determinant
    conic_b = -cov_b / determinant
    conic_c = cov_a / determinant
    distance = jnp.sqrt(sum((member * member for member in camera_pt)))
    direction = [
        sum((rotation[middle][across] * camera_pt[middle] for middle in range(3))) / distance
        for across in range(3)
    ]
    basis = harmonic_basis(direction)
    colour = [
        0.5 + sum((basis[level] * raw_rows[11 + 16 * channel + level] for level in range(16)))
        for channel in range(3)
    ]
    pieces = jnp.broadcast_arrays(
        screen_u, screen_v, conic_a, conic_b, conic_c, colour[0], colour[1], colour[2], opacity
    )
    return jnp.stack(pieces)


def exclusive_sum(strict_lower, log_keep):
    return jnp.dot(strict_lower, log_keep, precision=lax.Precision.HIGHEST)


def blend_tile(tile_feat, tile_code, live_count, prefix):
    list_len = tile_feat.shape[1]
    crop_cell = tile_code % (CROP * CROP)
    tile_row = crop_cell // CROP
    tile_col = crop_cell % CROP
    pixel = jnp.arange(256, dtype=jnp.int32)
    pixel_x = (tile_col * 16 + pixel % 16).astype(jnp.float32) + 0.5
    pixel_y = (tile_row * 16 + pixel // 16).astype(jnp.float32) + 0.5
    offset_x = pixel_x[None, :] - tile_feat[0][:, None]
    offset_y = pixel_y[None, :] - tile_feat[1][:, None]
    power = (
        -0.5
        * (
            tile_feat[2][:, None] * offset_x * offset_x
            + tile_feat[4][:, None] * offset_y * offset_y
        )
        - tile_feat[3][:, None] * offset_x * offset_y
    )
    live = (jnp.arange(list_len, dtype=jnp.int32) < live_count).astype(jnp.float32)
    alpha = tile_feat[8][:, None] * jnp.exp(power) * live[:, None]
    log_keep = jnp.log1p(-alpha)
    before = prefix(log_keep)
    weight = jnp.exp(before) * alpha
    colour = jnp.dot(tile_feat[5:8], weight, precision=lax.Precision.HIGHEST)
    remain = jnp.exp(jnp.sum(log_keep, axis=0))
    return colour + backdrop * remain[None, :]


def body(params, cameras, send_index, tile_id, tile_count, tile_slot, targets):
    chosen_rows = send_index[0, 0].reshape(-1)
    entry_slot = tile_slot[0, 0]
    tile_codes = tile_id[0, 0]
    live_counts = tile_count[0, 0]
    wanted = targets[0, 0]
    views_here = cameras.shape[0]
    view_of = tile_codes // (CROP * CROP)
    list_len = entry_slot.shape[1]
    position = jnp.arange(list_len, dtype=jnp.int32)
    strict_lower = (position[None, :] < position[:, None]).astype(jnp.float32)
    prefix = partial(exclusive_sum, strict_lower)
    outgoing = params[:, chosen_rows]
    arrived = lax.all_to_all(outgoing, "render", split_axis=1, concat_axis=1, tiled=True)
    picked = arrived[:, entry_slot]
    lookup = (view_of[:, None] == jnp.arange(views_here, dtype=jnp.int32)[None, :]).astype(
        jnp.float32
    )
    tile_cams = jnp.dot(lookup, cameras, precision=lax.Precision.HIGHEST)

    def tile_work(inputs):
        raw_tile, frame, tile_code, live_count, target_tile = inputs

        def render(rows_in):
            return blend_tile(project(rows_in, frame[:, None]), tile_code, live_count, prefix)

        colour, pullback = jax.vjp(render, raw_tile)
        (grad_raw,) = pullback(colour - target_tile)
        return (colour, grad_raw)

    colours, grad_raws = lax.map(
        tile_work, (jnp.moveaxis(picked, 1, 0), tile_cams, tile_codes, live_counts, wanted)
    )
    returned = jnp.zeros_like(arrived).at[:, entry_slot].add(jnp.moveaxis(grad_raws, 0, 1))
    row_grads = lax.all_to_all(returned, "render", split_axis=1, concat_axis=1, tiled=True)
    owned = jnp.zeros_like(params).at[:, chosen_rows].add(row_grads)
    grad_part = lax.psum_scatter(owned, "view", scatter_dimension=1, tiled=True)
    return (colours[None, None], grad_part)


def solution(mesh):
    in_specs = (
        P(None, ("groups", "render")),
        P(("groups", "view"), None),
        P(("groups", "render"), "view", None, None),
        P(("groups", "render"), "view", None),
        P(("groups", "render"), "view", None),
        P(("groups", "render"), "view", None, None),
        P(("groups", "render"), "view", None, None, None),
    )
    out_specs = (
        P(("groups", "render"), "view", None, None, None),
        P(None, ("groups", "render", "view")),
    )
    return jax.shard_map(body, mesh=mesh, in_specs=in_specs, out_specs=out_specs, check_vma=False)
```

profile of v0, /device:TPU:0, one launch (start us, length us, event | category | flops | bytes accessed | tf_op | source)
XLA Modules:
  0.0 340.5 jit_solution(14163109705173550776)
XLA Ops:
  7.9 1.9 copy.31
  9.8 5.5 %gather_fusion = f32[2048,59]{1,0:T(8,128)S(1)} fusion(f32[59,4096]{0,1:T(8,128)S(1)} %copy.31, s32[2048]{0:T(1024)S(1)} %broadcast_clamp_fusion.1), kind=kCustom, calls=%fused_computation | custom fusion | bytes 974848 | tf_op jit(solution)/shard_map/gather | solution.py:198
  15.3 1.2 copy.32
  16.5 4.2 %all-to-all-start = ((f32[59,4,512]{2,0,1:T(8,128)}), f32[59,4,512]{2,0,1:T(8,128)S(1)}, u32[]{:S(2)}, u32[]{:S(2)}) async-start(f32[59,4,512]{2,0,1:T(8,128)} %copy.32), calls=%async_computation | async-start | bytes 1048576 | tf_op jit(solution)/shard_map/all_to_all | solution.py:199
  21.0 8.6 %all-to-all-done = f32[59,4,512]{2,0,1:T(8,128)S(1)} async-done(((f32[59,4,512]{2,0,1:T(8,128)}), f32[59,4,512]{2,0,1:T(8,128)S(1)}, u32[]{:S(2)}, u32[]{:S(2)}) %all-to-all-start) | async-done | bytes 483360 | tf_op jit(solution)/shard_map/all_to_all | solution.py:199
  29.9 10.8 %gather_fusion.1 = f32[4096,59]{1,0:T(8,128)S(1)} fusion(f32[59,2048]{0,1:T(8,128)S(1)} %bitcast.973, s32[4096]{0:T(1024)S(1)} %broadcast_clamp_fusion), kind=kCustom, calls=%fused_computation.1 | custom fusion | bytes 1949696 | tf_op jit(solution)/shard_map/gather | solution.py:200
  41.4 195.4 %while.17 = (s32[]{:T(128)}, f32[8,3,256]{2,0,1:T(8,128)S(1)}, f32[8,59,512]{2,1,0:T(8,128)}, f32[8,7]{1,0:T(8,128)S(1)}, f32[8,59,512]{2,1,0:T(8,128)S(1)}, /*i...) while((s32[]{:T(128)}, f32[8,3,256]{2,0,1:T(8,128)S(1)}, ...), condition=%wide.region_9.10_spmd.clone.clone, body=%wide.region_0.9_spmd.clone.clone.sunk | while | flops 1643947008 | bytes 4820185 | solution.py:216
  46.2 2.0 fusion.278
  48.2 1.3 fusion.279
  55.8 1.4 fusion.283
  60.0 2.2 fusion.286
  70.6 2.0 fusion.278
  72.6 1.3 fusion.279
  80.2 1.4 fusion.283
  84.4 2.2 fusion.286
  89.2 1.0 bitcast_dynamic-update-slice_fusion.2
  95.1 2.0 fusion.278
  97.1 1.3 fusion.279
  104.6 1.4 fusion.283
  108.9 2.2 fusion.286
  113.6 1.0 bitcast_dynamic-update-slice_fusion.2
  119.5 2.0 fusion.278
  121.5 1.3 fusion.279
  129.1 1.4 fusion.283
  133.3 2.2 fusion.286
  143.9 2.0 fusion.278
  145.9 1.3 fusion.279
  153.5 1.4 fusion.283
  157.7 2.2 fusion.286
  168.3 2.0 fusion.278
  170.3 1.3 fusion.279
  177.9 1.4 fusion.283
  182.1 2.2 fusion.286
  192.7 2.0 fusion.278
  194.7 1.3 fusion.279
  202.3 1.4 fusion.283
  206.5 2.2 fusion.286
  211.3 1.0 bitcast_dynamic-update-slice_fusion.2
  217.2 2.0 fusion.278
  219.2 1.3 fusion.279
  226.7 1.4 fusion.283
  231.0 2.2 fusion.286
  236.8 1.9 copy.43
  238.6 22.6 %scatter_custom_fusion = f32[59,2048]{0,1:T(8,128)S(1)} fusion(s32[4096]{0:T(1024)S(1)} %bitcast.1032, f32[4096,59]{1,0:T(8,128)S(1)} %bitcast.985, f32[]{:T(128)} %constant.268.clone.1), kind=kCustom, calls=%fused_computation.538 | custom fusion | flops 241664 | bytes 483332 | tf_op jit(solution)/shard_map/scatter-add | solution.py:219
  261.6 11.2 %all_to_all.24 = f32[59,4,512]{2,0,1:T(8,128)S(1)} all-to-all(f32[59,4,512]{2,0,1:T(8,128)S(1)} %copy.39), channel_id=1, replica_groups=mesh['groups'=2,'render'=4,'view'=4] {'render'}, dimensions={1} | all-to-all | bytes 966656 | tf_op jit(solution)/shard_map/all_to_all | solution.py:220
  273.8 12.9 %scatter_custom_fusion.1 = f32[59,4096]{0,1:T(8,128)} fusion(s32[2048]{0:T(1024)S(1)} %bitcast.1035, f32[2048,59]{1,0:T(8,128)S(1)} %copy.41, f32[]{:T(128)} %constant.268.clone.1), kind=kCustom, calls=%fused_computation.536 | custom fusion | flops 120832 | bytes 966660 | tf_op jit(solution)/shard_map/scatter-add | solution.py:221
  286.7 45.0 %reduce-scatter.2.cloned.1.call-done = f32[59,1024]{0,1:T(8,128)} async-done(((f32[59,4096]{0,1:T(8,128)}), f32[59,1024]{0,1:T(8,128)}) %reduce-scatter.2.cloned.1.call-update) | async-done | bytes 241680 | tf_op jit(solution)/shard_map/reduce_scatter | solution.py:222
  331.7 1.9 copy.42
  (397 shorter events, 88.9 us)
Async XLA Ops:
  7.2 13.7 %copy-start = (f32[4,7]{1,0:T(4,128)S(1)}, f32[4,7]{1,0:T(4,128)}, u32[]{:S(2)}) copy-start(f32[4,7]{1,0:T(4,128)} %param.10) | copy-start | bytes 340
  15.3 5.5 %copy-start.2 = (s32[1,1,8,512]{3,2,1,0:T(8,128)S(1)}, s32[1,1,8,512]{3,2,1,0:T(8,128)}, u32[]{:S(2)}) copy-start(s32[1,1,8,512]{3,2,1,0:T(8,128)} %param.14) | copy-start | bytes 49156
  15.3 5.5 %copy-start.1 = (f32[1,1,8,3,256]{4,2,3,1,0:T(8,128)S(1)}, f32[1,1,8,3,256]{4,2,3,1,0:T(8,128)}, u32[]{:S(2)}) copy-start(f32[1,1,8,3,256]{4,2,3,1,0:T(8,128)} %param.15) | copy-start | bytes 73732
  15.3 5.5 %copy-start.4 = (s32[1,1,8]{2,1,0:T(1,128)S(1)}, s32[1,1,8]{2,1,0:T(1,128)}, u32[]{:S(2)}) copy-start(s32[1,1,8]{2,1,0:T(1,128)} %param.12) | copy-start | bytes 100
  16.5 13.1 %all-to-all-start = ((f32[59,4,512]{2,0,1:T(8,128)}), f32[59,4,512]{2,0,1:T(8,128)S(1)}, u32[]{:S(2)}, u32[]{:S(2)}) async-start(f32[59,4,512]{2,0,1:T(8,128)} %copy.32), calls=%async_computation | async-start | bytes 1048576 | tf_op jit(solution)/shard_map/all_to_all | solution.py:199
  20.7 310.9 %reduce-scatter.2.cloned.1.call-start = ((), (), s32[]{:S(2)}) async-start(), calls=%async_computation.3 | async-start | bytes 2621440 | tf_op jit(solution)/shard_map/reduce_scatter | solution.py:222
  40.7 0.7 copy-start.5
  236.7 24.5 %copy-start.3 = (f32[8,3,256]{2,0,1:T(8,128)}, f32[8,3,256]{2,0,1:T(8,128)S(1)}, u32[]{:S(2)}) copy-start(f32[8,3,256]{2,0,1:T(8,128)S(1)} %get-tuple-element.168) | copy-start | bytes 73732
Sparse Core Ops, SparseCore 0:
  286.8 44.7 reduce-scatter.1
where the time goes:
time: 342 us; the launch traced here: 340 us
  other arithmetic  118 us (35%)
  waiting for transfers between devices  53.5 us (16%)
  loops' own time  51.4 us (15%)
  matrix products  46.6 us (14%)
  local copies, waits for them, and re-layouts  41.3 us (12%)
  between operations  14.2 us (4%)
  blocking collectives  11.2 us (3%)
  starting transfers between devices  4.24 us (1%)
    another operation x1, loops' own time, body(): lax.map(tile_work, (jnp.moveaxis(picked, 1, 0), tile_cams, tile_codes, li...  51.4 us
    reduce_scatter x1, waiting for transfers between devices, body(): grad_part = lax.psum_scatter(owned, 'view', scatter_dimension=1, tiled=True)  45 us
    dot_general x16, matrix products, exclusive_sum(): return jnp.dot(strict_lower, log_keep, precision=lax.Precision.HIGHEST)  29 us
    scatter-add x1, other arithmetic, body(): jnp.zeros_like(arrived).at[:, entry_slot].add(jnp.moveaxis(grad_raws, 0, 1))  22.6 us
    dot_general x24, matrix products, blend_tile(): colour = jnp.dot(tile_feat[5:8], weight, precision=lax.Precision.HIGHEST)  17.4 us
    mul x16, other arithmetic, project(): focal * camera_pt[0] * inv_depth * inv_depth  15.7 us
    mul x8, other arithmetic, project(): focal * camera_pt[1] * inv_depth * inv_depth  15.7 us
    scatter-add x1, other arithmetic, body(): owned = jnp.zeros_like(params).at[:, chosen_rows].add(row_grads)  12.9 us
  transfers between devices with their start and end apart: 2, of which 2 were waited for; matrix products, arithmetic and copies ran while one was open for 0% of the time, Pallas kernels for 0%

commit v1 on v0

v1 whole, which is shorter than its diff:
```python
from functools import partial

import jax
import jax.numpy as jnp
from jax import lax
from jax.experimental import pallas as pl
from jax.experimental.pallas import tpu as pltpu
from jax.sharding import PartitionSpec as P

CROP = 2
PIXELS = 256
GEOMETRY = 11
COLOUR_ROW = 12
SPAN = 256
LOG2_E = 1.4426950408889634
DEAD = -1e30

dilation = 0.3
backdrop = 1.0
band_zero = 0.28209479177387814
band_one = 0.4886025119029199
band_two = [
    1.0925484305920792,
    -1.0925484305920792,
    0.31539156525252005,
    -1.0925484305920792,
    0.5462742152960396,
]
band_three = [
    -0.5900435899266435,
    2.890611442640554,
    -0.4570457994644658,
    0.3731763325901154,
    -0.4570457994644658,
    1.445305721320277,
    -0.5900435899266435,
]

F32 = jnp.float32
BF16 = jnp.bfloat16


def harmonic_basis(along_x, along_y, along_z):
    square_x = along_x * along_x
    square_y = along_y * along_y
    square_z = along_z * along_z
    return [
        jnp.full_like(along_x, band_zero),
        -band_one * along_y,
        band_one * along_z,
        -band_one * along_x,
        band_two[0] * along_x * along_y,
        band_two[1] * along_y * along_z,
        band_two[2] * (2.0 * square_z - square_x - square_y),
        band_two[3] * along_x * along_z,
        band_two[4] * (square_x - square_y),
        band_three[0] * along_y * (3.0 * square_x - square_y),
        band_three[1] * along_x * along_y * along_z,
        band_three[2] * along_y * (4.0 * square_z - square_x - square_y),
        band_three[3] * along_z * (2.0 * square_z - 3.0 * square_x - 3.0 * square_y),
        band_three[4] * along_x * (4.0 * square_z - square_x - square_y),
        band_three[5] * along_z * (square_x - square_y),
        band_three[6] * along_x * (square_x - 3.0 * square_y),
    ]


def high_low(value):
    high = value.astype(BF16).astype(F32)
    return high, value - high


def dot_plain(left, right):
    return lax.dot_general(left, right, (((1,), (0,)), ((), ())), preferred_element_type=F32)


def dot_lanes(left, right):
    return lax.dot_general(left, right, (((1,), (1,)), ((), ())), preferred_element_type=F32)


def camera_table(cameras):
    cosine, sine = jnp.cos(cameras[:, :3]), jnp.sin(cameras[:, :3])
    c0, c1, c2 = cosine[:, 0], cosine[:, 1], cosine[:, 2]
    s0, s1, s2 = sine[:, 0], sine[:, 1], sine[:, 2]
    rotation = [
        [c1 * c2, s0 * s1 * c2 - c0 * s2, c0 * s1 * c2 + s0 * s2],
        [c1 * s2, s0 * s1 * s2 + c0 * c2, c0 * s1 * s2 - s0 * c2],
        [-s1, s0 * c1, c0 * c1],
    ]
    shift = [cameras[:, 3], cameras[:, 4], cameras[:, 5]]
    origin = [sum(rotation[m][a] * shift[m] for m in range(3)) for a in range(3)]
    return jnp.stack([e for row in rotation for e in row] + shift + [cameras[:, 6]] + origin, 1)


def lane_pick(source, lanes):
    return jnp.take_along_axis(source, lanes, axis=1, mode="promise_in_bounds")


def slab_kernel(n_render, views, params_ref, table_ref, index_ref, *rest):
    outs, dense_ref = rest[:n_render], rest[n_render]
    rows, gaussians = dense_ref.shape
    cap = index_ref.shape[1]
    width = 256

    def shade(step, _):
        lanes = pl.ds(pl.multiple_of(step * width, width), width)
        dense_ref[0:16, lanes] = params_ref[0:16, lanes]
        away = [params_ref[a : a + 1, lanes] + table_ref[:, 13 + a : 14 + a] for a in range(3)]
        inverse = lax.rsqrt(away[0] * away[0] + away[1] * away[1] + away[2] * away[2])
        basis = harmonic_basis(*[part * inverse for part in away])
        for channel in range(3):
            base = GEOMETRY + 16 * channel
            colour = 0.5 + basis[0] * params_ref[base : base + 1, lanes]
            for level in range(1, 16):
                colour += basis[level] * params_ref[base + level : base + level + 1, lanes]
            first = COLOUR_ROW + channel * views
            dense_ref[first : first + views, lanes] = colour
        return 0

    lax.fori_loop(0, gaussians // width, shade, 0)

    for turn in range(n_render):

        def pick(step, _):
            lanes = pl.ds(pl.multiple_of(step * 128, 128), 128)
            index = jnp.broadcast_to(index_ref[turn : turn + 1, lanes], (8, 128))
            lane, block = index & 127, index >> 7
            found = [jnp.zeros((8, 128), F32) for _ in range(rows // 8)]
            for b in range(gaussians // 128):
                here = block == b
                for s in range(rows // 8):
                    piece = dense_ref[8 * s : 8 * s + 8, 128 * b : 128 * b + 128]
                    found[s] = jnp.where(here, lane_pick(piece, lane), found[s])
            for s in range(rows // 8):
                outs[turn][8 * s : 8 * s + 8, lanes] = found[s]
            return 0

        lax.fori_loop(0, cap // 128, pick, 0)


def entry_coefficients(raw, cam):
    px, py, pz = raw[0], raw[1], raw[2]
    extent = [jnp.exp(raw[3 + a]) for a in range(3)]
    norm = lax.rsqrt(raw[6] * raw[6] + raw[7] * raw[7] + raw[8] * raw[8] + raw[9] * raw[9])
    qw, qx, qy, qz = [raw[6 + a] * norm for a in range(4)]
    turn = [[cam[3 * a + b] for b in range(3)] for a in range(3)]
    x, y, z = [turn[a][0] * px + turn[a][1] * py + turn[a][2] * pz + cam[9 + a] for a in range(3)]
    scale = cam[12] / z
    slope_x, slope_y = x / z, y / z
    u = cam[12] * slope_x + cam[13]
    v = cam[12] * slope_y + cam[14]
    quat = [
        [1.0 - 2.0 * (qy * qy + qz * qz), 2.0 * (qx * qy - qw * qz), 2.0 * (qx * qz + qw * qy)],
        [2.0 * (qx * qy + qw * qz), 1.0 - 2.0 * (qx * qx + qz * qz), 2.0 * (qy * qz - qw * qx)],
        [2.0 * (qx * qz - qw * qy), 2.0 * (qy * qz + qw * qx), 1.0 - 2.0 * (qx * qx + qy * qy)],
    ]
    screen = [
        [scale * (turn[a][b] - slope * turn[2][b]) for b in range(3)]
        for a, slope in ((0, slope_x), (1, slope_y))
    ]
    foot = [
        [sum(screen[a][m] * quat[m][b] for m in range(3)) * extent[b] for b in range(3)]
        for a in range(2)
    ]
    cov_a = sum(foot[0][b] * foot[0][b] for b in range(3)) + dilation
    cov_b = sum(foot[0][b] * foot[1][b] for b in range(3))
    cov_c = sum(foot[1][b] * foot[1][b] for b in range(3)) + dilation
    inverse = 1.0 / (cov_a * cov_c - cov_b * cov_b)
    conic_a, conic_b, conic_c = cov_c * inverse, -cov_b * inverse, cov_a * inverse
    log_opacity = -jnp.log(1.0 + jnp.exp(-raw[10]))
    pull_x = conic_a * u + conic_b * v
    pull_y = conic_c * v + conic_b * u
    return [
        -0.5 * conic_a,
        -conic_b,
        -0.5 * conic_c,
        pull_x,
        pull_y,
        log_opacity - 0.5 * (pull_x * u + pull_y * v),
    ]


def monomials(rows):
    row = lax.broadcasted_iota(jnp.int32, (rows, PIXELS), 0) & 7
    pixel = lax.broadcasted_iota(jnp.int32, (rows, PIXELS), 1)
    x = (pixel & 15).astype(F32) - 7.5
    y = (pixel >> 4).astype(F32) - 7.5
    value = jnp.where(row == 0, x * x, 0.0)
    for number, term in ((1, x * y), (2, y * y), (3, x), (4, y), (5, jnp.ones_like(x))):
        value = jnp.where(row == number, term, value)
    return value


def render_kernel(n_render, views, where_ref, *refs):
    blocks, refs = refs[:n_render], refs[n_render:]
    slot_ref, cam_ref, target_ref, refs = refs[0], refs[1], refs[2], refs[3:]
    image_ref, outs, refs = refs[0], refs[1 : 1 + n_render], refs[1 + n_render :]
    raw_ref, stack_ref, wide_ref, tall_ref, alpha_ref, weight_ref, high_ref, low_ref, lhs_ref, acc_ref = refs
    tiles = target_ref.shape[0]
    entry_rows = slot_ref.shape[0]
    entries = entry_rows * 128
    cap = blocks[0].shape[1]
    rows = blocks[0].shape[0]
    per_block = cap // 128
    me = where_ref[0]
    groups = entry_rows // 8

    def fetch(group, _):
        here = pl.ds(pl.multiple_of(group * 8, 8), 8)
        slot = slot_ref[here, :]
        lane, block = slot & 127, slot >> 7
        view = jnp.broadcast_to(cam_ref[15:16, :], (8, 128)).astype(jnp.int32)
        found = [jnp.zeros((8, 128), F32) for _ in range(GEOMETRY + 3)]
        for turn in range(n_render):
            first = (me ^ turn) * per_block
            for j in range(per_block):
                hit = block == first + j
                cut = slice(128 * j, 128 * j + 128)
                for p in range(GEOMETRY):
                    piece = jnp.broadcast_to(blocks[turn][p : p + 1, cut], (8, 128))
                    found[p] = jnp.where(hit, lane_pick(piece, lane), found[p])
                for w in range(views):
                    seen = hit & (view == w)
                    for channel in range(3):
                        p = COLOUR_ROW + channel * views + w
                        piece = jnp.broadcast_to(blocks[turn][p : p + 1, cut], (8, 128))
                        at = GEOMETRY + channel
                        found[at] = jnp.where(seen, lane_pick(piece, lane), found[at])
        for p in range(GEOMETRY + 3):
            raw_ref[p, here, :] = found[p]
        return 0

    lax.fori_loop(0, groups, fetch, 0)

    def cam_rows():
        return [jnp.broadcast_to(cam_ref[i : i + 1, :], (8, 128)) for i in range(15)]

    stack_ref[...] = jnp.zeros_like(stack_ref)

    def forward_entries(group, _):
        here = pl.ds(pl.multiple_of(group * 8, 8), 8)
        coefficient = entry_coefficients([raw_ref[p, here, :] for p in range(GEOMETRY)], cam_rows())
        row = lax.broadcasted_iota(jnp.int32, (8, 128), 0) + group * 8
        lane = lax.broadcasted_iota(jnp.int32, (8, 128), 1)
        order = (row * 128 + lane) // tiles
        live = order < jnp.broadcast_to(cam_ref[16:17, :], (8, 128)).astype(jnp.int32)
        for c in range(6):
            value = coefficient[c] * LOG2_E
            if c == 5:
                value = jnp.where(live, value, DEAD)
            at = pl.ds(pl.multiple_of(c * entry_rows + group * 8, 8), 8)
            stack_ref[at, :] = value
        for channel in range(3):
            at = pl.ds(pl.multiple_of((8 + channel) * entry_rows + group * 8, 8), 8)
            stack_ref[at, :] = raw_ref[GEOMETRY + channel, here, :]
        return 0

    lax.fori_loop(0, groups, forward_entries, 0)

    wide_ref[96:128, :] = jnp.zeros((32, entries), BF16)
    own_tile = (lax.broadcasted_iota(jnp.int32, (8, 128), 1) & (tiles - 1)) == lax.broadcasted_iota(
        jnp.int32, (8, 128), 0
    )

    def widen(row, _):
        value = stack_ref[pl.ds(row, 16, stride=entry_rows), :]
        high, rest = high_low(value)
        middle, low = high_low(rest)

        def spread(part):
            return [
                jnp.where(own_tile, jnp.broadcast_to(part[8 + ch : 9 + ch, :], (8, 128)), 0.0)
                for ch in range(3)
            ]

        pieces = [high[0:8], middle[0:8], low[0:8]] + spread(high) * 2 + spread(middle)
        lanes = pl.ds(pl.multiple_of(row * 128, 128), 128)
        wide_ref[0:96, lanes] = jnp.concatenate(pieces, axis=0).astype(BF16)
        return 0

    lax.fori_loop(0, entry_rows, widen, 0)

    eye = (
        lax.broadcasted_iota(jnp.int32, (256, 256), 0) == lax.broadcasted_iota(jnp.int32, (256, 256), 1)
    ).astype(F32).astype(BF16)
    left = jnp.concatenate([monomials(24), jnp.zeros((104, PIXELS), F32)], axis=0).astype(BF16)
    moment_rows = monomials(16)
    moment_rows = jnp.where(
        lax.broadcasted_iota(jnp.int32, (16, PIXELS), 0) < 8, moment_rows, 0.0
    ).astype(BF16)
    steps = 256 // tiles

    def forward(chunk, carry):
        passing, image = carry
        at = pl.ds(pl.multiple_of(chunk * 256, 256), 256)
        tall = dot_lanes(eye, wide_ref[:, at]).astype(BF16)
        tall_ref[at, :] = tall
        alpha = jnp.exp2(dot_plain(tall, left))
        alpha_ref[at, :] = alpha
        weights = []
        for k in range(steps):
            weight = passing * alpha[tiles * k : tiles * k + tiles, :]
            passing = passing - weight
            weights.append(weight)
        weight = jnp.concatenate(weights, axis=0)
        weight_ref[at, :] = weight
        high, low = high_low(weight)
        high, low = high.astype(BF16), low.astype(BF16)
        high_ref[at, :] = high
        low_ref[at, :] = low
        colours = wide_ref[48:96, at]
        image = image + (dot_plain(colours, high) + dot_plain(colours, low))
        return passing, image

    remain, image = lax.fori_loop(
        0,
        entries // 256,
        forward,
        (jnp.ones((tiles, PIXELS), F32), jnp.zeros((48, PIXELS), F32)),
    )
    image = image[0:24] + image[24:48]
    residual = []
    for channel in range(3):
        shown = image[8 * channel : 8 * channel + 8] + backdrop * remain
        image_ref[:, channel, :] = shown
        residual.append(shown - target_ref[:, channel, :])
    behind = backdrop * (residual[0] + residual[1] + residual[2])
    high, low = high_low(jnp.concatenate(residual, axis=0))
    zeros = jnp.zeros((24, PIXELS), F32)
    right = jnp.concatenate([zeros, high, low, high, jnp.zeros((32, PIXELS), F32)], axis=0).astype(BF16)
    both = jnp.concatenate([high, low], axis=0).astype(BF16)
    own_wide = (lax.broadcasted_iota(jnp.int32, (8, 256), 1) & (tiles - 1)) == lax.broadcasted_iota(
        jnp.int32, (8, 256), 0
    )

    def backward(step, behind):
        chunk = entries // 256 - 1 - step
        at = pl.ds(pl.multiple_of(chunk * 256, 256), 256)
        shade = dot_plain(tall_ref[at, :], right)
        alpha, weight = alpha_ref[at, :], weight_ref[at, :]
        slopes = [None] * steps
        for k in reversed(range(steps)):
            cut = slice(tiles * k, tiles * k + tiles)
            gap = shade[cut, :] - behind
            slopes[k] = weight[cut, :] * gap
            behind = behind + alpha[cut, :] * gap
        high, low = high_low(jnp.concatenate(slopes, axis=0))
        moments = dot_lanes(moment_rows, high.astype(BF16)) + dot_lanes(moment_rows, low.astype(BF16))
        tint = dot_lanes(both, high_ref[at, :]) + dot_lanes(both, low_ref[at, :])
        tint = tint[0:24] + tint[24:48]
        for half in range(2):
            row = chunk * 2 + half
            cut = slice(128 * half, 128 * half + 128)
            stack_ref[pl.ds(row, 8, stride=entry_rows), :] = moments[0:8, cut]
            for channel in range(3):
                part = jnp.where(own_tile, tint[8 * channel : 8 * channel + 8, cut], 0.0)
                stack_ref[pl.ds((8 + channel) * entry_rows + row, 1), :] = jnp.sum(
                    part, axis=0, keepdims=True
                )
        return behind

    lax.fori_loop(0, entries // 256, backward, behind)

    def backward_entries(group, _):
        here = pl.ds(pl.multiple_of(group * 8, 8), 8)
        cam = cam_rows()
        given = [
            stack_ref[pl.ds(pl.multiple_of(c * entry_rows + group * 8, 8), 8), :] for c in range(6)
        ]
        _, pull = jax.vjp(
            lambda raw: entry_coefficients(raw, cam), [raw_ref[p, here, :] for p in range(GEOMETRY)]
        )
        (grads,) = pull(given)
        for channel in range(3):
            at = pl.ds(pl.multiple_of((8 + channel) * entry_rows + group * 8, 8), 8)
            grads.append(stack_ref[at, :])
        for p in range(GEOMETRY + 3):
            high, low = high_low(grads[p])
            raw_ref[p, here, :] = high
            raw_ref[GEOMETRY + 3 + p, here, :] = low
        return 0

    lax.fori_loop(0, groups, backward_entries, 0)

    spans = n_render * cap // SPAN
    acc_ref[...] = jnp.zeros_like(acc_ref)
    view = cam_ref[15:16, :].astype(jnp.int32)
    view = jnp.concatenate([view] * 4, axis=1)

    def scatter(step, _):
        def line(ref, *lead):
            return jnp.concatenate(
                [ref[lead + (pl.ds(step * 4 + i, 1), slice(None))] for i in range(4)], axis=1
            )

        slot = line(slot_ref)
        span, lane = slot // SPAN, slot & (SPAN - 1)
        lanes_of = jnp.where(
            lax.broadcasted_iota(jnp.int32, (SPAN, 512), 0) == jnp.broadcast_to(lane, (SPAN, 512)), 1.0, 0.0
        ).astype(BF16)
        in_span = lax.broadcasted_iota(jnp.int32, (spans, 512), 0) == jnp.broadcast_to(span, (spans, 512))
        key = view * spans + span
        in_view = lax.broadcasted_iota(jnp.int32, (views * spans, 512), 0) == jnp.broadcast_to(
            key, (views * spans, 512)
        )
        half_rows = rows * spans
        for part in range(2):
            base = part * half_rows
            pieces = []
            for p in range(COLOUR_ROW):
                if p < GEOMETRY:
                    value = line(raw_ref, part * (GEOMETRY + 3) + p)
                    value = jnp.broadcast_to(value, (spans, 512))
                    pieces.append(jnp.where(in_span, value, 0.0))
                else:
                    pieces.append(jnp.zeros((spans, 512), F32))
                if len(pieces) == 2:
                    at = base + (p - 1) * spans
                    lhs_ref[at : at + 2 * spans, :] = jnp.concatenate(pieces, axis=0).astype(BF16)
                    pieces = []
            for channel in range(3):
                value = line(raw_ref, part * (GEOMETRY + 3) + GEOMETRY + channel)
                value = jnp.where(in_view, jnp.broadcast_to(value, (views * spans, 512)), 0.0)
                at = base + (COLOUR_ROW + channel * views) * spans
                lhs_ref[at : at + views * spans, :] = value.astype(BF16)
        product = dot_lanes(lhs_ref[...], lanes_of)
        for half in range(SPAN // 128):
            at = slice(half * 2 * half_rows, (half + 1) * 2 * half_rows)
            acc_ref[at, :] += product[:, 128 * half : 128 * half + 128]
        return 0

    lax.fori_loop(0, entry_rows // 4, scatter, 0)
    for turn in range(n_render):
        for part in range(cap // SPAN):
            span = (me ^ turn) * (cap // SPAN) + part
            for half in range(SPAN // 128):
                cut = slice(128 * half, 128 * half + 128)
                total = (
                    acc_ref[pl.ds(half * 2 * rows * spans + span, rows, stride=spans), :]
                    + acc_ref[pl.ds(half * 2 * rows * spans + rows * spans + span, rows, stride=spans), :]
                )
                first = part * SPAN + 128 * half
                outs[turn][:, first : first + 128] = total


def collect_kernel(n_render, n_view, where_ref, *refs):
    blocks, refs = refs[:n_render], refs[n_render:]
    index_ref, origin_ref, refs = refs[0], refs[1], refs[2:]
    outs, (lhs_ref, acc_ref) = refs[:n_view], refs[n_view:]
    rows, cap = blocks[0].shape
    own = outs[0].shape[0] // rows * 128
    gaussians = own * n_view
    spans = gaussians // SPAN
    column = where_ref[1]
    for turn in range(n_render):
        index = index_ref[turn : turn + 1, :]
        span, lane = index // SPAN, index & (SPAN - 1)
        lanes_of = jnp.where(
            lax.broadcasted_iota(jnp.int32, (SPAN, cap), 0) == jnp.broadcast_to(lane, (SPAN, cap)), 1.0, 0.0
        ).astype(BF16)
        in_span = lax.broadcasted_iota(jnp.int32, (spans, cap), 0) == jnp.broadcast_to(span, (spans, cap))
        high, low = high_low(blocks[turn][...])
        for part, value in ((0, high), (1, low)):
            for p in range(rows):
                at = (part * rows + p) * spans
                piece = jnp.broadcast_to(value[p : p + 1, :], (spans, cap))
                lhs_ref[at : at + spans, :] = jnp.where(in_span, piece, 0.0).astype(BF16)
        product = dot_lanes(lhs_ref[...], lanes_of)
        for half in range(2):
            at = slice(half * 2 * rows * spans, (half + 1) * 2 * rows * spans)
            piece = product[:, 128 * half : 128 * half + 128]
            if turn == 0:
                acc_ref[at, :] = piece
            else:
                acc_ref[at, :] += piece
    strips = own // 128
    for turn in range(n_view):
        for strip in range(strips):
            span = (column ^ turn) * (own // SPAN) + strip // 2
            first = (strip % 2) * 2 * rows * spans
            total = (
                acc_ref[pl.ds(first + span, rows, stride=spans), :]
                + acc_ref[pl.ds(first + rows * spans + span, rows, stride=spans), :]
            )
            outs[turn][pl.ds(strip, rows, stride=strips), :] = total
        outs[turn][GEOMETRY * strips : GEOMETRY * strips + 1, :] = origin_ref[...]


def owner_kernel(n_view, views, *refs):
    blocks, (own_ref, out_ref, sum_ref) = refs[:n_view], refs[n_view:]
    strips = out_ref.shape[1] // 128

    def of(ref, p):
        return ref[p * strips : (p + 1) * strips, :]

    position = [of(own_ref, a) for a in range(3)]
    levels = [[None] * 16 for _ in range(3)]
    moved = [0.0, 0.0, 0.0]
    for block in blocks:
        for w in range(views):
            away = []
            for a in range(3):
                at = 3 * w + a
                offset = block[GEOMETRY * strips : GEOMETRY * strips + 1, at : at + 1]
                away.append(position[a] + jnp.broadcast_to(offset, (strips, 128)))
            inverse = lax.rsqrt(away[0] * away[0] + away[1] * away[1] + away[2] * away[2])
            direction = [part * inverse for part in away]
            basis, pull = jax.vjp(harmonic_basis, *direction)
            tint = [of(block, COLOUR_ROW + ch * views + w) for ch in range(3)]
            for ch in range(3):
                for b in range(16):
                    term = tint[ch] * basis[b]
                    levels[ch][b] = term if levels[ch][b] is None else levels[ch][b] + term
            given = [
                sum(tint[ch] * of(own_ref, GEOMETRY + 16 * ch + b) for ch in range(3)) for b in range(16)
            ]
            turned = pull(given)
            along = sum(turned[a] * direction[a] for a in range(3))
            for a in range(3):
                moved[a] = moved[a] + inverse * (turned[a] - direction[a] * along)
    for p in range(GEOMETRY):
        total = sum(of(block, p) for block in blocks)
        sum_ref[p * strips : (p + 1) * strips, :] = total + moved[p] if p < 3 else total
    for ch in range(3):
        for b in range(16):
            p = GEOMETRY + 16 * ch + b
            sum_ref[p * strips : (p + 1) * strips, :] = levels[ch][b]
    count = out_ref.shape[0]
    for strip in range(strips):
        out_ref[:, 128 * strip : 128 * strip + 128] = sum_ref[pl.ds(strip, count, stride=strips), :]


def swap(blocks, axis):
    n = len(blocks)
    return [blocks[0]] + [
        lax.ppermute(blocks[turn], axis, [(i, i ^ turn) for i in range(n)]) for turn in range(1, n)
    ]


def call(kernel, out_shape, scratch, in_smem, *args):
    specs = [
        pl.BlockSpec(memory_space=pltpu.SMEM) if i < in_smem else pl.BlockSpec(memory_space=pltpu.VMEM)
        for i in range(len(args))
    ]
    return pl.pallas_call(
        kernel,
        out_shape=out_shape,
        in_specs=specs,
        out_specs=[pl.BlockSpec(memory_space=pltpu.VMEM)] * len(out_shape),
        scratch_shapes=scratch,
        compiler_params=pltpu.CompilerParams(vmem_limit_bytes=48 * 1024 * 1024),
    )(*args)


def body(n_render, n_view, params, cameras, send_index, tile_id, tile_count, tile_slot, targets):
    index = send_index[0, 0]
    slot = tile_slot[0, 0]
    code = tile_id[0, 0]
    live = tile_count[0, 0]
    wanted = targets[0, 0]
    views = cameras.shape[0]
    gaussians = params.shape[1]
    cap = index.shape[1]
    tiles, length = slot.shape
    own = gaussians // n_view
    rows = -(-(COLOUR_ROW + 3 * views) // 8) * 8
    order = lax.axis_index("render") ^ jnp.arange(n_render, dtype=jnp.int32)
    index = sum(jnp.where((order == o)[:, None], index[o][None], 0) for o in range(n_render))
    where = jnp.stack([lax.axis_index("render"), lax.axis_index("view")]).astype(jnp.int32)

    table = camera_table(cameras)
    view = code // (CROP * CROP)
    cell = code % (CROP * CROP)
    tile_table = sum(
        jnp.where((view == w)[:, None], table[w : w + 1, :13], 0.0) for w in range(views)
    )
    extra = jnp.stack(
        [
            (8 * CROP - 8 - 16 * (cell % CROP)).astype(F32),
            (8 * CROP - 8 - 16 * (cell // CROP)).astype(F32),
            view.astype(F32),
            live.astype(F32),
        ],
        axis=1,
    )
    lane_table = jnp.concatenate([tile_table, extra, jnp.zeros((tiles, 7), F32)], axis=1).T
    lane_table = jnp.tile(lane_table, (1, 128 // tiles))
    slot_lanes = slot.T.reshape(-1, 128)
    origin = jnp.pad(table[:, 13:16].reshape(1, 3 * views), ((0, 0), (0, 128 - 3 * views)))
    mine = lax.dynamic_slice_in_dim(params, lax.axis_index("view") * own, own, 1).reshape(-1, 128)

    block = jax.ShapeDtypeStruct((rows, cap), F32)
    sent = call(
        partial(slab_kernel, n_render, views),
        [block] * n_render,
        [pltpu.VMEM((rows, gaussians), F32)],
        0,
        params,
        table,
        index,
    )
    arrived = swap(list(sent), "render")
    entries = tiles * length
    entry_rows = entries // 128
    spans = n_render * cap // SPAN
    image, *returned = call(
        partial(render_kernel, n_render, views),
        [jax.ShapeDtypeStruct(wanted.shape, F32)] + [block] * n_render,
        [
            pltpu.VMEM((2 * (GEOMETRY + 3), entry_rows, 128), F32),
            pltpu.VMEM((16 * entry_rows, 128), F32),
            pltpu.VMEM((128, entries), BF16),
            pltpu.VMEM((entries, 128), BF16),
            pltpu.VMEM((entries, PIXELS), F32),
            pltpu.VMEM((entries, PIXELS), F32),
            pltpu.VMEM((entries, PIXELS), BF16),
            pltpu.VMEM((entries, PIXELS), BF16),
            pltpu.VMEM((2 * rows * spans, 512), BF16),
            pltpu.VMEM((4 * rows * spans, 128), F32),
        ],
        1,
        where,
        *arrived,
        slot_lanes,
        lane_table,
        wanted,
    )
    homed = swap(list(returned), "render")
    slab_spans = gaussians // SPAN
    shares = call(
        partial(collect_kernel, n_render, n_view),
        [jax.ShapeDtypeStruct((rows * own // 128, 128), F32)] * n_view,
        [
            pltpu.VMEM((2 * rows * slab_spans, cap), BF16),
            pltpu.VMEM((4 * rows * slab_spans, 128), F32),
        ],
        1,
        where,
        *homed,
        index,
        origin,
    )
    owned = swap(list(shares), "view")
    (gradients,) = call(
        partial(owner_kernel, n_view, views),
        [jax.ShapeDtypeStruct((params.shape[0], own), F32)],
        [pltpu.VMEM((params.shape[0] * own // 128, 128), F32)],
        0,
        *owned,
        mine,
    )
    return (image[None, None], gradients)


def solution(mesh):
    in_specs = (
        P(None, ("groups", "render")),
        P(("groups", "view"), None),
        P(("groups", "render"), "view", None, None),
        P(("groups", "render"), "view", None),
        P(("groups", "render"), "view", None),
        P(("groups", "render"), "view", None, None),
        P(("groups", "render"), "view", None, None, None),
    )
    out_specs = (
        P(("groups", "render"), "view", None, None, None),
        P(None, ("groups", "render", "view")),
    )
    work = partial(body, mesh.shape["render"], mesh.shape["view"])
    return jax.shard_map(work, mesh=mesh, in_specs=in_specs, out_specs=out_specs, check_vma=False)
```

time: 342 us -> 60.3 us (0.18)
  other arithmetic: 118 us -> 0.53 us
  loops' own time: 51.4 us -> 0 us
  matrix products: 46.6 us -> 0 us
  waiting for transfers between devices: 53.5 us -> 9.69 us
  local copies, waits for them, and re-layouts: 41.3 us -> 7.85 us
  Pallas kernels: 0 us -> 31.5 us
  between operations: 14.2 us -> 0.79 us
  blocking collectives: 11.2 us -> 0 us
  starting transfers between devices: 4.24 us -> 9.56 us
    another operation x1 -> x0, loops' own time: 51.4 us -> none  [body(): lax.map(tile_work, (jnp.moveaxis(picked, 1, 0), tile_cams, tile_codes, li...]
    dot_general x41 -> x0, matrix products: 46.6 us -> none  [the longest x16 29 us: exclusive_sum(): return jnp.dot(strict_lower, log_keep, precision=lax.Precision.HIGHEST)]
    reduce_scatter x1 -> x0, waiting for transfers between devices: 45 us -> none  [body(): grad_part = lax.psum_scatter(owned, 'view', scatter_dimension=1, tiled=True)]
    mul x96 -> x0, other arithmetic: 36 us -> none  [the longest x16 15.7 us: project(): focal * camera_pt[0] * inv_depth * inv_depth]
    scatter-add x2 -> x0, other arithmetic: 35.5 us -> none  [the longest x1 22.6 us: body(): jnp.zeros_like(arrived).at[:, entry_slot].add(jnp.moveaxis(grad_raws, 0, 1))]
    pallas_call x0 -> x4, Pallas kernels: none -> 31.5 us  [call(): pl.pallas_call(kernel, out_shape=out_shape, in_specs=specs, out_specs=[pl...]
    gather x3 -> x0, local copies, waits for them, and re-layouts: 16.9 us -> none  [the longest x2 11.4 us: body(): picked = arrived[:, entry_slot]]
    add_any x72 -> x0, other arithmetic: 14.6 us -> none  [the longest x16 6.32 us: project(): determinant = cov_a * cov_c - cov_b * cov_b]
  transfers between devices with their start and end apart: 2 -> 9, of which waited for: 2 -> 3; matrix products, arithmetic and copies ran while one was open for 0% -> 5% of each run, Pallas kernels for 0% -> 0%
where the time goes in v1:
time: 60.3 us; the launch traced here: 59.9 us
  Pallas kernels  31.5 us (52%)
  waiting for transfers between devices  9.69 us (16%)
  starting transfers between devices  9.56 us (16%)
  local copies, waits for them, and re-layouts  7.85 us (13%)
  between operations  0.79 us (1%)
    pallas_call x4, Pallas kernels, call(): pl.pallas_call(kernel, out_shape=out_shape, in_specs=specs, out_specs=[pl...  31.5 us
    ppermute x9, waiting for transfers between devices, swap(): lax.ppermute(blocks[turn], axis, [(i, i ^ turn) for i in range(n)])  9.69 us
    ppermute x9, starting transfers between devices, swap(): lax.ppermute(blocks[turn], axis, [(i, i ^ turn) for i in range(n)])  9.56 us
    unnamed x16, local copies, waits for them, and re-layouts  5.69 us
  transfers between devices with their start and end apart: 9, of which 3 were waited for; matrix products, arithmetic and copies ran while one was open for 5% of the time, Pallas kernels for 0%

profile of v1, /device:TPU:0, one launch (start us, length us, event | category | flops | bytes accessed | tf_op | source)
XLA Modules:
  0.0 59.9 jit_solution(5729271667699143807)
XLA Ops:
  0.7 0.6 %copy-done.1 = f32[4,7]{1,0:T(4,128)S(1)} copy-done((f32[4,7]{1,0:T(4,128)S(1)}, f32[4,7]{1,0:T(4,128)}, u32[]{:S(2)}) %copy-start.1) | copy-done | bytes 136
  1.3 0.1 slice.76
  1.4 0.1 multiply_add_fusion.1
  1.5 0.1 multiply_add_fusion
  1.6 0.6 %copy-done.4 = s32[1,1,4,512]{3,2,1,0:T(4,128)S(1)} copy-done((s32[1,1,4,512]{3,2,1,0:T(4,128)S(1)}, s32[1,1,4,512]{3,2,1,0:T(4,128)}, u32[]{:S(2)}) %copy-start.4) | copy-done | bytes 8216
  2.2 0.1 select_add_fusion.index_ref.refs_4_
  2.3 0.1 stack.15.table_ref
  2.4 0.0 copy-start
  2.4 1.2 %copy-done = f32[59,4096]{1,0:T(8,128)S(1)} copy-done((f32[59,4096]{1,0:T(8,128)S(1)}, f32[59,4096]{1,0:T(8,128)}, u32[]{:S(2)}) %copy-start) | copy-done | bytes 966680
  3.6 4.8 %shard_map.86 = (f32[24,512]{1,0:T(8,128)S(1)}, f32[24,512]{1,0:T(8,128)S(1)}, f32[24,512]{1,0:T(8,128)S(1)}, f32[24,512]{1,0:T(8,128)S(1)}) custom-call(f32[59,4096]{1,0:T(8,128)S(1)} %copy-done, f32[4,16]{1,0:T(4,128)S(1)} %stack.15.table_ref, s32[4,512]{1,0:T(4,128)S(1)} %select_add_fusion.index_ref.refs_4_), custom_call_target="tpu_custom_call" | custom-call | tf_op jit(solution)/shard_map/pallas_call | solution.py:544
  8.4 0.5 collective-permute-start
  9.0 2.6 %collective-permute-start.1 = (f32[24,512]{1,0:T(8,128)S(1)}, f32[24,512]{1,0:T(8,128)S(1)}, u32[]{:S(2)}, u32[]{:S(2)}) collective-permute-start(f32[24,512]{1,0:T(8,128)S(1)} %get-tuple-element.17), channel_id=1, source_target_pairs={{0,8},{4,12},{8,0},{12,4},{1,9},{5,13},{9,1},{13,5},{2,10},{6,14},... | collective-permute-start | bytes 147464 | tf_op jit(solution)/shard_map/ppermute | solution.py:535
  11.6 0.1 collective-permute-start.2
  11.6 0.6 copy-done.5
  12.2 0.1 stack.16
  12.4 0.7 %copy-done.6 = s32[1,1,8]{2,1,0:T(1,128)S(1)} copy-done((s32[1,1,8]{2,1,0:T(1,128)S(1)}, s32[1,1,8]{2,1,0:T(1,128)}, u32[]{:S(2)}) %copy-start.6) | copy-done | bytes 56
  13.1 0.1 copy.13
  13.1 0.1 copy.14
  13.2 0.1 copy.15
  13.3 0.1 copy.16
  13.4 0.1 select_add_fusion.1
  13.5 0.1 concatenate.8
  13.6 0.1 pad_add_fusion.where_ref
  13.6 0.7 %copy-done.2 = f32[1,1,8,3,256]{4,2,3,1,0:T(8,128)S(1)} copy-done((f32[1,1,8,3,256]{4,2,3,1,0:T(8,128)S(1)}, f32[1,1,8,3,256]{4,2,3,1,0:T(8,128)}, u32[]{:S(2)}) %copy-start.2) | copy-done | bytes 24600
  14.3 0.0 copy-start.3
  14.3 0.1 copy.18.refs_5_
  14.4 0.7 %copy-done.3 = s32[1,1,8,512]{3,2,1,0:T(8,128)S(1)} copy-done((s32[1,1,8,512]{3,2,1,0:T(8,128)S(1)}, s32[1,1,8,512]{3,2,1,0:T(8,128)}, u32[]{:S(2)}) %copy-start.3) | copy-done | bytes 16408
  15.0 0.1 copy.12
  15.1 0.2 reshape.287.refs_4_
  15.3 0.0 collective-permute-done.refs_1_
  15.3 0.0 collective-permute-done.1.refs_2_
  15.3 23.3 %shard_map.87 = (f32[8,3,256]{2,1,0:T(4,128)S(1)}, f32[24,512]{1,0:T(8,128)S(1)}, f32[24,512]{1,0:T(8,128)S(1)}, f32[24,512]{1,0:T(8,128)S(1)}, f32[24,512]{1,0:T(8,128)S(1)}) custom-call(s32[2]{0:T(128)S(1)} %pad_add_fusion.where_ref, f32[24,512]{1,0:T(8,128)S(1)} %get-tuple-element.15.refs_0_, f32[24,512]{1,0:T(8,128)S(1)} %collective-permute-done.refs_1_, ...), custom_call_target="tpu_custom_call" | custom-call | tf_op jit(solution)/shard_map/pallas_call | solution.py:544
  38.6 0.2 collective-permute-start.3
  38.8 1.3 %collective-permute-start.4 = (f32[24,512]{1,0:T(8,128)S(1)}, f32[24,512]{1,0:T(8,128)S(1)}, u32[]{:S(2)}, u32[]{:S(2)}) collective-permute-start(f32[24,512]{1,0:T(8,128)S(1)} %get-tuple-element.22), channel_id=1, source_target_pairs={{0,8},{4,12},{8,0},{12,4},{1,9},{5,13},{9,1},{13,5},{2,10},{6,14},... | collective-permute-start | bytes 147464 | tf_op jit(solution)/shard_map/ppermute | solution.py:535
  40.2 0.4 collective-permute-start.5
  40.5 0.1 pad_maximum_fusion
  40.6 0.1 reshape.288
  40.7 0.0 collective-permute-done.3.refs_1_
  40.7 2.2 %collective-permute-done.4.refs_2_ = f32[24,512]{1,0:T(8,128)S(1)} collective-permute-done((f32[24,512]{1,0:T(8,128)S(1)}, f32[24,512]{1,0:T(8,128)S(1)}, u32[]{:S(2)}, u32[]{:S(2)}) %collective-permute-start.4) | collective-permute-done | bytes 49184 | tf_op jit(solution)/shard_map/ppermute | solution.py:535
  42.9 1.2 %collective-permute-done.5.refs_3_ = f32[24,512]{1,0:T(8,128)S(1)} collective-permute-done((f32[24,512]{1,0:T(8,128)S(1)}, f32[24,512]{1,0:T(8,128)S(1)}, u32[]{:S(2)}, u32[]{:S(2)}) %collective-permute-start.5) | collective-permute-done | bytes 49184 | tf_op jit(solution)/shard_map/ppermute | solution.py:535
  44.2 1.8 %shard_map.88 = (f32[192,128]{1,0:T(8,128)S(1)}, f32[192,128]{1,0:T(8,128)S(1)}, f32[192,128]{1,0:T(8,128)S(1)}, f32[192,128]{1,0:T(8,128)S(1)}) custom-call(s32[2]{0:T(128)S(1)} %pad_add_fusion.where_ref, f32[24,512]{1,0:T(8,128)S(1)} %get-tuple-element.20.refs_0_, f32[24,512]{1,0:T(8,128)S(1)} %collective-permute-done.3.refs_1_, ...), custom_call_target="tpu_custom_call" | custom-call | tf_op jit(solution)/shard_map/pallas_call | solution.py:544
  46.0 1.6 %collective-permute-start.6 = (f32[192,128]{1,0:T(8,128)S(1)}, f32[192,128]{1,0:T(8,128)S(1)}, u32[]{:S(2)}, u32[]{:S(2)}) collective-permute-start(f32[192,128]{1,0:T(8,128)S(1)} %get-tuple-element.25), channel_id=1, source_target_pairs={{0,1},{1,0},{2,3},{3,2},{4,5},{5,4},{6,7},{7,6},{8,9},{9,8},{10,11... | collective-permute-start | bytes 294920 | tf_op jit(solution)/shard_map/ppermute | solution.py:535
  47.6 2.6 %collective-permute-start.7 = (f32[192,128]{1,0:T(8,128)S(1)}, f32[192,128]{1,0:T(8,128)S(1)}, u32[]{:S(2)}, u32[]{:S(2)}) collective-permute-start(f32[192,128]{1,0:T(8,128)S(1)} %get-tuple-element.26), channel_id=1, source_target_pairs={{0,2},{1,3},{2,0},{3,1},{4,6},{5,7},{6,4},{7,5},{8,10},{9,11},{10,... | collective-permute-start | bytes 294920 | tf_op jit(solution)/shard_map/ppermute | solution.py:535
  50.2 0.3 collective-permute-start.8
  50.4 1.0 %constant_dynamic-slice_fusion = f32[59,1024]{1,0:T(8,128)S(1)} fusion(f32[59,4096]{1,0:T(8,128)} %params_ref.1, s32[]{:T(128)S(6)} %select_n.107), kind=kLoop, calls=%fused_computation.57 | loop fusion | bytes 483332 | tf_op jit(solution)/shard_map/dynamic_slice | solution.py:589
  51.5 0.6 %copy.19 = f32[1,1,8,3,256]{4,2,3,1,0:T(8,128)} copy(f32[1,1,8,3,256]{4,3,2,1,0:T(4,128)S(1)} %bitcast.50) | data formatting | bytes 49152
  52.1 6.2 %collective-permute-done.7.refs_2_ = f32[192,128]{1,0:T(8,128)S(1)} collective-permute-done((f32[192,128]{1,0:T(8,128)S(1)}, f32[192,128]{1,0:T(8,128)S(1)}, u32[]{:S(2)}, u32[]{:S(2)}) %collective-permute-start.7) | collective-permute-done | bytes 98336 | tf_op jit(solution)/shard_map/ppermute | solution.py:535
  58.3 1.6 %shard_map.89 = f32[59,1024]{1,0:T(8,128)} custom-call(f32[192,128]{1,0:T(8,128)S(1)} %get-tuple-element.24.refs_0_, f32[192,128]{1,0:T(8,128)S(1)} %collective-permute-done.6.refs_1_, f32[192,128]{1,0:T(8,128)S(1)} %collective-permute-done.7.refs_2_, f32[192,128]{1,0:T(8,128)S(1)} %collective-permute-done.8.refs_3_, f32[472,128]{1,0:T(8,128)S(1)} %reshape.289.refs_4_), custom_call_target="tpu_custom_call" | custom-call | tf_op jit(solution)/shard_map/pallas_call | solution.py:544
  (24 shorter events, 0.2 us)
Async XLA Ops:
  0.6 0.7 %copy-start.1 = (f32[4,7]{1,0:T(4,128)S(1)}, f32[4,7]{1,0:T(4,128)}, u32[]{:S(2)}) copy-start(f32[4,7]{1,0:T(4,128)} %param.8) | copy-start | bytes 340
  1.5 0.7 %copy-start.4 = (s32[1,1,4,512]{3,2,1,0:T(4,128)S(1)}, s32[1,1,4,512]{3,2,1,0:T(4,128)}, u32[]{:S(2)}) copy-start(s32[1,1,4,512]{3,2,1,0:T(4,128)} %param.9) | copy-start | bytes 24580
  2.4 1.2 %copy-start = (f32[59,4096]{1,0:T(8,128)S(1)}, f32[59,4096]{1,0:T(8,128)}, u32[]{:S(2)}) copy-start(f32[59,4096]{1,0:T(8,128)} %params_ref.1) | copy-start | bytes 2899972
  8.4 6.9 %collective-permute-start = (f32[24,512]{1,0:T(8,128)S(1)}, f32[24,512]{1,0:T(8,128)S(1)}, u32[]{:S(2)}, u32[]{:S(2)}) collective-permute-start(f32[24,512]{1,0:T(8,128)S(1)} %get-tuple-element.16), channel_id=1, source_target_pairs={{0,4},{4,0},{8,12},{12,8},{1,5},{5,1},{9,13},{13,9},{2,6},{6,2},{1... | collective-permute-start | bytes 147464 | tf_op jit(solution)/shard_map/ppermute | solution.py:535
  9.0 6.3 %collective-permute-start.1 = (f32[24,512]{1,0:T(8,128)S(1)}, f32[24,512]{1,0:T(8,128)S(1)}, u32[]{:S(2)}, u32[]{:S(2)}) collective-permute-start(f32[24,512]{1,0:T(8,128)S(1)} %get-tuple-element.17), channel_id=1, source_target_pairs={{0,8},{4,12},{8,0},{12,4},{1,9},{5,13},{9,1},{13,5},{2,10},{6,14},... | collective-permute-start | bytes 147464 | tf_op jit(solution)/shard_map/ppermute | solution.py:535
  11.6 0.7 %copy-start.5 = (s32[1,1,8]{2,1,0:T(1,128)S(1)}, s32[1,1,8]{2,1,0:T(1,128)}, u32[]{:S(2)}) copy-start(s32[1,1,8]{2,1,0:T(1,128)} %param.10) | copy-start | bytes 100
  11.6 3.8 %collective-permute-start.2 = (f32[24,512]{1,0:T(8,128)S(1)}, f32[24,512]{1,0:T(8,128)S(1)}, u32[]{:S(2)}, u32[]{:S(2)}) collective-permute-start(f32[24,512]{1,0:T(8,128)S(1)} %get-tuple-element.18), channel_id=1, source_target_pairs={{0,12},{4,8},{8,4},{12,0},{1,13},{5,9},{9,5},{13,1},{2,14},{6,10},... | collective-permute-start | bytes 147464 | tf_op jit(solution)/shard_map/ppermute | solution.py:535
  12.4 0.7 %copy-start.6 = (s32[1,1,8]{2,1,0:T(1,128)S(1)}, s32[1,1,8]{2,1,0:T(1,128)}, u32[]{:S(2)}) copy-start(s32[1,1,8]{2,1,0:T(1,128)} %param.11) | copy-start | bytes 100
  13.5 0.7 %copy-start.2 = (f32[1,1,8,3,256]{4,2,3,1,0:T(8,128)S(1)}, f32[1,1,8,3,256]{4,2,3,1,0:T(8,128)}, u32[]{:S(2)}) copy-start(f32[1,1,8,3,256]{4,2,3,1,0:T(8,128)} %param.13) | copy-start | bytes 73732
  14.3 0.7 %copy-start.3 = (s32[1,1,8,512]{3,2,1,0:T(8,128)S(1)}, s32[1,1,8,512]{3,2,1,0:T(8,128)}, u32[]{:S(2)}) copy-start(s32[1,1,8,512]{3,2,1,0:T(8,128)} %param.12) | copy-start | bytes 49156
  38.6 2.1 %collective-permute-start.3 = (f32[24,512]{1,0:T(8,128)S(1)}, f32[24,512]{1,0:T(8,128)S(1)}, u32[]{:S(2)}, u32[]{:S(2)}) collective-permute-start(f32[24,512]{1,0:T(8,128)S(1)} %get-tuple-element.21), channel_id=1, source_target_pairs={{0,4},{4,0},{8,12},{12,8},{1,5},{5,1},{9,13},{13,9},{2,6},{6,2},{1... | collective-permute-start | bytes 147464 | tf_op jit(solution)/shard_map/ppermute | solution.py:535
  38.8 4.1 %collective-permute-start.4 = (f32[24,512]{1,0:T(8,128)S(1)}, f32[24,512]{1,0:T(8,128)S(1)}, u32[]{:S(2)}, u32[]{:S(2)}) collective-permute-start(f32[24,512]{1,0:T(8,128)S(1)} %get-tuple-element.22), channel_id=1, source_target_pairs={{0,8},{4,12},{8,0},{12,4},{1,9},{5,13},{9,1},{13,5},{2,10},{6,14},... | collective-permute-start | bytes 147464 | tf_op jit(solution)/shard_map/ppermute | solution.py:535
  40.2 4.0 %collective-permute-start.5 = (f32[24,512]{1,0:T(8,128)S(1)}, f32[24,512]{1,0:T(8,128)S(1)}, u32[]{:S(2)}, u32[]{:S(2)}) collective-permute-start(f32[24,512]{1,0:T(8,128)S(1)} %get-tuple-element.23), channel_id=1, source_target_pairs={{0,12},{4,8},{8,4},{12,0},{1,13},{5,9},{9,5},{13,1},{2,14},{6,10},... | collective-permute-start | bytes 147464 | tf_op jit(solution)/shard_map/ppermute | solution.py:535
  46.0 6.1 %collective-permute-start.6 = (f32[192,128]{1,0:T(8,128)S(1)}, f32[192,128]{1,0:T(8,128)S(1)}, u32[]{:S(2)}, u32[]{:S(2)}) collective-permute-start(f32[192,128]{1,0:T(8,128)S(1)} %get-tuple-element.25), channel_id=1, source_target_pairs={{0,1},{1,0},{2,3},{3,2},{4,5},{5,4},{6,7},{7,6},{8,9},{9,8},{10,11... | collective-permute-start | bytes 294920 | tf_op jit(solution)/shard_map/ppermute | solution.py:535
  47.6 10.7 %collective-permute-start.7 = (f32[192,128]{1,0:T(8,128)S(1)}, f32[192,128]{1,0:T(8,128)S(1)}, u32[]{:S(2)}, u32[]{:S(2)}) collective-permute-start(f32[192,128]{1,0:T(8,128)S(1)} %get-tuple-element.26), channel_id=1, source_target_pairs={{0,2},{1,3},{2,0},{3,1},{4,6},{5,7},{6,4},{7,5},{8,10},{9,11},{10,... | collective-permute-start | bytes 294920 | tf_op jit(solution)/shard_map/ppermute | solution.py:535
  50.2 8.1 %collective-permute-start.8 = (f32[192,128]{1,0:T(8,128)S(1)}, f32[192,128]{1,0:T(8,128)S(1)}, u32[]{:S(2)}, u32[]{:S(2)}) collective-permute-start(f32[192,128]{1,0:T(8,128)S(1)} %get-tuple-element.27), channel_id=1, source_target_pairs={{0,3},{1,2},{2,1},{3,0},{4,7},{5,6},{6,5},{7,4},{8,11},{9,10},{10,... | collective-permute-start | bytes 294920 | tf_op jit(solution)/shard_map/ppermute | solution.py:535

commit v2 on v1

--- a/solution.py
+++ b/solution.py
@@ -12,6 +12,7 @@
 GEOMETRY = 11
 COLOUR_ROW = 12
 SPAN = 256
+CHUNK = 2048
 LOG2_E = 1.4426950408889634
 DEAD = -1e30
 
@@ -97,13 +98,15 @@
 
 def slab_kernel(n_render, views, params_ref, table_ref, index_ref, *rest):
     outs, dense_ref = rest[:n_render], rest[n_render]
-    rows, gaussians = dense_ref.shape
+    rows, gaussians = outs[0].shape[0], params_ref.shape[1]
     cap = index_ref.shape[1]
-    width = 256
-
-    def shade(step, _):
-        lanes = pl.ds(pl.multiple_of(step * width, width), width)
-        dense_ref[0:16, lanes] = params_ref[0:16, lanes]
+    width = 512
+    picks = [(turn, step) for turn in range(n_render) for step in range(cap // 128)]
+    shades = gaussians // width
+
+    def shade(step):
+        lanes = slice(step * width, step * width + width)
+        dense_ref[0:8, lanes] = params_ref[8:16, lanes]
         away = [params_ref[a : a + 1, lanes] + table_ref[:, 13 + a : 14 + a] for a in range(3)]
         inverse = lax.rsqrt(away[0] * away[0] + away[1] * away[1] + away[2] * away[2])
         basis = harmonic_basis(*[part * inverse for part in away])
@@ -112,29 +115,28 @@
             colour = 0.5 + basis[0] * params_ref[base : base + 1, lanes]
             for level in range(1, 16):
                 colour += basis[level] * params_ref[base + level : base + level + 1, lanes]
-            first = COLOUR_ROW + channel * views
+            first = COLOUR_ROW + channel * views - 8
             dense_ref[first : first + views, lanes] = colour
-        return 0
-
-    lax.fori_loop(0, gaussians // width, shade, 0)
-
-    for turn in range(n_render):
-
-        def pick(step, _):
-            lanes = pl.ds(pl.multiple_of(step * 128, 128), 128)
-            index = jnp.broadcast_to(index_ref[turn : turn + 1, lanes], (8, 128))
-            lane, block = index & 127, index >> 7
-            found = [jnp.zeros((8, 128), F32) for _ in range(rows // 8)]
-            for b in range(gaussians // 128):
-                here = block == b
-                for s in range(rows // 8):
-                    piece = dense_ref[8 * s : 8 * s + 8, 128 * b : 128 * b + 128]
-                    found[s] = jnp.where(here, lane_pick(piece, lane), found[s])
-            for s in range(rows // 8):
-                outs[turn][8 * s : 8 * s + 8, lanes] = found[s]
-            return 0
-
-        lax.fori_loop(0, cap // 128, pick, 0)
+
+    def pick(source, groups, skip, turn, step):
+        lanes = slice(128 * step, 128 * step + 128)
+        index = jnp.broadcast_to(index_ref[turn : turn + 1, lanes], (8, 128))
+        lane, block = index & 127, index >> 7
+        found = [jnp.zeros((8, 128), F32) for _ in range(groups)]
+        for b in range(gaussians // 128):
+            here = block == b
+            for s in range(groups):
+                piece = source[8 * s : 8 * s + 8, 128 * b : 128 * b + 128]
+                found[s] = jnp.where(here, lane_pick(piece, lane), found[s])
+        for s in range(groups):
+            outs[turn][8 * (s + skip) : 8 * (s + skip) + 8, lanes] = found[s]
+
+    for step in range(shades):
+        shade(step)
+        for turn, at in picks[step * len(picks) // shades : (step + 1) * len(picks) // shades]:
+            pick(params_ref, 1, 0, turn, at)
+    for turn, at in picks:
+        pick(dense_ref, rows // 8 - 1, 1, turn, at)
 
 
 def entry_coefficients(raw, cam):
@@ -179,22 +181,22 @@
     ]
 
 
-def monomials(rows):
-    row = lax.broadcasted_iota(jnp.int32, (rows, PIXELS), 0) & 7
-    pixel = lax.broadcasted_iota(jnp.int32, (rows, PIXELS), 1)
+def monomials(shape, axis):
+    number = lax.broadcasted_iota(jnp.int32, shape, axis)
+    pixel = lax.broadcasted_iota(jnp.int32, shape, 1 - axis)
     x = (pixel & 15).astype(F32) - 7.5
     y = (pixel >> 4).astype(F32) - 7.5
-    value = jnp.where(row == 0, x * x, 0.0)
-    for number, term in ((1, x * y), (2, y * y), (3, x), (4, y), (5, jnp.ones_like(x))):
-        value = jnp.where(row == number, term, value)
-    return value
+    value = jnp.zeros(shape, F32)
+    for at, term in enumerate((x * x, x * y, y * y, x, y, jnp.ones_like(x))):
+        value = jnp.where((number & 7) == at, term, value)
+    return value, number
 
 
 def render_kernel(n_render, views, where_ref, *refs):
     blocks, refs = refs[:n_render], refs[n_render:]
     slot_ref, cam_ref, target_ref, refs = refs[0], refs[1], refs[2], refs[3:]
     image_ref, outs, refs = refs[0], refs[1 : 1 + n_render], refs[1 + n_render :]
-    raw_ref, stack_ref, wide_ref, tall_ref, alpha_ref, weight_ref, high_ref, low_ref, lhs_ref, acc_ref = refs
+    raw_ref, stack_ref, wide_ref, alpha_ref, weight_ref, shade_ref, high_ref, low_ref, pass_ref, enter_ref, behind_ref, lhs_ref, hot_ref, acc_ref = refs
     tiles = target_ref.shape[0]
     entry_rows = slot_ref.shape[0]
     entries = entry_rows * 128
@@ -241,7 +243,7 @@
         coefficient = entry_coefficients([raw_ref[p, here, :] for p in range(GEOMETRY)], cam_rows())
         row = lax.broadcasted_iota(jnp.int32, (8, 128), 0) + group * 8
         lane = lax.broadcasted_iota(jnp.int32, (8, 128), 1)
-        order = (row * 128 + lane) // tiles
+        order = (lane // tiles) * entry_rows + row
         live = order < jnp.broadcast_to(cam_ref[16:17, :], (8, 128)).astype(jnp.int32)
         for c in range(6):
             value = coefficient[c] * LOG2_E
@@ -256,10 +258,13 @@
 
     lax.fori_loop(0, groups, forward_entries, 0)
 
-    wide_ref[96:128, :] = jnp.zeros((32, entries), BF16)
-    own_tile = (lax.broadcasted_iota(jnp.int32, (8, 128), 1) & (tiles - 1)) == lax.broadcasted_iota(
-        jnp.int32, (8, 128), 0
-    )
+    wide_ref[...] = jnp.zeros_like(wide_ref)
+    lane = lax.broadcasted_iota(jnp.int32, (8, 128), 1)
+    own_tile = (lane & (tiles - 1)) == lax.broadcasted_iota(jnp.int32, (8, 128), 0)
+    chunks = entries // CHUNK
+
+    def chunk_of(chunk):
+        return pl.ds(pl.multiple_of(chunk * CHUNK, CHUNK), CHUNK)
 
     def widen(row, _):
         value = stack_ref[pl.ds(row, 16, stride=entry_rows), :]
@@ -272,93 +277,126 @@
                 for ch in range(3)
             ]
 
-        pieces = [high[0:8], middle[0:8], low[0:8]] + spread(high) * 2 + spread(middle)
+        zero = jnp.zeros((8, 128), F32)
+        bright = spread(high)
+        pieces = [high[0:8], middle[0:8], low[0:8], zero] + bright + spread(middle) + bright + [zero]
         lanes = pl.ds(pl.multiple_of(row * 128, 128), 128)
-        wide_ref[0:96, lanes] = jnp.concatenate(pieces, axis=0).astype(BF16)
+        wide_ref[:, lanes] = jnp.concatenate(pieces, axis=0).astype(BF16)
         return 0
 
     lax.fori_loop(0, entry_rows, widen, 0)
 
-    eye = (
-        lax.broadcasted_iota(jnp.int32, (256, 256), 0) == lax.broadcasted_iota(jnp.int32, (256, 256), 1)
-    ).astype(F32).astype(BF16)
-    left = jnp.concatenate([monomials(24), jnp.zeros((104, PIXELS), F32)], axis=0).astype(BF16)
-    moment_rows = monomials(16)
-    moment_rows = jnp.where(
-        lax.broadcasted_iota(jnp.int32, (16, PIXELS), 0) < 8, moment_rows, 0.0
-    ).astype(BF16)
-    steps = 256 // tiles
-
-    def forward(chunk, carry):
-        passing, image = carry
-        at = pl.ds(pl.multiple_of(chunk * 256, 256), 256)
-        tall = dot_lanes(eye, wide_ref[:, at]).astype(BF16)
-        tall_ref[at, :] = tall
-        alpha = jnp.exp2(dot_plain(tall, left))
-        alpha_ref[at, :] = alpha
+    value, number = monomials((PIXELS, 32), 1)
+    left = jnp.where(number < 24, value, 0.0).astype(BF16)
+    value, number = monomials((16, PIXELS), 0)
+    moment_rows = jnp.where(number < 8, value, 0.0).astype(BF16)
+    segment = lax.broadcasted_iota(jnp.int32, (PIXELS, 128), 1) // tiles
+    last = 128 // tiles - 1
+
+    def attenuate(chunk, _):
+        alpha = jnp.exp2(dot_plain(left, wide_ref[0:32, chunk_of(chunk)]))
+        alpha_ref[:, chunk_of(chunk)] = alpha
+        passing = pass_ref[...]
         weights = []
-        for k in range(steps):
-            weight = passing * alpha[tiles * k : tiles * k + tiles, :]
+        for k in range(CHUNK // 128):
+            weight = passing * alpha[:, 128 * k : 128 * k + 128]
             passing = passing - weight
             weights.append(weight)
-        weight = jnp.concatenate(weights, axis=0)
-        weight_ref[at, :] = weight
-        high, low = high_low(weight)
-        high, low = high.astype(BF16), low.astype(BF16)
-        high_ref[at, :] = high
-        low_ref[at, :] = low
-        colours = wide_ref[48:96, at]
-        image = image + (dot_plain(colours, high) + dot_plain(colours, low))
-        return passing, image
-
-    remain, image = lax.fori_loop(
-        0,
-        entries // 256,
-        forward,
-        (jnp.ones((tiles, PIXELS), F32), jnp.zeros((48, PIXELS), F32)),
-    )
+        weight_ref[:, chunk_of(chunk)] = jnp.concatenate(weights, axis=1)
+        pass_ref[...] = passing
+        return 0
+
+    pass_ref[...] = jnp.ones_like(pass_ref)
+    lax.fori_loop(0, chunks, attenuate, 0)
+
+    through = pass_ref[...]
+    hop = 1
+    while hop <= last:
+        through = through * jnp.where(segment >= hop, pltpu.roll(through, tiles * hop, 1), 1.0)
+        hop *= 2
+    enter_ref[...] = jnp.where(segment >= 1, pltpu.roll(through, tiles, 1), 1.0)
+    remain = through.T[tiles * last : tiles * last + tiles, :]
+
+    def paint(chunk, image):
+        weight = weight_ref[:, chunk_of(chunk)] * jnp.concatenate([enter_ref[...]] * (CHUNK // 128), axis=1)
+        weight_ref[:, chunk_of(chunk)] = weight
+        high = weight.astype(BF16)
+        low = (weight - high.astype(F32)).astype(BF16)
+        high_ref[:, chunk_of(chunk)] = high
+        low_ref[:, chunk_of(chunk)] = low
+        colours = wide_ref[32:80, chunk_of(chunk)]
+        return image + (dot_lanes(colours, high) + dot_lanes(colours, low))
+
+    image = lax.fori_loop(0, chunks, paint, jnp.zeros((48, PIXELS), F32))
     image = image[0:24] + image[24:48]
     residual = []
     for channel in range(3):
         shown = image[8 * channel : 8 * channel + 8] + backdrop * remain
         image_ref[:, channel, :] = shown
         residual.append(shown - target_ref[:, channel, :])
-    behind = backdrop * (residual[0] + residual[1] + residual[2])
     high, low = high_low(jnp.concatenate(residual, axis=0))
-    zeros = jnp.zeros((24, PIXELS), F32)
-    right = jnp.concatenate([zeros, high, low, high, jnp.zeros((32, PIXELS), F32)], axis=0).astype(BF16)
     both = jnp.concatenate([high, low], axis=0).astype(BF16)
-    own_wide = (lax.broadcasted_iota(jnp.int32, (8, 256), 1) & (tiles - 1)) == lax.broadcasted_iota(
-        jnp.int32, (8, 256), 0
-    )
-
-    def backward(step, behind):
-        chunk = entries // 256 - 1 - step
-        at = pl.ds(pl.multiple_of(chunk * 256, 256), 256)
-        shade = dot_plain(tall_ref[at, :], right)
-        alpha, weight = alpha_ref[at, :], weight_ref[at, :]
-        slopes = [None] * steps
-        for k in reversed(range(steps)):
-            cut = slice(tiles * k, tiles * k + tiles)
-            gap = shade[cut, :] - behind
-            slopes[k] = weight[cut, :] * gap
-            behind = behind + alpha[cut, :] * gap
-        high, low = high_low(jnp.concatenate(slopes, axis=0))
-        moments = dot_lanes(moment_rows, high.astype(BF16)) + dot_lanes(moment_rows, low.astype(BF16))
-        tint = dot_lanes(both, high_ref[at, :]) + dot_lanes(both, low_ref[at, :])
+    right = jnp.concatenate([high, high, low, jnp.zeros((56, PIXELS), F32)], axis=0).T.astype(BF16)
+    right = right[:, 0:80]
+    number = lax.broadcasted_iota(jnp.int32, (80, 128), 0)
+    unit = (number & (tiles - 1)) == (lax.broadcasted_iota(jnp.int32, (80, 128), 1) & (tiles - 1))
+    unit = jnp.where(unit & ((number < 24) | ((number >= 48) & (number < 72))), backdrop, 0.0)
+    open_end = dot_plain(right, unit.astype(BF16))
+
+    def shade(step, _):
+        chunk = chunks - 1 - step
+        colour = dot_plain(right, wide_ref[32:112, chunk_of(chunk)])
+        shade_ref[:, chunk_of(chunk)] = colour
+        alpha = alpha_ref[:, chunk_of(chunk)]
+        behind = behind_ref[...]
+        for k in reversed(range(CHUNK // 128)):
+            cut = slice(128 * k, 128 * k + 128)
+            behind = behind + alpha[:, cut] * (colour[:, cut] - behind)
+        behind_ref[...] = behind
+        return 0
+
+    behind_ref[...] = jnp.zeros_like(behind_ref)
+    lax.fori_loop(0, chunks, shade, 0)
+
+    keep, add = pass_ref[...], behind_ref[...]
+    hop = 1
+    while hop <= last:
+        inside = segment + hop <= last
+        add = add + keep * jnp.where(inside, pltpu.roll(add, 128 - tiles * hop, 1), 0.0)
+        keep = keep * jnp.where(inside, pltpu.roll(keep, 128 - tiles * hop, 1), 1.0)
+        hop *= 2
+    behind_ref[...] = jnp.where(
+        segment < last, pltpu.roll(add + keep * open_end, 128 - tiles, 1), open_end
+    )
+
+    def descend(step, _):
+        chunk = chunks - 1 - step
+        behind = behind_ref[...]
+        slopes = [None] * (CHUNK // 128)
+        for k in reversed(range(CHUNK // 128)):
+            cut = pl.ds(pl.multiple_of(chunk * CHUNK + 128 * k, 128), 128)
+            gap = shade_ref[:, cut] - behind
+            behind = behind + alpha_ref[:, cut] * gap
+            slopes[k] = weight_ref[:, cut] * gap
+        behind_ref[...] = behind
+        slope = jnp.concatenate(slopes, axis=1)
+        high = slope.astype(BF16)
+        low = (slope - high.astype(F32)).astype(BF16)
+        moments = dot_plain(moment_rows, high) + dot_plain(moment_rows, low)
+        tint = dot_plain(both, high_ref[:, chunk_of(chunk)]) + dot_plain(both, low_ref[:, chunk_of(chunk)])
         tint = tint[0:24] + tint[24:48]
-        for half in range(2):
-            row = chunk * 2 + half
-            cut = slice(128 * half, 128 * half + 128)
+        for k in range(CHUNK // 128):
+            row = chunk * (CHUNK // 128) + k
+            cut = slice(128 * k, 128 * k + 128)
             stack_ref[pl.ds(row, 8, stride=entry_rows), :] = moments[0:8, cut]
             for channel in range(3):
                 part = jnp.where(own_tile, tint[8 * channel : 8 * channel + 8, cut], 0.0)
                 stack_ref[pl.ds((8 + channel) * entry_rows + row, 1), :] = jnp.sum(
                     part, axis=0, keepdims=True
                 )
-        return behind
-
-    lax.fori_loop(0, entries // 256, backward, behind)
+        return 0
+
+    lax.fori_loop(0, chunks, descend, 0)
 
     def backward_entries(group, _):
         here = pl.ds(pl.multiple_of(group * 8, 8), 8)
@@ -382,53 +420,49 @@
     lax.fori_loop(0, groups, backward_entries, 0)
 
     spans = n_render * cap // SPAN
-    acc_ref[...] = jnp.zeros_like(acc_ref)
+    half_rows = rows * spans
     view = cam_ref[15:16, :].astype(jnp.int32)
-    view = jnp.concatenate([view] * 4, axis=1)
-
-    def scatter(step, _):
-        def line(ref, *lead):
-            return jnp.concatenate(
-                [ref[lead + (pl.ds(step * 4 + i, 1), slice(None))] for i in range(4)], axis=1
-            )
-
-        slot = line(slot_ref)
+
+    def spread_out(row, _):
+        at_lanes = pl.ds(pl.multiple_of(row * 128, 128), 128)
+        slot = slot_ref[pl.ds(row, 1), :]
         span, lane = slot // SPAN, slot & (SPAN - 1)
-        lanes_of = jnp.where(
-            lax.broadcasted_iota(jnp.int32, (SPAN, 512), 0) == jnp.broadcast_to(lane, (SPAN, 512)), 1.0, 0.0
-        ).astype(BF16)
-        in_span = lax.broadcasted_iota(jnp.int32, (spans, 512), 0) == jnp.broadcast_to(span, (spans, 512))
+        lanes_of = lax.broadcasted_iota(jnp.int32, (SPAN, 128), 0) == jnp.broadcast_to(lane, (SPAN, 128))
+        hot_ref[:, at_lanes] = jnp.where(lanes_of, 1.0, 0.0).astype(BF16)
+        in_span = lax.broadcasted_iota(jnp.int32, (spans, 128), 0) == jnp.broadcast_to(span, (spans, 128))
         key = view * spans + span
-        in_view = lax.broadcasted_iota(jnp.int32, (views * spans, 512), 0) == jnp.broadcast_to(
-            key, (views * spans, 512)
+        in_view = lax.broadcasted_iota(jnp.int32, (views * spans, 128), 0) == jnp.broadcast_to(
+            key, (views * spans, 128)
         )
-        half_rows = rows * spans
         for part in range(2):
             base = part * half_rows
             pieces = []
             for p in range(COLOUR_ROW):
                 if p < GEOMETRY:
-                    value = line(raw_ref, part * (GEOMETRY + 3) + p)
-                    value = jnp.broadcast_to(value, (spans, 512))
-                    pieces.append(jnp.where(in_span, value, 0.0))
+                    value = raw_ref[part * (GEOMETRY + 3) + p, pl.ds(row, 1), :]
+                    pieces.append(jnp.where(in_span, jnp.broadcast_to(value, (spans, 128)), 0.0))
                 else:
-                    pieces.append(jnp.zeros((spans, 512), F32))
+                    pieces.append(jnp.zeros((spans, 128), F32))
                 if len(pieces) == 2:
                     at = base + (p - 1) * spans
-                    lhs_ref[at : at + 2 * spans, :] = jnp.concatenate(pieces, axis=0).astype(BF16)
+                    lhs_ref[at : at + 2 * spans, at_lanes] = jnp.concatenate(pieces, axis=0).astype(BF16)
                     pieces = []
             for channel in range(3):
-                value = line(raw_ref, part * (GEOMETRY + 3) + GEOMETRY + channel)
-                value = jnp.where(in_view, jnp.broadcast_to(value, (views * spans, 512)), 0.0)
+                value = raw_ref[part * (GEOMETRY + 3) + GEOMETRY + channel, pl.ds(row, 1), :]
+                value = jnp.where(in_view, jnp.broadcast_to(value, (views * spans, 128)), 0.0)
                 at = base + (COLOUR_ROW + channel * views) * spans
-                lhs_ref[at : at + views * spans, :] = value.astype(BF16)
-        product = dot_lanes(lhs_ref[...], lanes_of)
-        for half in range(SPAN // 128):
-            at = slice(half * 2 * half_rows, (half + 1) * 2 * half_rows)
-            acc_ref[at, :] += product[:, 128 * half : 128 * half + 128]
+                lhs_ref[at : at + views * spans, at_lanes] = value.astype(BF16)
+
+    def spread_rows(step, _):
+        for i in range(4):
+            spread_out(step * 4 + i, 0)
         return 0
 
-    lax.fori_loop(0, entry_rows // 4, scatter, 0)
+    lax.fori_loop(0, entry_rows // 4, spread_rows, 0)
+    product = dot_lanes(lhs_ref[...], hot_ref[...])
+    for half in range(SPAN // 128):
+        at = slice(half * 2 * half_rows, (half + 1) * 2 * half_rows)
+        acc_ref[at, :] = product[:, 128 * half : 128 * half + 128]
     for turn in range(n_render):
         for part in range(cap // SPAN):
             span = (me ^ turn) * (cap // SPAN) + part
@@ -445,33 +479,29 @@
 def collect_kernel(n_render, n_view, where_ref, *refs):
     blocks, refs = refs[:n_render], refs[n_render:]
     index_ref, origin_ref, refs = refs[0], refs[1], refs[2:]
-    outs, (lhs_ref, acc_ref) = refs[:n_view], refs[n_view:]
+    outs, (lhs_ref, hot_ref, acc_ref) = refs[:n_view], refs[n_view:]
     rows, cap = blocks[0].shape
     own = outs[0].shape[0] // rows * 128
     gaussians = own * n_view
     spans = gaussians // SPAN
     column = where_ref[1]
     for turn in range(n_render):
+        lanes = slice(turn * cap, (turn + 1) * cap)
         index = index_ref[turn : turn + 1, :]
         span, lane = index // SPAN, index & (SPAN - 1)
-        lanes_of = jnp.where(
-            lax.broadcasted_iota(jnp.int32, (SPAN, cap), 0) == jnp.broadcast_to(lane, (SPAN, cap)), 1.0, 0.0
-        ).astype(BF16)
+        hot = lax.broadcasted_iota(jnp.int32, (SPAN, cap), 0) == jnp.broadcast_to(lane, (SPAN, cap))
+        hot_ref[:, lanes] = jnp.where(hot, 1.0, 0.0).astype(BF16)
         in_span = lax.broadcasted_iota(jnp.int32, (spans, cap), 0) == jnp.broadcast_to(span, (spans, cap))
         high, low = high_low(blocks[turn][...])
         for part, value in ((0, high), (1, low)):
             for p in range(rows):
                 at = (part * rows + p) * spans
                 piece = jnp.broadcast_to(value[p : p + 1, :], (spans, cap))
-                lhs_ref[at : at + spans, :] = jnp.where(in_span, piece, 0.0).astype(BF16)
-        product = dot_lanes(lhs_ref[...], lanes_of)
-        for half in range(2):
-            at = slice(half * 2 * rows * spans, (half + 1) * 2 * rows * spans)
-            piece = product[:, 128 * half : 128 * half + 128]
-            if turn == 0:
-                acc_ref[at, :] = piece
-            else:
-                acc_ref[at, :] += piece
+                lhs_ref[at : at + spans, lanes] = jnp.where(in_span, piece, 0.0).astype(BF16)
+    product = dot_lanes(lhs_ref[...], hot_ref[...])
+    for half in range(2):
+        at = slice(half * 2 * rows * spans, (half + 1) * 2 * rows * spans)
+        acc_ref[at, :] = product[:, 128 * half : 128 * half + 128]
     strips = own // 128
     for turn in range(n_view):
         for strip in range(strips):
@@ -551,23 +581,9 @@
     )(*args)
 
 
-def body(n_render, n_view, params, cameras, send_index, tile_id, tile_count, tile_slot, targets):
-    index = send_index[0, 0]
-    slot = tile_slot[0, 0]
-    code = tile_id[0, 0]
-    live = tile_count[0, 0]
-    wanted = targets[0, 0]
-    views = cameras.shape[0]
-    gaussians = params.shape[1]
-    cap = index.shape[1]
+def render(n_render, views, where, arrived, table, code, live, slot, wanted):
     tiles, length = slot.shape
-    own = gaussians // n_view
-    rows = -(-(COLOUR_ROW + 3 * views) // 8) * 8
-    order = lax.axis_index("render") ^ jnp.arange(n_render, dtype=jnp.int32)
-    index = sum(jnp.where((order == o)[:, None], index[o][None], 0) for o in range(n_render))
-    where = jnp.stack([lax.axis_index("render"), lax.axis_index("view")]).astype(jnp.int32)
-
-    table = camera_table(cameras)
+    rows, cap = arrived[0].shape
     view = code // (CROP * CROP)
     cell = code % (CROP * CROP)
     tile_table = sum(
@@ -584,37 +600,28 @@
     )
     lane_table = jnp.concatenate([tile_table, extra, jnp.zeros((tiles, 7), F32)], axis=1).T
     lane_table = jnp.tile(lane_table, (1, 128 // tiles))
-    slot_lanes = slot.T.reshape(-1, 128)
-    origin = jnp.pad(table[:, 13:16].reshape(1, 3 * views), ((0, 0), (0, 128 - 3 * views)))
-    mine = lax.dynamic_slice_in_dim(params, lax.axis_index("view") * own, own, 1).reshape(-1, 128)
-
-    block = jax.ShapeDtypeStruct((rows, cap), F32)
-    sent = call(
-        partial(slab_kernel, n_render, views),
-        [block] * n_render,
-        [pltpu.VMEM((rows, gaussians), F32)],
-        0,
-        params,
-        table,
-        index,
-    )
-    arrived = swap(list(sent), "render")
+    slot_lanes = slot.reshape(tiles, 128 // tiles, -1).transpose(2, 1, 0).reshape(-1, 128)
     entries = tiles * length
     entry_rows = entries // 128
     spans = n_render * cap // SPAN
-    image, *returned = call(
+    return call(
         partial(render_kernel, n_render, views),
-        [jax.ShapeDtypeStruct(wanted.shape, F32)] + [block] * n_render,
+        [jax.ShapeDtypeStruct(wanted.shape, F32)]
+        + [jax.ShapeDtypeStruct((rows, cap), F32)] * n_render,
         [
             pltpu.VMEM((2 * (GEOMETRY + 3), entry_rows, 128), F32),
             pltpu.VMEM((16 * entry_rows, 128), F32),
-            pltpu.VMEM((128, entries), BF16),
-            pltpu.VMEM((entries, 128), BF16),
-            pltpu.VMEM((entries, PIXELS), F32),
-            pltpu.VMEM((entries, PIXELS), F32),
-            pltpu.VMEM((entries, PIXELS), BF16),
-            pltpu.VMEM((entries, PIXELS), BF16),
-            pltpu.VMEM((2 * rows * spans, 512), BF16),
+            pltpu.VMEM((112, entries), BF16),
+            pltpu.VMEM((PIXELS, entries), F32),
+            pltpu.VMEM((PIXELS, entries), F32),
+            pltpu.VMEM((PIXELS, entries), F32),
+            pltpu.VMEM((PIXELS, entries), BF16),
+            pltpu.VMEM((PIXELS, entries), BF16),
+            pltpu.VMEM((PIXELS, 128), F32),
+            pltpu.VMEM((PIXELS, 128), F32),
+            pltpu.VMEM((PIXELS, 128), F32),
+            pltpu.VMEM((2 * rows * spans, entries), BF16),
+            pltpu.VMEM((SPAN, entries), BF16),
             pltpu.VMEM((4 * rows * spans, 128), F32),
         ],
         1,
@@ -624,14 +631,31 @@
         lane_table,
         wanted,
     )
-    homed = swap(list(returned), "render")
-    slab_spans = gaussians // SPAN
-    shares = call(
+
+
+def slab(n_render, views, params, table, index):
+    rows = -(-(COLOUR_ROW + 3 * views) // 8) * 8
+    return call(
+        partial(slab_kernel, n_render, views),
+        [jax.ShapeDtypeStruct((rows, index.shape[1]), F32)] * n_render,
+        [pltpu.VMEM((rows - 8, params.shape[1]), F32)],
+        0,
+        params,
+        table,
+        index,
+    )
+
+
+def collect(n_render, n_view, where, homed, index, origin, own):
+    rows, cap = homed[0].shape
+    spans = n_view * own // SPAN
+    return call(
         partial(collect_kernel, n_render, n_view),
         [jax.ShapeDtypeStruct((rows * own // 128, 128), F32)] * n_view,
         [
-            pltpu.VMEM((2 * rows * slab_spans, cap), BF16),
-            pltpu.VMEM((4 * rows * slab_spans, 128), F32),
+            pltpu.VMEM((2 * rows * spans, n_render * cap), BF16),
+            pltpu.VMEM((SPAN, n_render * cap), BF16),
+            pltpu.VMEM((4 * rows * spans, 128), F32),
         ],
         1,
         where,
@@ -639,7 +663,33 @@
         index,
         origin,
     )
-    owned = swap(list(shares), "view")
+
+
+def body(n_render, n_view, params, cameras, send_index, tile_id, tile_count, tile_slot, targets):
+    index = send_index[0, 0]
+    views = cameras.shape[0]
+    own = params.shape[1] // n_view
+    order = lax.axis_index("render") ^ jnp.arange(n_render, dtype=jnp.int32)
+    index = sum(jnp.where((order == o)[:, None], index[o][None], 0) for o in range(n_render))
+    where = jnp.stack([lax.axis_index("render"), lax.axis_index("view")]).astype(jnp.int32)
+    table = camera_table(cameras)
+    origin = jnp.pad(table[:, 13:16].reshape(1, 3 * views), ((0, 0), (0, 128 - 3 * views)))
+    mine = lax.dynamic_slice_in_dim(params, lax.axis_index("view") * own, own, 1).reshape(-1, 128)
+
+    arrived = swap(list(slab(n_render, views, params, table, index)), "render")
+    image, *returned = render(
+        n_render,
+        views,
+        where,
+        arrived,
+        table,
+        tile_id[0, 0],
+        tile_count[0, 0],
+        tile_slot[0, 0],
+        targets[0, 0],
+    )
+    homed = swap(returned, "render")
+    owned = swap(list(collect(n_render, n_view, where, homed, index, origin, own)), "view")
     (gradients,) = call(
         partial(owner_kernel, n_view, views),
         [jax.ShapeDtypeStruct((params.shape[0], own), F32)],

time: 60.3 us -> 49 us (0.81)
  Pallas kernels: 31.5 us -> 20.4 us
    pallas_call x4, Pallas kernels: 31.5 us -> 20.4 us  [call(): pl.pallas_call(kernel, out_shape=out_shape, in_specs=specs, out_specs=[pl...]
  transfers between devices with their start and end apart: 9 -> 9, of which waited for: 3 -> 3; matrix products, arithmetic and copies ran while one was open for 5% -> 6% of each run, Pallas kernels for 0% -> 0%
where the time goes in v2:
time: 49 us; the launch traced here: 48.7 us
  Pallas kernels  20.4 us (42%)
  waiting for transfers between devices  9.69 us (20%)
  starting transfers between devices  9.55 us (19%)
  local copies, waits for them, and re-layouts  7.73 us (16%)
  between operations  0.76 us (2%)
  other arithmetic  0.53 us (1%)
    pallas_call x4, Pallas kernels, call(): pl.pallas_call(kernel, out_shape=out_shape, in_specs=specs, out_specs=[pl...  20.4 us
    ppermute x9, waiting for transfers between devices, swap(): lax.ppermute(blocks[turn], axis, [(i, i ^ turn) for i in range(n)])  9.69 us
    ppermute x9, starting transfers between devices, swap(): lax.ppermute(blocks[turn], axis, [(i, i ^ turn) for i in range(n)])  9.55 us
    unnamed x16, local copies, waits for them, and re-layouts  5.69 us
  transfers between devices with their start and end apart: 9, of which 3 were waited for; matrix products, arithmetic and copies ran while one was open for 6% of the time, Pallas kernels for 0%

profile of v2, /device:TPU:0, one launch (start us, length us, event | category | flops | bytes accessed | tf_op | source)
XLA Modules:
  0.0 48.7 jit_solution(16087822225993164011)
XLA Ops:
  0.7 0.6 %copy-done.1 = f32[4,7]{1,0:T(4,128)S(1)} copy-done((f32[4,7]{1,0:T(4,128)S(1)}, f32[4,7]{1,0:T(4,128)}, u32[]{:S(2)}) %copy-start.1) | copy-done | bytes 136
  1.3 0.1 slice.76
  1.4 0.1 multiply_add_fusion.1
  1.5 0.1 multiply_add_fusion
  1.6 0.6 %copy-done.4 = s32[1,1,4,512]{3,2,1,0:T(4,128)S(1)} copy-done((s32[1,1,4,512]{3,2,1,0:T(4,128)S(1)}, s32[1,1,4,512]{3,2,1,0:T(4,128)}, u32[]{:S(2)}) %copy-start.4) | copy-done | bytes 8216
  2.2 0.1 select_add_fusion.index_ref.refs_4_
  2.3 0.1 stack.15.table_ref
  2.4 0.0 copy-start
  2.4 1.2 %copy-done = f32[59,4096]{1,0:T(8,128)S(1)} copy-done((f32[59,4096]{1,0:T(8,128)S(1)}, f32[59,4096]{1,0:T(8,128)}, u32[]{:S(2)}) %copy-start) | copy-done | bytes 966680
  3.6 2.5 %shard_map.86 = (f32[24,512]{1,0:T(8,128)S(1)}, f32[24,512]{1,0:T(8,128)S(1)}, f32[24,512]{1,0:T(8,128)S(1)}, f32[24,512]{1,0:T(8,128)S(1)}) custom-call(f32[59,4096]{1,0:T(8,128)S(1)} %copy-done, f32[4,16]{1,0:T(4,128)S(1)} %stack.15.table_ref, s32[4,512]{1,0:T(4,128)S(1)} %select_add_fusion.index_ref.refs_4_), custom_call_target="tpu_custom_call" | custom-call | tf_op jit(solution)/shard_map/pallas_call | solution.py:574
  6.2 0.5 %collective-permute-start = (f32[24,512]{1,0:T(8,128)S(1)}, f32[24,512]{1,0:T(8,128)S(1)}, u32[]{:S(2)}, u32[]{:S(2)}) collective-permute-start(f32[24,512]{1,0:T(8,128)S(1)} %get-tuple-element.16), channel_id=1, source_target_pairs={{0,4},{4,0},{8,12},{12,8},{1,5},{5,1},{9,13},{13,9},{2,6},{6,2},{1... | collective-permute-start | bytes 147464 | tf_op jit(solution)/shard_map/ppermute | solution.py:565
  6.7 2.6 %collective-permute-start.1 = (f32[24,512]{1,0:T(8,128)S(1)}, f32[24,512]{1,0:T(8,128)S(1)}, u32[]{:S(2)}, u32[]{:S(2)}) collective-permute-start(f32[24,512]{1,0:T(8,128)S(1)} %get-tuple-element.17), channel_id=1, source_target_pairs={{0,8},{4,12},{8,0},{12,4},{1,9},{5,13},{9,1},{13,5},{2,10},{6,14},... | collective-permute-start | bytes 147464 | tf_op jit(solution)/shard_map/ppermute | solution.py:565
  9.3 0.1 collective-permute-start.2
  9.3 0.6 %copy-done.5 = s32[1,1,8]{2,1,0:T(1,128)S(1)} copy-done((s32[1,1,8]{2,1,0:T(1,128)S(1)}, s32[1,1,8]{2,1,0:T(1,128)}, u32[]{:S(2)}) %copy-start.5) | copy-done | bytes 56
  10.0 0.1 stack.16
  10.1 0.7 %copy-done.6 = s32[1,1,8]{2,1,0:T(1,128)S(1)} copy-done((s32[1,1,8]{2,1,0:T(1,128)S(1)}, s32[1,1,8]{2,1,0:T(1,128)}, u32[]{:S(2)}) %copy-start.6) | copy-done | bytes 56
  10.8 0.1 copy.13
  10.9 0.1 copy.14
  10.9 0.1 copy.15
  11.0 0.1 copy.16
  11.1 0.1 select_add_fusion.1
  11.2 0.1 concatenate.8
  11.3 0.1 pad_add_fusion.where_ref
  11.3 0.7 %copy-done.2 = f32[1,1,8,3,256]{4,2,3,1,0:T(8,128)S(1)} copy-done((f32[1,1,8,3,256]{4,2,3,1,0:T(8,128)S(1)}, f32[1,1,8,3,256]{4,2,3,1,0:T(8,128)}, u32[]{:S(2)}) %copy-start.2) | copy-done | bytes 24600
  12.0 0.0 copy-start.3
  12.0 0.1 copy.19.refs_5_
  12.1 0.7 %copy-done.3 = s32[1,1,8,512]{3,2,1,0:T(8,128)S(1)} copy-done((s32[1,1,8,512]{3,2,1,0:T(8,128)S(1)}, s32[1,1,8,512]{3,2,1,0:T(8,128)}, u32[]{:S(2)}) %copy-start.3) | copy-done | bytes 16408
  12.7 0.1 reshape_squeeze.3
  12.8 0.1 copy.18.refs_4_
  12.9 0.0 collective-permute-done.refs_1_
  12.9 0.0 collective-permute-done.1.refs_2_
  12.9 0.0 collective-permute-done.2.refs_3_
  13.0 14.4 %shard_map.87 = (f32[8,3,256]{2,1,0:T(4,128)S(1)}, f32[24,512]{1,0:T(8,128)S(1)}, f32[24,512]{1,0:T(8,128)S(1)}, f32[24,512]{1,0:T(8,128)S(1)}, f32[24,512]{1,0:T(8,128)S(1)}) custom-call(s32[2]{0:T(128)S(1)} %pad_add_fusion.where_ref, f32[24,512]{1,0:T(8,128)S(1)} %get-tuple-element.15.refs_0_, f32[24,512]{1,0:T(8,128)S(1)} %collective-permute-done.refs_1_, ...), custom_call_target="tpu_custom_call" | custom-call | tf_op jit(solution)/shard_map/pallas_call | solution.py:574
  27.4 0.2 collective-permute-start.3
  27.6 1.3 %collective-permute-start.4 = (f32[24,512]{1,0:T(8,128)S(1)}, f32[24,512]{1,0:T(8,128)S(1)}, u32[]{:S(2)}, u32[]{:S(2)}) collective-permute-start(f32[24,512]{1,0:T(8,128)S(1)} %get-tuple-element.22), channel_id=1, source_target_pairs={{0,8},{4,12},{8,0},{12,4},{1,9},{5,13},{9,1},{13,5},{2,10},{6,14},... | collective-permute-start | bytes 147464 | tf_op jit(solution)/shard_map/ppermute | solution.py:565
  28.9 0.4 collective-permute-start.5
  29.3 0.1 pad_maximum_fusion
  29.4 0.1 reshape.288
  29.5 2.2 %collective-permute-done.4.refs_2_ = f32[24,512]{1,0:T(8,128)S(1)} collective-permute-done((f32[24,512]{1,0:T(8,128)S(1)}, f32[24,512]{1,0:T(8,128)S(1)}, u32[]{:S(2)}, u32[]{:S(2)}) %collective-permute-start.4) | collective-permute-done | bytes 49184 | tf_op jit(solution)/shard_map/ppermute | solution.py:565
  31.7 1.2 %collective-permute-done.5.refs_3_ = f32[24,512]{1,0:T(8,128)S(1)} collective-permute-done((f32[24,512]{1,0:T(8,128)S(1)}, f32[24,512]{1,0:T(8,128)S(1)}, u32[]{:S(2)}, u32[]{:S(2)}) %collective-permute-start.5) | collective-permute-done | bytes 49184 | tf_op jit(solution)/shard_map/ppermute | solution.py:565
  32.9 1.8 %shard_map.88 = (f32[192,128]{1,0:T(8,128)S(1)}, f32[192,128]{1,0:T(8,128)S(1)}, f32[192,128]{1,0:T(8,128)S(1)}, f32[192,128]{1,0:T(8,128)S(1)}) custom-call(s32[2]{0:T(128)S(1)} %pad_add_fusion.where_ref, f32[24,512]{1,0:T(8,128)S(1)} %get-tuple-element.20.refs_0_, f32[24,512]{1,0:T(8,128)S(1)} %collective-permute-done.3.refs_1_, ...), custom_call_target="tpu_custom_call" | custom-call | tf_op jit(solution)/shard_map/pallas_call | solution.py:574
  34.7 1.6 %collective-permute-start.6 = (f32[192,128]{1,0:T(8,128)S(1)}, f32[192,128]{1,0:T(8,128)S(1)}, u32[]{:S(2)}, u32[]{:S(2)}) collective-permute-start(f32[192,128]{1,0:T(8,128)S(1)} %get-tuple-element.25), channel_id=1, source_target_pairs={{0,1},{1,0},{2,3},{3,2},{4,5},{5,4},{6,7},{7,6},{8,9},{9,8},{10,11... | collective-permute-start | bytes 294920 | tf_op jit(solution)/shard_map/ppermute | solution.py:565
  36.4 2.6 %collective-permute-start.7 = (f32[192,128]{1,0:T(8,128)S(1)}, f32[192,128]{1,0:T(8,128)S(1)}, u32[]{:S(2)}, u32[]{:S(2)}) collective-permute-start(f32[192,128]{1,0:T(8,128)S(1)} %get-tuple-element.26), channel_id=1, source_target_pairs={{0,2},{1,3},{2,0},{3,1},{4,6},{5,7},{6,4},{7,5},{8,10},{9,11},{10,... | collective-permute-start | bytes 294920 | tf_op jit(solution)/shard_map/ppermute | solution.py:565
  39.0 0.2 collective-permute-start.8
  39.2 1.0 %constant_dynamic-slice_fusion = f32[59,1024]{1,0:T(8,128)S(1)} fusion(f32[59,4096]{1,0:T(8,128)} %params_ref.1, s32[]{:T(128)S(6)} %select_n.107), kind=kLoop, calls=%fused_computation.58 | loop fusion | bytes 483332 | tf_op jit(solution)/shard_map/dynamic_slice | solution.py:677
  40.2 0.6 %copy.20 = f32[1,1,8,3,256]{4,2,3,1,0:T(8,128)} copy(f32[1,1,8,3,256]{4,3,2,1,0:T(4,128)S(1)} %bitcast.54) | data formatting | bytes 49152
  40.8 6.2 %collective-permute-done.7.refs_2_ = f32[192,128]{1,0:T(8,128)S(1)} collective-permute-done((f32[192,128]{1,0:T(8,128)S(1)}, f32[192,128]{1,0:T(8,128)S(1)}, u32[]{:S(2)}, u32[]{:S(2)}) %collective-permute-start.7) | collective-permute-done | bytes 98336 | tf_op jit(solution)/shard_map/ppermute | solution.py:565
  47.0 1.6 %shard_map.89 = f32[59,1024]{1,0:T(8,128)} custom-call(f32[192,128]{1,0:T(8,128)S(1)} %get-tuple-element.24.refs_0_, f32[192,128]{1,0:T(8,128)S(1)} %collective-permute-done.6.refs_1_, f32[192,128]{1,0:T(8,128)S(1)} %collective-permute-done.7.refs_2_, f32[192,128]{1,0:T(8,128)S(1)} %collective-permute-done.8.refs_3_, f32[472,128]{1,0:T(8,128)S(1)} %reshape.289.refs_4_), custom_call_target="tpu_custom_call" | custom-call | tf_op jit(solution)/shard_map/pallas_call | solution.py:574
  (25 shorter events, 0.2 us)
Async XLA Ops:
  0.6 0.7 %copy-start.1 = (f32[4,7]{1,0:T(4,128)S(1)}, f32[4,7]{1,0:T(4,128)}, u32[]{:S(2)}) copy-start(f32[4,7]{1,0:T(4,128)} %param.8) | copy-start | bytes 340
  1.5 0.7 %copy-start.4 = (s32[1,1,4,512]{3,2,1,0:T(4,128)S(1)}, s32[1,1,4,512]{3,2,1,0:T(4,128)}, u32[]{:S(2)}) copy-start(s32[1,1,4,512]{3,2,1,0:T(4,128)} %param.9) | copy-start | bytes 24580
  2.4 1.2 %copy-start = (f32[59,4096]{1,0:T(8,128)S(1)}, f32[59,4096]{1,0:T(8,128)}, u32[]{:S(2)}) copy-start(f32[59,4096]{1,0:T(8,128)} %params_ref.1) | copy-start | bytes 2899972
  6.2 6.7 %collective-permute-start = (f32[24,512]{1,0:T(8,128)S(1)}, f32[24,512]{1,0:T(8,128)S(1)}, u32[]{:S(2)}, u32[]{:S(2)}) collective-permute-start(f32[24,512]{1,0:T(8,128)S(1)} %get-tuple-element.16), channel_id=1, source_target_pairs={{0,4},{4,0},{8,12},{12,8},{1,5},{5,1},{9,13},{13,9},{2,6},{6,2},{1... | collective-permute-start | bytes 147464 | tf_op jit(solution)/shard_map/ppermute | solution.py:565
  6.7 6.2 %collective-permute-start.1 = (f32[24,512]{1,0:T(8,128)S(1)}, f32[24,512]{1,0:T(8,128)S(1)}, u32[]{:S(2)}, u32[]{:S(2)}) collective-permute-start(f32[24,512]{1,0:T(8,128)S(1)} %get-tuple-element.17), channel_id=1, source_target_pairs={{0,8},{4,12},{8,0},{12,4},{1,9},{5,13},{9,1},{13,5},{2,10},{6,14},... | collective-permute-start | bytes 147464 | tf_op jit(solution)/shard_map/ppermute | solution.py:565
  9.3 0.7 %copy-start.5 = (s32[1,1,8]{2,1,0:T(1,128)S(1)}, s32[1,1,8]{2,1,0:T(1,128)}, u32[]{:S(2)}) copy-start(s32[1,1,8]{2,1,0:T(1,128)} %param.10) | copy-start | bytes 100
  9.3 3.7 %collective-permute-start.2 = (f32[24,512]{1,0:T(8,128)S(1)}, f32[24,512]{1,0:T(8,128)S(1)}, u32[]{:S(2)}, u32[]{:S(2)}) collective-permute-start(f32[24,512]{1,0:T(8,128)S(1)} %get-tuple-element.18), channel_id=1, source_target_pairs={{0,12},{4,8},{8,4},{12,0},{1,13},{5,9},{9,5},{13,1},{2,14},{6,10},... | collective-permute-start | bytes 147464 | tf_op jit(solution)/shard_map/ppermute | solution.py:565
  10.1 0.7 %copy-start.6 = (s32[1,1,8]{2,1,0:T(1,128)S(1)}, s32[1,1,8]{2,1,0:T(1,128)}, u32[]{:S(2)}) copy-start(s32[1,1,8]{2,1,0:T(1,128)} %param.11) | copy-start | bytes 100
  11.3 0.7 %copy-start.2 = (f32[1,1,8,3,256]{4,2,3,1,0:T(8,128)S(1)}, f32[1,1,8,3,256]{4,2,3,1,0:T(8,128)}, u32[]{:S(2)}) copy-start(f32[1,1,8,3,256]{4,2,3,1,0:T(8,128)} %param.13) | copy-start | bytes 73732
  12.0 0.7 %copy-start.3 = (s32[1,1,8,512]{3,2,1,0:T(8,128)S(1)}, s32[1,1,8,512]{3,2,1,0:T(8,128)}, u32[]{:S(2)}) copy-start(s32[1,1,8,512]{3,2,1,0:T(8,128)} %param.12) | copy-start | bytes 49156
  27.4 2.1 %collective-permute-start.3 = (f32[24,512]{1,0:T(8,128)S(1)}, f32[24,512]{1,0:T(8,128)S(1)}, u32[]{:S(2)}, u32[]{:S(2)}) collective-permute-start(f32[24,512]{1,0:T(8,128)S(1)} %get-tuple-element.21), channel_id=1, source_target_pairs={{0,4},{4,0},{8,12},{12,8},{1,5},{5,1},{9,13},{13,9},{2,6},{6,2},{1... | collective-permute-start | bytes 147464 | tf_op jit(solution)/shard_map/ppermute | solution.py:565
  27.6 4.1 %collective-permute-start.4 = (f32[24,512]{1,0:T(8,128)S(1)}, f32[24,512]{1,0:T(8,128)S(1)}, u32[]{:S(2)}, u32[]{:S(2)}) collective-permute-start(f32[24,512]{1,0:T(8,128)S(1)} %get-tuple-element.22), channel_id=1, source_target_pairs={{0,8},{4,12},{8,0},{12,4},{1,9},{5,13},{9,1},{13,5},{2,10},{6,14},... | collective-permute-start | bytes 147464 | tf_op jit(solution)/shard_map/ppermute | solution.py:565
  28.9 4.0 %collective-permute-start.5 = (f32[24,512]{1,0:T(8,128)S(1)}, f32[24,512]{1,0:T(8,128)S(1)}, u32[]{:S(2)}, u32[]{:S(2)}) collective-permute-start(f32[24,512]{1,0:T(8,128)S(1)} %get-tuple-element.23), channel_id=1, source_target_pairs={{0,12},{4,8},{8,4},{12,0},{1,13},{5,9},{9,5},{13,1},{2,14},{6,10},... | collective-permute-start | bytes 147464 | tf_op jit(solution)/shard_map/ppermute | solution.py:565
  34.7 6.1 %collective-permute-start.6 = (f32[192,128]{1,0:T(8,128)S(1)}, f32[192,128]{1,0:T(8,128)S(1)}, u32[]{:S(2)}, u32[]{:S(2)}) collective-permute-start(f32[192,128]{1,0:T(8,128)S(1)} %get-tuple-element.25), channel_id=1, source_target_pairs={{0,1},{1,0},{2,3},{3,2},{4,5},{5,4},{6,7},{7,6},{8,9},{9,8},{10,11... | collective-permute-start | bytes 294920 | tf_op jit(solution)/shard_map/ppermute | solution.py:565
  36.4 10.7 %collective-permute-start.7 = (f32[192,128]{1,0:T(8,128)S(1)}, f32[192,128]{1,0:T(8,128)S(1)}, u32[]{:S(2)}, u32[]{:S(2)}) collective-permute-start(f32[192,128]{1,0:T(8,128)S(1)} %get-tuple-element.26), channel_id=1, source_target_pairs={{0,2},{1,3},{2,0},{3,1},{4,6},{5,7},{6,4},{7,5},{8,10},{9,11},{10,... | collective-permute-start | bytes 294920 | tf_op jit(solution)/shard_map/ppermute | solution.py:565
  39.0 8.1 %collective-permute-start.8 = (f32[192,128]{1,0:T(8,128)S(1)}, f32[192,128]{1,0:T(8,128)S(1)}, u32[]{:S(2)}, u32[]{:S(2)}) collective-permute-start(f32[192,128]{1,0:T(8,128)S(1)} %get-tuple-element.27), channel_id=1, source_target_pairs={{0,3},{1,2},{2,1},{3,0},{4,7},{5,6},{6,5},{7,4},{8,11},{9,10},{10,... | collective-permute-start | bytes 294920 | tf_op jit(solution)/shard_map/ppermute | solution.py:565

commit v3 on v2

--- a/solution.py
+++ b/solution.py
@@ -13,6 +13,7 @@
 COLOUR_ROW = 12
 SPAN = 256
 CHUNK = 2048
+STRIP = 128
 LOG2_E = 1.4426950408889634
 DEAD = -1e30
 
@@ -78,36 +79,72 @@
     return lax.dot_general(left, right, (((1,), (1,)), ((), ())), preferred_element_type=F32)
 
 
-def camera_table(cameras):
-    cosine, sine = jnp.cos(cameras[:, :3]), jnp.sin(cameras[:, :3])
-    c0, c1, c2 = cosine[:, 0], cosine[:, 1], cosine[:, 2]
-    s0, s1, s2 = sine[:, 0], sine[:, 1], sine[:, 2]
+def camera_columns(cameras):
+    cosine, sine = jnp.cos(cameras), jnp.sin(cameras)
+    c0, c1, c2 = [cosine[:, a : a + 1] for a in range(3)]
+    s0, s1, s2 = [sine[:, a : a + 1] for a in range(3)]
     rotation = [
         [c1 * c2, s0 * s1 * c2 - c0 * s2, c0 * s1 * c2 + s0 * s2],
         [c1 * s2, s0 * s1 * s2 + c0 * c2, c0 * s1 * s2 - s0 * c2],
         [-s1, s0 * c1, c0 * c1],
     ]
-    shift = [cameras[:, 3], cameras[:, 4], cameras[:, 5]]
+    shift = [cameras[:, a : a + 1] for a in (3, 4, 5)]
     origin = [sum(rotation[m][a] * shift[m] for m in range(3)) for a in range(3)]
-    return jnp.stack([e for row in rotation for e in row] + shift + [cameras[:, 6]] + origin, 1)
+    return [e for row in rotation for e in row] + shift + [cameras[:, 6:7]] + origin
+
+
+def camera_table(cameras):
+    return jnp.concatenate(camera_columns(cameras), axis=1)
 
 
 def lane_pick(source, lanes):
     return jnp.take_along_axis(source, lanes, axis=1, mode="promise_in_bounds")
 
 
-def slab_kernel(n_render, views, params_ref, table_ref, index_ref, *rest):
-    outs, dense_ref = rest[:n_render], rest[n_render]
+def partner_rows(index_ref, n_render):
+    me = lax.axis_index("render")
+    rows = [index_ref[o : o + 1, :] for o in range(n_render)]
+    return [
+        sum(jnp.where((me ^ turn) == o, rows[o], 0) for o in range(n_render)) for turn in range(n_render)
+    ]
+
+
+def slab_kernel(n_render, views, params_hbm, cameras_hbm, index_hbm, *rest):
+    outs, refs = rest[:n_render], rest[n_render:]
+    params_ref, cameras_ref, index_ref, order_ref, dense_ref, arrival = refs
     rows, gaussians = outs[0].shape[0], params_ref.shape[1]
     cap = index_ref.shape[1]
     width = 512
+    shades = gaussians // width
+    count = params_ref.shape[0]
+    copies = [
+        pltpu.make_async_copy(cameras_hbm, cameras_ref, arrival.at[0]),
+        pltpu.make_async_copy(index_hbm, index_ref, arrival.at[1]),
+        pltpu.make_async_copy(params_hbm.at[0:8, :], params_ref.at[0:8, :], arrival.at[2]),
+    ]
+    for step in range(shades):
+        lanes = pl.ds(step * width, width)
+        copies.append(
+            pltpu.make_async_copy(
+                params_hbm.at[8:count, lanes], params_ref.at[8:count, lanes], arrival.at[3 + step]
+            )
+        )
+    for copy in copies:
+        copy.start()
+    copies[0].wait()
+    origin = camera_columns(cameras_ref[...])[13:16]
+    copies[1].wait()
+    for turn, row in enumerate(partner_rows(index_ref, n_render)):
+        order_ref[turn : turn + 1, :] = row
+    copies[2].wait()
+
     picks = [(turn, step) for turn in range(n_render) for step in range(cap // 128)]
-    shades = gaussians // width
 
     def shade(step):
         lanes = slice(step * width, step * width + width)
+        copies[3 + step].wait()
         dense_ref[0:8, lanes] = params_ref[8:16, lanes]
-        away = [params_ref[a : a + 1, lanes] + table_ref[:, 13 + a : 14 + a] for a in range(3)]
+        away = [params_ref[a : a + 1, lanes] + origin[a] for a in range(3)]
         inverse = lax.rsqrt(away[0] * away[0] + away[1] * away[1] + away[2] * away[2])
         basis = harmonic_basis(*[part * inverse for part in away])
         for channel in range(3):
@@ -120,7 +157,7 @@
 
     def pick(source, groups, skip, turn, step):
         lanes = slice(128 * step, 128 * step + 128)
-        index = jnp.broadcast_to(index_ref[turn : turn + 1, lanes], (8, 128))
+        index = jnp.broadcast_to(order_ref[turn : turn + 1, lanes], (8, 128))
         lane, block = index & 127, index >> 7
         found = [jnp.zeros((8, 128), F32) for _ in range(groups)]
         for b in range(gaussians // 128):
@@ -192,18 +229,18 @@
     return value, number
 
 
-def render_kernel(n_render, views, where_ref, *refs):
+def render_kernel(n_render, views, *refs):
     blocks, refs = refs[:n_render], refs[n_render:]
     slot_ref, cam_ref, target_ref, refs = refs[0], refs[1], refs[2], refs[3:]
     image_ref, outs, refs = refs[0], refs[1 : 1 + n_render], refs[1 + n_render :]
-    raw_ref, stack_ref, wide_ref, alpha_ref, weight_ref, shade_ref, high_ref, low_ref, pass_ref, enter_ref, behind_ref, lhs_ref, hot_ref, acc_ref = refs
+    raw_ref, stack_ref, wide_ref, alpha_ref, weight_ref, shown_ref, pass_ref, enter_ref, behind_ref, right_ref, sums_ref, lhs_ref, hot_ref, acc_ref = refs
     tiles = target_ref.shape[0]
     entry_rows = slot_ref.shape[0]
     entries = entry_rows * 128
     cap = blocks[0].shape[1]
     rows = blocks[0].shape[0]
     per_block = cap // 128
-    me = where_ref[0]
+    me = lax.axis_index("render")
     groups = entry_rows // 8
 
     def fetch(group, _):
@@ -258,13 +295,13 @@
 
     lax.fori_loop(0, groups, forward_entries, 0)
 
-    wide_ref[...] = jnp.zeros_like(wide_ref)
+    chunks = entries // CHUNK
+
+    def chunk_of(chunk):
+        return pl.ds(pl.multiple_of(chunk * CHUNK, CHUNK), CHUNK)
+
     lane = lax.broadcasted_iota(jnp.int32, (8, 128), 1)
     own_tile = (lane & (tiles - 1)) == lax.broadcasted_iota(jnp.int32, (8, 128), 0)
-    chunks = entries // CHUNK
-
-    def chunk_of(chunk):
-        return pl.ds(pl.multiple_of(chunk * CHUNK, CHUNK), CHUNK)
 
     def widen(row, _):
         value = stack_ref[pl.ds(row, 16, stride=entry_rows), :]
@@ -288,77 +325,78 @@
 
     value, number = monomials((PIXELS, 32), 1)
     left = jnp.where(number < 24, value, 0.0).astype(BF16)
-    value, number = monomials((16, PIXELS), 0)
-    moment_rows = jnp.where(number < 8, value, 0.0).astype(BF16)
     segment = lax.broadcasted_iota(jnp.int32, (PIXELS, 128), 1) // tiles
     last = 128 // tiles - 1
 
-    def attenuate(chunk, _):
-        alpha = jnp.exp2(dot_plain(left, wide_ref[0:32, chunk_of(chunk)]))
-        alpha_ref[:, chunk_of(chunk)] = alpha
-        passing = pass_ref[...]
-        weights = []
-        for k in range(CHUNK // 128):
-            weight = passing * alpha[:, 128 * k : 128 * k + 128]
-            passing = passing - weight
-            weights.append(weight)
-        weight_ref[:, chunk_of(chunk)] = jnp.concatenate(weights, axis=1)
-        pass_ref[...] = passing
-        return 0
-
-    pass_ref[...] = jnp.ones_like(pass_ref)
-    lax.fori_loop(0, chunks, attenuate, 0)
+    def expose(chunk, _):
+        alpha_ref[:, chunk_of(chunk)] = jnp.exp2(dot_plain(left, wide_ref[0:32, chunk_of(chunk)]))
+        return 0
+
+    lax.fori_loop(0, chunks, expose, 0)
+
+    def colour_rows(row):
+        return [
+            jnp.broadcast_to(stack_ref[(8 + ch) * entry_rows + row : (8 + ch) * entry_rows + row + 1, :], (8, 128))
+            for ch in range(3)
+        ]
+
+    def strip_of(strip, part):
+        return pl.ds(pl.multiple_of(strip * STRIP + 8 * part, 8), 8)
+
+    parts = STRIP // 8
+
+    def attenuate(strip, _):
+        passing = [jnp.ones((8, 128), F32) for _ in range(parts)]
+        shown = [[None] * parts for _ in range(3)]
+        for row in range(entry_rows):
+            cut = slice(128 * row, 128 * row + 128)
+            colours = colour_rows(row)
+            for part in range(parts):
+                weight = passing[part] * alpha_ref[strip_of(strip, part), cut]
+                passing[part] = passing[part] - weight
+                weight_ref[strip_of(strip, part), cut] = weight
+                for ch in range(3):
+                    term = weight * colours[ch]
+                    shown[ch][part] = term if row == 0 else shown[ch][part] + term
+        for part in range(parts):
+            pass_ref[strip_of(strip, part), :] = passing[part]
+            for ch in range(3):
+                shown_ref[ch, strip_of(strip, part), :] = shown[ch][part]
+        return 0
+
+    lax.fori_loop(0, PIXELS // STRIP, attenuate, 0)
 
     through = pass_ref[...]
     hop = 1
     while hop <= last:
         through = through * jnp.where(segment >= hop, pltpu.roll(through, tiles * hop, 1), 1.0)
         hop *= 2
-    enter_ref[...] = jnp.where(segment >= 1, pltpu.roll(through, tiles, 1), 1.0)
-    remain = through.T[tiles * last : tiles * last + tiles, :]
-
-    def paint(chunk, image):
-        weight = weight_ref[:, chunk_of(chunk)] * jnp.concatenate([enter_ref[...]] * (CHUNK // 128), axis=1)
-        weight_ref[:, chunk_of(chunk)] = weight
-        high = weight.astype(BF16)
-        low = (weight - high.astype(F32)).astype(BF16)
-        high_ref[:, chunk_of(chunk)] = high
-        low_ref[:, chunk_of(chunk)] = low
-        colours = wide_ref[32:80, chunk_of(chunk)]
-        return image + (dot_lanes(colours, high) + dot_lanes(colours, low))
-
-    image = lax.fori_loop(0, chunks, paint, jnp.zeros((48, PIXELS), F32))
-    image = image[0:24] + image[24:48]
-    residual = []
+    enter = jnp.where(segment >= 1, pltpu.roll(through, tiles, 1), 1.0)
+    enter_ref[...] = enter
+    remain = jnp.where(segment == last, backdrop * through, 0.0)
+    open_end = jnp.zeros((PIXELS, 128), F32)
+    add = jnp.zeros((PIXELS, 128), F32)
+    right = jnp.zeros((PIXELS, 128), F32)
     for channel in range(3):
-        shown = image[8 * channel : 8 * channel + 8] + backdrop * remain
-        image_ref[:, channel, :] = shown
-        residual.append(shown - target_ref[:, channel, :])
-    high, low = high_low(jnp.concatenate(residual, axis=0))
-    both = jnp.concatenate([high, low], axis=0).astype(BF16)
-    right = jnp.concatenate([high, high, low, jnp.zeros((56, PIXELS), F32)], axis=0).T.astype(BF16)
-    right = right[:, 0:80]
-    number = lax.broadcasted_iota(jnp.int32, (80, 128), 0)
-    unit = (number & (tiles - 1)) == (lax.broadcasted_iota(jnp.int32, (80, 128), 1) & (tiles - 1))
-    unit = jnp.where(unit & ((number < 24) | ((number >= 48) & (number < 72))), backdrop, 0.0)
-    open_end = dot_plain(right, unit.astype(BF16))
-
-    def shade(step, _):
-        chunk = chunks - 1 - step
-        colour = dot_plain(right, wide_ref[32:112, chunk_of(chunk)])
-        shade_ref[:, chunk_of(chunk)] = colour
-        alpha = alpha_ref[:, chunk_of(chunk)]
-        behind = behind_ref[...]
-        for k in reversed(range(CHUNK // 128)):
-            cut = slice(128 * k, 128 * k + 128)
-            behind = behind + alpha[:, cut] * (colour[:, cut] - behind)
-        behind_ref[...] = behind
-        return 0
-
-    behind_ref[...] = jnp.zeros_like(behind_ref)
-    lax.fori_loop(0, chunks, shade, 0)
-
-    keep, add = pass_ref[...], behind_ref[...]
+        alone = shown_ref[channel]
+        total = alone * enter + remain
+        hop = 1
+        while hop <= last:
+            total = total + pltpu.roll(total, tiles * hop, 1)
+            hop *= 2
+        image_ref[:, channel, :] = total.T[0:tiles, :]
+        wanted = jnp.concatenate([target_ref[:, channel, :]] * (last + 1), axis=0).T
+        residual = total - wanted
+        high, low = high_low(residual)
+        right = jnp.where((segment == channel) | (segment == 3 + channel), high, right)
+        right = jnp.where(segment == 6 + channel, low, right)
+        shown_ref[channel] = residual
+        open_end = open_end + backdrop * residual
+        add = add + residual * alone
+
+    right_ref[...] = right.astype(BF16)
+
+    keep = pass_ref[...]
     hop = 1
     while hop <= last:
         inside = segment + hop <= last
@@ -369,34 +407,74 @@
         segment < last, pltpu.roll(add + keep * open_end, 128 - tiles, 1), open_end
     )
 
-    def descend(step, _):
-        chunk = chunks - 1 - step
-        behind = behind_ref[...]
-        slopes = [None] * (CHUNK // 128)
-        for k in reversed(range(CHUNK // 128)):
-            cut = pl.ds(pl.multiple_of(chunk * CHUNK + 128 * k, 128), 128)
-            gap = shade_ref[:, cut] - behind
-            behind = behind + alpha_ref[:, cut] * gap
-            slopes[k] = weight_ref[:, cut] * gap
-        behind_ref[...] = behind
-        slope = jnp.concatenate(slopes, axis=1)
-        high = slope.astype(BF16)
-        low = (slope - high.astype(F32)).astype(BF16)
-        moments = dot_plain(moment_rows, high) + dot_plain(moment_rows, low)
-        tint = dot_plain(both, high_ref[:, chunk_of(chunk)]) + dot_plain(both, low_ref[:, chunk_of(chunk)])
-        tint = tint[0:24] + tint[24:48]
-        for k in range(CHUNK // 128):
-            row = chunk * (CHUNK // 128) + k
-            cut = slice(128 * k, 128 * k + 128)
-            stack_ref[pl.ds(row, 8, stride=entry_rows), :] = moments[0:8, cut]
-            for channel in range(3):
-                part = jnp.where(own_tile, tint[8 * channel : 8 * channel + 8, cut], 0.0)
-                stack_ref[pl.ds((8 + channel) * entry_rows + row, 1), :] = jnp.sum(
-                    part, axis=0, keepdims=True
-                )
-        return 0
-
-    lax.fori_loop(0, chunks, descend, 0)
+    def sums_at(strip, number, row):
+        return pl.ds(pl.multiple_of(((strip * 9 + number) * entry_rows + row) * 8, 8), 8)
+
+    def descend(strip, _):
+        behind = [behind_ref[strip_of(strip, part), :] for part in range(parts)]
+        enter = [enter_ref[strip_of(strip, part), :] for part in range(parts)]
+        residual = [[shown_ref[ch, strip_of(strip, part), :] for part in range(parts)] for ch in range(3)]
+        facing = right_ref[pl.ds(pl.multiple_of(strip * STRIP, STRIP), STRIP), 0:80]
+        for row in reversed(range(entry_rows)):
+            cut = slice(128 * row, 128 * row + 128)
+            if row % 2:
+                shade = dot_plain(facing, wide_ref[32:112, 128 * row - 128 : 128 * row + 128])
+            side = slice(128 * (row % 2), 128 * (row % 2) + 128)
+            tint = [None] * 3
+            tall = [[None] * 3, [None] * 3]
+            for part in range(parts):
+                here = [residual[ch][part] for ch in range(3)]
+                gap = shade[8 * part : 8 * part + 8, side] - behind[part]
+                behind[part] = behind[part] + alpha_ref[strip_of(strip, part), cut] * gap
+                weight = weight_ref[strip_of(strip, part), cut] * enter[part]
+                slope = weight * gap
+                for ch in range(3):
+                    term = weight * here[ch]
+                    tint[ch] = term if part == 0 else tint[ch] + term
+                half, up = part % 2, float(part // 2)
+                terms = [slope, slope * up, slope * (up * up)] if up else [slope, None, None]
+                for power in range(3):
+                    if terms[power] is None:
+                        continue
+                    known = tall[half][power]
+                    tall[half][power] = terms[power] if known is None else known + terms[power]
+            base = (strip * (STRIP // 16)).astype(F32) - 7.5
+            for half in range(2):
+                level, rise, bend = tall[half]
+                bend = bend + (2.0 * base) * rise + (base * base) * level
+                rise = rise + base * level
+                for power, value in ((0, level), (1, rise), (2, bend)):
+                    at = 3 * half + power
+                    sums_ref[sums_at(strip, at, row), :] = value
+            for ch in range(3):
+                sums_ref[sums_at(strip, 6 + ch, row), :] = tint[ch]
+        return 0
+
+    lax.fori_loop(0, PIXELS // STRIP, descend, 0)
+
+    def gather_sums(group, _):
+        def summed(number, sub):
+            return sum(
+                sums_ref[pl.ds((strip * 9 + number) * 8 * entry_rows + group * 64 + sub, 8, stride=8), :]
+                for strip in range(PIXELS // STRIP)
+            )
+
+        values = [0.0] * 9
+        for sub in range(8):
+            for half in range(2):
+                x = 8.0 * half + sub - 7.5
+                level, rise, bend = [summed(3 * half + power, sub) for power in range(3)]
+                terms = [(x * x) * level, x * rise, bend, x * level, rise, level]
+                for c in range(6):
+                    values[c] = values[c] + terms[c]
+            for ch in range(3):
+                values[6 + ch] = values[6 + ch] + summed(6 + ch, sub)
+        for c, value in enumerate(values):
+            line = c * entry_rows if c < 6 else (c + 2) * entry_rows
+            stack_ref[pl.ds(pl.multiple_of(line + group * 8, 8), 8), :] = value
+        return 0
+
+    lax.fori_loop(0, groups, gather_sums, 0)
 
     def backward_entries(group, _):
         here = pl.ds(pl.multiple_of(group * 8, 8), 8)
@@ -476,7 +554,7 @@
                 outs[turn][:, first : first + 128] = total
 
 
-def collect_kernel(n_render, n_view, where_ref, *refs):
+def collect_kernel(n_render, n_view, *refs):
     blocks, refs = refs[:n_render], refs[n_render:]
     index_ref, origin_ref, refs = refs[0], refs[1], refs[2:]
     outs, (lhs_ref, hot_ref, acc_ref) = refs[:n_view], refs[n_view:]
@@ -484,10 +562,9 @@
     own = outs[0].shape[0] // rows * 128
     gaussians = own * n_view
     spans = gaussians // SPAN
-    column = where_ref[1]
-    for turn in range(n_render):
+    column = lax.axis_index("view")
+    for turn, index in enumerate(partner_rows(index_ref, n_render)):
         lanes = slice(turn * cap, (turn + 1) * cap)
-        index = index_ref[turn : turn + 1, :]
         span, lane = index // SPAN, index & (SPAN - 1)
         hot = lax.broadcasted_iota(jnp.int32, (SPAN, cap), 0) == jnp.broadcast_to(lane, (SPAN, cap))
         hot_ref[:, lanes] = jnp.where(hot, 1.0, 0.0).astype(BF16)
@@ -566,22 +643,18 @@
     ]
 
 
-def call(kernel, out_shape, scratch, in_smem, *args):
-    specs = [
-        pl.BlockSpec(memory_space=pltpu.SMEM) if i < in_smem else pl.BlockSpec(memory_space=pltpu.VMEM)
-        for i in range(len(args))
-    ]
+def call(kernel, out_shape, scratch, space, *args):
     return pl.pallas_call(
         kernel,
         out_shape=out_shape,
-        in_specs=specs,
+        in_specs=[pl.BlockSpec(memory_space=space)] * len(args),
         out_specs=[pl.BlockSpec(memory_space=pltpu.VMEM)] * len(out_shape),
         scratch_shapes=scratch,
-        compiler_params=pltpu.CompilerParams(vmem_limit_bytes=48 * 1024 * 1024),
+        compiler_params=pltpu.CompilerParams(vmem_limit_bytes=(64 if space == pl.ANY else 48) * 1024 * 1024),
     )(*args)
 
 
-def render(n_render, views, where, arrived, table, code, live, slot, wanted):
+def render(n_render, views, arrived, table, code, live, slot, wanted):
     tiles, length = slot.shape
     rows, cap = arrived[0].shape
     view = code // (CROP * CROP)
@@ -614,18 +687,17 @@
             pltpu.VMEM((112, entries), BF16),
             pltpu.VMEM((PIXELS, entries), F32),
             pltpu.VMEM((PIXELS, entries), F32),
-            pltpu.VMEM((PIXELS, entries), F32),
-            pltpu.VMEM((PIXELS, entries), BF16),
-            pltpu.VMEM((PIXELS, entries), BF16),
+            pltpu.VMEM((3, PIXELS, 128), F32),
             pltpu.VMEM((PIXELS, 128), F32),
             pltpu.VMEM((PIXELS, 128), F32),
             pltpu.VMEM((PIXELS, 128), F32),
+            pltpu.VMEM((PIXELS, 128), BF16),
+            pltpu.VMEM((9 * PIXELS // STRIP * 8 * entry_rows, 128), F32),
             pltpu.VMEM((2 * rows * spans, entries), BF16),
             pltpu.VMEM((SPAN, entries), BF16),
             pltpu.VMEM((4 * rows * spans, 128), F32),
         ],
-        1,
-        where,
+        pltpu.VMEM,
         *arrived,
         slot_lanes,
         lane_table,
@@ -633,20 +705,28 @@
     )
 
 
-def slab(n_render, views, params, table, index):
+def slab(n_render, params, cameras, index):
+    views, (count, gaussians), cap = cameras.shape[0], params.shape, index.shape[1]
     rows = -(-(COLOUR_ROW + 3 * views) // 8) * 8
     return call(
         partial(slab_kernel, n_render, views),
-        [jax.ShapeDtypeStruct((rows, index.shape[1]), F32)] * n_render,
-        [pltpu.VMEM((rows - 8, params.shape[1]), F32)],
-        0,
+        [jax.ShapeDtypeStruct((rows, cap), F32)] * n_render,
+        [
+            pltpu.VMEM((count, gaussians), F32),
+            pltpu.VMEM(cameras.shape, F32),
+            pltpu.VMEM((n_render, cap), jnp.int32),
+            pltpu.VMEM((n_render, cap), jnp.int32),
+            pltpu.VMEM((rows - 8, gaussians), F32),
+            pltpu.SemaphoreType.DMA((3 + gaussians // 512,)),
+        ],
+        pl.ANY,
         params,
-        table,
+        cameras,
         index,
     )
 
 
-def collect(n_render, n_view, where, homed, index, origin, own):
+def collect(n_render, n_view, homed, index, origin, own):
     rows, cap = homed[0].shape
     spans = n_view * own // SPAN
     return call(
@@ -657,8 +737,7 @@
             pltpu.VMEM((SPAN, n_render * cap), BF16),
             pltpu.VMEM((4 * rows * spans, 128), F32),
         ],
-        1,
-        where,
+        pltpu.VMEM,
         *homed,
         index,
         origin,
@@ -669,18 +748,14 @@
     index = send_index[0, 0]
     views = cameras.shape[0]
     own = params.shape[1] // n_view
-    order = lax.axis_index("render") ^ jnp.arange(n_render, dtype=jnp.int32)
-    index = sum(jnp.where((order == o)[:, None], index[o][None], 0) for o in range(n_render))
-    where = jnp.stack([lax.axis_index("render"), lax.axis_index("view")]).astype(jnp.int32)
     table = camera_table(cameras)
     origin = jnp.pad(table[:, 13:16].reshape(1, 3 * views), ((0, 0), (0, 128 - 3 * views)))
     mine = lax.dynamic_slice_in_dim(params, lax.axis_index("view") * own, own, 1).reshape(-1, 128)
 
-    arrived = swap(list(slab(n_render, views, params, table, index)), "render")
+    arrived = swap(list(slab(n_render, params, cameras, index)), "render")
     image, *returned = render(
         n_render,
         views,
-        where,
         arrived,
         table,
         tile_id[0, 0],
@@ -689,12 +764,12 @@
         targets[0, 0],
     )
     homed = swap(returned, "render")
-    owned = swap(list(collect(n_render, n_view, where, homed, index, origin, own)), "view")
+    owned = swap(list(collect(n_render, n_view, homed, index, origin, own)), "view")
     (gradients,) = call(
         partial(owner_kernel, n_view, views),
         [jax.ShapeDtypeStruct((params.shape[0], own), F32)],
         [pltpu.VMEM((params.shape[0] * own // 128, 128), F32)],
-        0,
+        pltpu.VMEM,
         *owned,
         mine,
     )

time: 49 us -> 46.7 us (0.953)
  local copies, waits for them, and re-layouts: 7.73 us -> 5.8 us
    unnamed x16, local copies, waits for them, and re-layouts: 5.69 us -> 3.86 us
  transfers between devices with their start and end apart: 9 -> 9, of which waited for: 3 -> 4; matrix products, arithmetic and copies ran while one was open for 6% -> 6% of each run, Pallas kernels for 0% -> 0%
where the time goes in v3:
time: 46.7 us; the launch traced here: 46.4 us
  Pallas kernels  20.1 us (43%)
  waiting for transfers between devices  9.76 us (21%)
  starting transfers between devices  9.56 us (20%)
  local copies, waits for them, and re-layouts  5.8 us (12%)
  between operations  0.74 us (2%)
    pallas_call x4, Pallas kernels, call(): pl.pallas_call(kernel, out_shape=out_shape, in_specs=[pl.BlockSpec(memory...  20.1 us
    ppermute x9, waiting for transfers between devices, swap(): lax.ppermute(blocks[turn], axis, [(i, i ^ turn) for i in range(n)])  9.76 us
    ppermute x9, starting transfers between devices, swap(): lax.ppermute(blocks[turn], axis, [(i, i ^ turn) for i in range(n)])  9.56 us
    unnamed x16, local copies, waits for them, and re-layouts  3.86 us
    dynamic_slice x1, local copies, waits for them, and re-layouts, body(): lax.dynamic_slice_in_dim(params, lax.axis_index('view') * own, own, 1)  0.97 us
  transfers between devices with their start and end apart: 9, of which 4 were waited for; matrix products, arithmetic and copies ran while one was open for 6% of the time, Pallas kernels for 0%

profile of v3, /device:TPU:0, one launch (start us, length us, event | category | flops | bytes accessed | tf_op | source)
XLA Modules:
  0.0 46.4 jit_solution(4583435568235186661)
XLA Ops:
  0.6 4.6 %shard_map.86 = (f32[24,512]{1,0:T(8,128)}, f32[24,512]{1,0:T(8,128)}, f32[24,512]{1,0:T(8,128)}, f32[24,512]{1,0:T(8,128)}) custom-call(f32[59,4096]{1,0:T(8,128)} %params_hbm.1, f32[4,7]{1,0:T(4,128)} %cameras_hbm.1, s32[4,512]{1,0:T(4,128)} %bitcast.49), custom_call_target="tpu_custom_call" | custom-call | tf_op jit(solution)/shard_map/pallas_call | solution.py:647
  5.3 0.5 %collective-permute-start = (f32[24,512]{1,0:T(8,128)}, f32[24,512]{1,0:T(8,128)S(1)}, u32[]{:S(2)}, u32[]{:S(2)}) collective-permute-start(f32[24,512]{1,0:T(8,128)} %get-tuple-element.16), channel_id=1, source_target_pairs={{0,4},{4,0},{8,12},{12,8},{1,5},{5,1},{9,13},{13,9},{2,6},{6,2},{1... | collective-permute-start | bytes 147464 | tf_op jit(solution)/shard_map/ppermute | solution.py:642
  5.8 2.6 %collective-permute-start.1 = (f32[24,512]{1,0:T(8,128)}, f32[24,512]{1,0:T(8,128)S(1)}, u32[]{:S(2)}, u32[]{:S(2)}) collective-permute-start(f32[24,512]{1,0:T(8,128)} %get-tuple-element.17), channel_id=1, source_target_pairs={{0,8},{4,12},{8,0},{12,4},{1,9},{5,13},{9,1},{13,5},{2,10},{6,14},... | collective-permute-start | bytes 147464 | tf_op jit(solution)/shard_map/ppermute | solution.py:642
  8.4 0.1 collective-permute-start.2
  8.4 0.0 copy-done.5
  8.5 0.6 %copy-done.2 = f32[4,7]{1,0:T(4,128)S(1)} copy-done((f32[4,7]{1,0:T(4,128)S(1)}, f32[4,7]{1,0:T(4,128)}, u32[]{:S(2)}) %copy-start.2) | copy-done | bytes 136
  9.1 0.1 slice.55
  9.2 0.1 multiply_add_fusion.1
  9.3 0.1 multiply_add_fusion
  9.3 0.6 %copy-done.6 = s32[1,1,8]{2,1,0:T(1,128)S(1)} copy-done((s32[1,1,8]{2,1,0:T(1,128)S(1)}, s32[1,1,8]{2,1,0:T(1,128)}, u32[]{:S(2)}) %copy-start.6) | copy-done | bytes 56
  10.0 0.1 copy.13
  10.0 0.1 copy.14
  10.1 0.1 copy.15
  10.2 0.1 copy.16
  10.3 0.1 concatenate.14
  10.4 0.1 select_add_fusion
  10.5 0.1 concatenate.15
  10.6 0.7 %copy-done.3 = f32[1,1,8,3,256]{4,2,3,1,0:T(8,128)S(1)} copy-done((f32[1,1,8,3,256]{4,2,3,1,0:T(8,128)S(1)}, f32[1,1,8,3,256]{4,2,3,1,0:T(8,128)}, u32[]{:S(2)}) %copy-start.3) | copy-done | bytes 24600
  11.3 0.0 copy-start.4
  11.3 0.1 copy.19.refs_5_
  11.4 0.7 %copy-done.4 = s32[1,1,8,512]{3,2,1,0:T(8,128)S(1)} copy-done((s32[1,1,8,512]{3,2,1,0:T(8,128)S(1)}, s32[1,1,8,512]{3,2,1,0:T(8,128)}, u32[]{:S(2)}) %copy-start.4) | copy-done | bytes 16408
  12.0 0.1 reshape_squeeze.3
  12.1 0.0 copy-start
  12.2 0.1 copy.18.refs_4_
  12.2 0.0 collective-permute-done.refs_1_
  12.2 0.0 collective-permute-done.1.refs_2_
  12.2 0.1 collective-permute-done.2.refs_3_
  12.3 0.7 %copy-done = f32[24,512]{1,0:T(8,128)S(1)} copy-done((f32[24,512]{1,0:T(8,128)S(1)}, f32[24,512]{1,0:T(8,128)}, u32[]{:S(2)}) %copy-start) | copy-done | bytes 49176
  12.9 12.6 %shard_map.87 = (f32[8,3,256]{2,1,0:T(4,128)S(1)}, f32[24,512]{1,0:T(8,128)S(1)}, f32[24,512]{1,0:T(8,128)S(1)}, f32[24,512]{1,0:T(8,128)S(1)}, f32[24,512]{1,0:T(8,128)S(1)}) custom-call(f32[24,512]{1,0:T(8,128)S(1)} %copy-done, f32[24,512]{1,0:T(8,128)S(1)} %collective-permute-done.refs_1_, f32[24,512]{1,0:T(8,128)S(1)} %collective-permute-done.1.refs_2_, ...), custom_call_target="tpu_custom_call" | custom-call | tf_op jit(solution)/shard_map/pallas_call | solution.py:647
  25.6 0.2 collective-permute-start.3
  25.8 1.3 %collective-permute-start.4 = (f32[24,512]{1,0:T(8,128)S(1)}, f32[24,512]{1,0:T(8,128)S(1)}, u32[]{:S(2)}, u32[]{:S(2)}) collective-permute-start(f32[24,512]{1,0:T(8,128)S(1)} %get-tuple-element.22), channel_id=1, source_target_pairs={{0,8},{4,12},{8,0},{12,4},{1,9},{5,13},{9,1},{13,5},{2,10},{6,14},... | collective-permute-start | bytes 147464 | tf_op jit(solution)/shard_map/ppermute | solution.py:642
  27.1 0.4 collective-permute-start.5
  27.5 0.1 pad_maximum_fusion
  27.6 0.1 reshape.266
  27.7 0.0 collective-permute-done.3.refs_1_
  27.7 2.2 %collective-permute-done.4.refs_2_ = f32[24,512]{1,0:T(8,128)S(1)} collective-permute-done((f32[24,512]{1,0:T(8,128)S(1)}, f32[24,512]{1,0:T(8,128)S(1)}, u32[]{:S(2)}, u32[]{:S(2)}) %collective-permute-start.4) | collective-permute-done | bytes 49184 | tf_op jit(solution)/shard_map/ppermute | solution.py:642
  29.9 1.2 %collective-permute-done.5.refs_3_ = f32[24,512]{1,0:T(8,128)S(1)} collective-permute-done((f32[24,512]{1,0:T(8,128)S(1)}, f32[24,512]{1,0:T(8,128)S(1)}, u32[]{:S(2)}, u32[]{:S(2)}) %collective-permute-start.5) | collective-permute-done | bytes 49184 | tf_op jit(solution)/shard_map/ppermute | solution.py:642
  31.1 0.0 copy-done.1
  31.1 1.3 %shard_map.88 = (f32[192,128]{1,0:T(8,128)S(1)}, f32[192,128]{1,0:T(8,128)S(1)}, f32[192,128]{1,0:T(8,128)S(1)}, f32[192,128]{1,0:T(8,128)S(1)}) custom-call(f32[24,512]{1,0:T(8,128)S(1)} %get-tuple-element.20.refs_0_, f32[24,512]{1,0:T(8,128)S(1)} %collective-permute-done.3.refs_1_, f32[24,512]{1,0:T(8,128)S(1)} %collective-permute-done.4.refs_2_, ...), custom_call_target="tpu_custom_call" | custom-call | tf_op jit(solution)/shard_map/pallas_call | solution.py:647
  32.4 1.7 %collective-permute-start.6 = (f32[192,128]{1,0:T(8,128)S(1)}, f32[192,128]{1,0:T(8,128)S(1)}, u32[]{:S(2)}, u32[]{:S(2)}) collective-permute-start(f32[192,128]{1,0:T(8,128)S(1)} %get-tuple-element.25), channel_id=1, source_target_pairs={{0,1},{1,0},{2,3},{3,2},{4,5},{5,4},{6,7},{7,6},{8,9},{9,8},{10,11... | collective-permute-start | bytes 294920 | tf_op jit(solution)/shard_map/ppermute | solution.py:642
  34.1 2.6 %collective-permute-start.7 = (f32[192,128]{1,0:T(8,128)S(1)}, f32[192,128]{1,0:T(8,128)S(1)}, u32[]{:S(2)}, u32[]{:S(2)}) collective-permute-start(f32[192,128]{1,0:T(8,128)S(1)} %get-tuple-element.26), channel_id=1, source_target_pairs={{0,2},{1,3},{2,0},{3,1},{4,6},{5,7},{6,4},{7,5},{8,10},{9,11},{10,... | collective-permute-start | bytes 294920 | tf_op jit(solution)/shard_map/ppermute | solution.py:642
  36.7 0.2 collective-permute-start.8
  36.9 1.0 %constant_dynamic-slice_fusion = f32[59,1024]{1,0:T(8,128)S(1)} fusion(f32[59,4096]{1,0:T(8,128)} %params_hbm.1, s32[]{:T(128)S(6)} %select_n.90), kind=kLoop, calls=%fused_computation.48 | loop fusion | bytes 483332 | tf_op jit(solution)/shard_map/dynamic_slice | solution.py:753
  37.9 0.6 %copy.20 = f32[1,1,8,3,256]{4,2,3,1,0:T(8,128)} copy(f32[1,1,8,3,256]{4,3,2,1,0:T(4,128)S(1)} %bitcast.51) | data formatting | bytes 49152
  38.5 0.0 collective-permute-done.6.refs_1_
  38.5 6.2 %collective-permute-done.7.refs_2_ = f32[192,128]{1,0:T(8,128)S(1)} collective-permute-done((f32[192,128]{1,0:T(8,128)S(1)}, f32[192,128]{1,0:T(8,128)S(1)}, u32[]{:S(2)}, u32[]{:S(2)}) %collective-permute-start.7) | collective-permute-done | bytes 98336 | tf_op jit(solution)/shard_map/ppermute | solution.py:642
  44.7 0.0 collective-permute-done.8.refs_3_
  44.7 1.6 %shard_map.89 = f32[59,1024]{1,0:T(8,128)} custom-call(f32[192,128]{1,0:T(8,128)S(1)} %get-tuple-element.24.refs_0_, f32[192,128]{1,0:T(8,128)S(1)} %collective-permute-done.6.refs_1_, f32[192,128]{1,0:T(8,128)S(1)} %collective-permute-done.7.refs_2_, f32[192,128]{1,0:T(8,128)S(1)} %collective-permute-done.8.refs_3_, f32[472,128]{1,0:T(8,128)S(1)} %reshape.267.refs_4_), custom_call_target="tpu_custom_call" | custom-call | tf_op jit(solution)/shard_map/pallas_call | solution.py:647
  (19 shorter events, 0.2 us)
Async XLA Ops:
  5.3 7.0 %collective-permute-start = (f32[24,512]{1,0:T(8,128)}, f32[24,512]{1,0:T(8,128)S(1)}, u32[]{:S(2)}, u32[]{:S(2)}) collective-permute-start(f32[24,512]{1,0:T(8,128)} %get-tuple-element.16), channel_id=1, source_target_pairs={{0,4},{4,0},{8,12},{12,8},{1,5},{5,1},{9,13},{13,9},{2,6},{6,2},{1... | collective-permute-start | bytes 147464 | tf_op jit(solution)/shard_map/ppermute | solution.py:642
  5.8 2.7 %copy-start.5 = (s32[1,1,8]{2,1,0:T(1,128)S(1)}, s32[1,1,8]{2,1,0:T(1,128)}, u32[]{:S(2)}) copy-start(s32[1,1,8]{2,1,0:T(1,128)} %param.10) | copy-start | bytes 100
  5.8 6.5 %collective-permute-start.1 = (f32[24,512]{1,0:T(8,128)}, f32[24,512]{1,0:T(8,128)S(1)}, u32[]{:S(2)}, u32[]{:S(2)}) collective-permute-start(f32[24,512]{1,0:T(8,128)} %get-tuple-element.17), channel_id=1, source_target_pairs={{0,8},{4,12},{8,0},{12,4},{1,9},{5,13},{9,1},{13,5},{2,10},{6,14},... | collective-permute-start | bytes 147464 | tf_op jit(solution)/shard_map/ppermute | solution.py:642
  8.4 0.7 %copy-start.2 = (f32[4,7]{1,0:T(4,128)S(1)}, f32[4,7]{1,0:T(4,128)}, u32[]{:S(2)}) copy-start(f32[4,7]{1,0:T(4,128)} %cameras_hbm.1) | copy-start | bytes 340
  8.4 3.9 %collective-permute-start.2 = (f32[24,512]{1,0:T(8,128)}, f32[24,512]{1,0:T(8,128)S(1)}, u32[]{:S(2)}, u32[]{:S(2)}) collective-permute-start(f32[24,512]{1,0:T(8,128)} %get-tuple-element.18), channel_id=1, source_target_pairs={{0,12},{4,8},{8,4},{12,0},{1,13},{5,9},{9,5},{13,1},{2,14},{6,10},... | collective-permute-start | bytes 147464 | tf_op jit(solution)/shard_map/ppermute | solution.py:642
  9.3 0.7 %copy-start.6 = (s32[1,1,8]{2,1,0:T(1,128)S(1)}, s32[1,1,8]{2,1,0:T(1,128)}, u32[]{:S(2)}) copy-start(s32[1,1,8]{2,1,0:T(1,128)} %param.11) | copy-start | bytes 100
  10.6 0.7 %copy-start.3 = (f32[1,1,8,3,256]{4,2,3,1,0:T(8,128)S(1)}, f32[1,1,8,3,256]{4,2,3,1,0:T(8,128)}, u32[]{:S(2)}) copy-start(f32[1,1,8,3,256]{4,2,3,1,0:T(8,128)} %param.13) | copy-start | bytes 73732
  11.3 0.7 %copy-start.4 = (s32[1,1,8,512]{3,2,1,0:T(8,128)S(1)}, s32[1,1,8,512]{3,2,1,0:T(8,128)}, u32[]{:S(2)}) copy-start(s32[1,1,8,512]{3,2,1,0:T(8,128)} %param.12) | copy-start | bytes 49156
  12.1 0.8 %copy-start = (f32[24,512]{1,0:T(8,128)S(1)}, f32[24,512]{1,0:T(8,128)}, u32[]{:S(2)}) copy-start(f32[24,512]{1,0:T(8,128)} %get-tuple-element.15.refs_0_) | copy-start | bytes 147460
  25.6 2.1 %collective-permute-start.3 = (f32[24,512]{1,0:T(8,128)S(1)}, f32[24,512]{1,0:T(8,128)S(1)}, u32[]{:S(2)}, u32[]{:S(2)}) collective-permute-start(f32[24,512]{1,0:T(8,128)S(1)} %get-tuple-element.21), channel_id=1, source_target_pairs={{0,4},{4,0},{8,12},{12,8},{1,5},{5,1},{9,13},{13,9},{2,6},{6,2},{1... | collective-permute-start | bytes 147464 | tf_op jit(solution)/shard_map/ppermute | solution.py:642
  25.8 4.1 %collective-permute-start.4 = (f32[24,512]{1,0:T(8,128)S(1)}, f32[24,512]{1,0:T(8,128)S(1)}, u32[]{:S(2)}, u32[]{:S(2)}) collective-permute-start(f32[24,512]{1,0:T(8,128)S(1)} %get-tuple-element.22), channel_id=1, source_target_pairs={{0,8},{4,12},{8,0},{12,4},{1,9},{5,13},{9,1},{13,5},{2,10},{6,14},... | collective-permute-start | bytes 147464 | tf_op jit(solution)/shard_map/ppermute | solution.py:642
  27.1 4.0 %collective-permute-start.5 = (f32[24,512]{1,0:T(8,128)S(1)}, f32[24,512]{1,0:T(8,128)S(1)}, u32[]{:S(2)}, u32[]{:S(2)}) collective-permute-start(f32[24,512]{1,0:T(8,128)S(1)} %get-tuple-element.23), channel_id=1, source_target_pairs={{0,12},{4,8},{8,4},{12,0},{1,13},{5,9},{9,5},{13,1},{2,14},{6,10},... | collective-permute-start | bytes 147464 | tf_op jit(solution)/shard_map/ppermute | solution.py:642
  27.6 3.5 %copy-start.1 = (s32[1,1,4,512]{3,2,1,0:T(4,128)S(1)}, s32[1,1,4,512]{3,2,1,0:T(4,128)}, u32[]{:S(2)}) copy-start(s32[1,1,4,512]{3,2,1,0:T(4,128)} %param.9) | copy-start | bytes 24580
  32.4 6.1 %collective-permute-start.6 = (f32[192,128]{1,0:T(8,128)S(1)}, f32[192,128]{1,0:T(8,128)S(1)}, u32[]{:S(2)}, u32[]{:S(2)}) collective-permute-start(f32[192,128]{1,0:T(8,128)S(1)} %get-tuple-element.25), channel_id=1, source_target_pairs={{0,1},{1,0},{2,3},{3,2},{4,5},{5,4},{6,7},{7,6},{8,9},{9,8},{10,11... | collective-permute-start | bytes 294920 | tf_op jit(solution)/shard_map/ppermute | solution.py:642
  34.1 10.7 %collective-permute-start.7 = (f32[192,128]{1,0:T(8,128)S(1)}, f32[192,128]{1,0:T(8,128)S(1)}, u32[]{:S(2)}, u32[]{:S(2)}) collective-permute-start(f32[192,128]{1,0:T(8,128)S(1)} %get-tuple-element.26), channel_id=1, source_target_pairs={{0,2},{1,3},{2,0},{3,1},{4,6},{5,7},{6,4},{7,5},{8,10},{9,11},{10,... | collective-permute-start | bytes 294920 | tf_op jit(solution)/shard_map/ppermute | solution.py:642
  36.7 8.1 %collective-permute-start.8 = (f32[192,128]{1,0:T(8,128)S(1)}, f32[192,128]{1,0:T(8,128)S(1)}, u32[]{:S(2)}, u32[]{:S(2)}) collective-permute-start(f32[192,128]{1,0:T(8,128)S(1)} %get-tuple-element.27), channel_id=1, source_target_pairs={{0,3},{1,2},{2,1},{3,0},{4,7},{5,6},{6,5},{7,4},{8,11},{9,10},{10,... | collective-permute-start | bytes 294920 | tf_op jit(solution)/shard_map/ppermute | solution.py:642

commit v4 on v3

--- a/solution.py
+++ b/solution.py
@@ -13,7 +13,8 @@
 COLOUR_ROW = 12
 SPAN = 256
 CHUNK = 2048
-STRIP = 128
+STRIP = 256
+NEAR = 2
 LOG2_E = 1.4426950408889634
 DEAD = -1e30
 
@@ -79,22 +80,16 @@
     return lax.dot_general(left, right, (((1,), (1,)), ((), ())), preferred_element_type=F32)
 
 
-def camera_columns(cameras):
-    cosine, sine = jnp.cos(cameras), jnp.sin(cameras)
-    c0, c1, c2 = [cosine[:, a : a + 1] for a in range(3)]
-    s0, s1, s2 = [sine[:, a : a + 1] for a in range(3)]
+def camera_parts(angles, shift, focal):
+    c0, c1, c2 = [jnp.cos(angle) for angle in angles]
+    s0, s1, s2 = [jnp.sin(angle) for angle in angles]
     rotation = [
         [c1 * c2, s0 * s1 * c2 - c0 * s2, c0 * s1 * c2 + s0 * s2],
         [c1 * s2, s0 * s1 * s2 + c0 * c2, c0 * s1 * s2 - s0 * c2],
         [-s1, s0 * c1, c0 * c1],
     ]
-    shift = [cameras[:, a : a + 1] for a in (3, 4, 5)]
     origin = [sum(rotation[m][a] * shift[m] for m in range(3)) for a in range(3)]
-    return [e for row in rotation for e in row] + shift + [cameras[:, 6:7]] + origin
-
-
-def camera_table(cameras):
-    return jnp.concatenate(camera_columns(cameras), axis=1)
+    return [e for row in rotation for e in row] + shift + [focal] + origin
 
 
 def lane_pick(source, lanes):
@@ -132,7 +127,8 @@
     for copy in copies:
         copy.start()
     copies[0].wait()
-    origin = camera_columns(cameras_ref[...])[13:16]
+    cameras = [cameras_ref[:, a : a + 1] for a in range(7)]
+    origin = camera_parts(cameras[0:3], cameras[3:6], cameras[6])[13:16]
     copies[1].wait()
     for turn, row in enumerate(partner_rows(index_ref, n_render)):
         order_ref[turn : turn + 1, :] = row
@@ -229,46 +225,96 @@
     return value, number
 
 
+def fetch(slot, view, views, blocks, turns, found):
+    me = lax.axis_index("render")
+    per_block = blocks[0].shape[1] // 128
+    lane, block = slot & 127, slot >> 7
+    found = list(found)
+    for ref, turn in zip(blocks, turns):
+        first = (me ^ turn) * per_block
+        for j in range(per_block):
+            hit = block == first + j
+            cut = slice(128 * j, 128 * j + 128)
+            for p in range(GEOMETRY):
+                piece = jnp.broadcast_to(ref[p : p + 1, cut], (8, 128))
+                found[p] = jnp.where(hit, lane_pick(piece, lane), found[p])
+            for w in range(views):
+                seen = hit & (view == w)
+                for channel in range(3):
+                    p = COLOUR_ROW + channel * views + w
+                    piece = jnp.broadcast_to(ref[p : p + 1, cut], (8, 128))
+                    at = GEOMETRY + channel
+                    found[at] = jnp.where(seen, lane_pick(piece, lane), found[at])
+    return found
+
+
+def meet_kernel(views, small_ref, list_ref, *refs):
+    blocks, (slot_ref, cam_ref, part_ref, origin_ref) = refs[:NEAR], refs[NEAR:]
+    tiles, length = list_ref.shape
+    segments = 128 // tiles
+    steps = length // segments
+    lists = list_ref[...].astype(F32)
+    turned = []
+    for segment in range(segments):
+        begin = segment * steps
+        base = lists[:, begin // 128 * 128 : begin // 128 * 128 + 128]
+        turned.append(pltpu.roll(base, 128 - begin % 128, 1) if begin % 128 else base)
+    slot_ref[...] = jnp.concatenate(turned, axis=0).T[0:steps, :].astype(jnp.int32)
+
+    def small(row):
+        return jnp.broadcast_to(small_ref[row : row + 1, :], (8, 128))
+
+    lane = lax.broadcasted_iota(jnp.int32, (8, 128), 1)
+    tile = lane & (tiles - 1)
+    code = lane_pick(small(7), tile).astype(jnp.int32)
+    view = code // (CROP * CROP)
+    cell = code - view * (CROP * CROP)
+    down = cell // CROP
+    parts = camera_parts([small(a) for a in range(3)], [small(a) for a in (3, 4, 5)], small(6))
+    for c in range(13):
+        cam_ref[c : c + 1, :] = lane_pick(parts[c], view)[0:1, :]
+    cam_ref[13:14, :] = (8 * CROP - 8 - 16 * (cell - down * CROP)).astype(F32)[0:1, :]
+    cam_ref[14:15, :] = (8 * CROP - 8 - 16 * down).astype(F32)[0:1, :]
+    cam_ref[15:16, :] = view.astype(F32)[0:1, :]
+    cam_ref[16:17, :] = lane_pick(small(8), tile)[0:1, :]
+    row = jnp.where(lane < 32, parts[13], 0.0)
+    for a in (1, 2):
+        row = row + pltpu.roll(jnp.where(lane < 32, parts[13 + a], 0.0), 32 * a, 1)
+    origin_ref[...] = row[0:1, :]
+
+    def group_work(group, _):
+        here = pl.ds(pl.multiple_of(group * 8, 8), 8)
+        found = [jnp.zeros((8, 128), F32) for _ in range(GEOMETRY + 3)]
+        found = fetch(slot_ref[here, :], view, views, blocks, range(NEAR), found)
+        for p in range(GEOMETRY + 3):
+            part_ref[p, here, :] = found[p]
+        return 0
+
+    lax.fori_loop(0, steps // 8, group_work, 0)
+
+
 def render_kernel(n_render, views, *refs):
-    blocks, refs = refs[:n_render], refs[n_render:]
-    slot_ref, cam_ref, target_ref, refs = refs[0], refs[1], refs[2], refs[3:]
+    blocks, refs = refs[: n_render - NEAR], refs[n_render - NEAR :]
+    slot_ref, cam_ref, part_ref, target_ref, refs = *refs[0:4], refs[4:]
     image_ref, outs, refs = refs[0], refs[1 : 1 + n_render], refs[1 + n_render :]
     raw_ref, stack_ref, wide_ref, alpha_ref, weight_ref, shown_ref, pass_ref, enter_ref, behind_ref, right_ref, sums_ref, lhs_ref, hot_ref, acc_ref = refs
     tiles = target_ref.shape[0]
     entry_rows = slot_ref.shape[0]
     entries = entry_rows * 128
-    cap = blocks[0].shape[1]
-    rows = blocks[0].shape[0]
-    per_block = cap // 128
+    rows, cap = blocks[0].shape
     me = lax.axis_index("render")
     groups = entry_rows // 8
 
-    def fetch(group, _):
+    def complete(group, _):
         here = pl.ds(pl.multiple_of(group * 8, 8), 8)
-        slot = slot_ref[here, :]
-        lane, block = slot & 127, slot >> 7
         view = jnp.broadcast_to(cam_ref[15:16, :], (8, 128)).astype(jnp.int32)
-        found = [jnp.zeros((8, 128), F32) for _ in range(GEOMETRY + 3)]
-        for turn in range(n_render):
-            first = (me ^ turn) * per_block
-            for j in range(per_block):
-                hit = block == first + j
-                cut = slice(128 * j, 128 * j + 128)
-                for p in range(GEOMETRY):
-                    piece = jnp.broadcast_to(blocks[turn][p : p + 1, cut], (8, 128))
-                    found[p] = jnp.where(hit, lane_pick(piece, lane), found[p])
-                for w in range(views):
-                    seen = hit & (view == w)
-                    for channel in range(3):
-                        p = COLOUR_ROW + channel * views + w
-                        piece = jnp.broadcast_to(blocks[turn][p : p + 1, cut], (8, 128))
-                        at = GEOMETRY + channel
-                        found[at] = jnp.where(seen, lane_pick(piece, lane), found[at])
+        found = [part_ref[p, here, :] for p in range(GEOMETRY + 3)]
+        found = fetch(slot_ref[here, :], view, views, blocks, range(NEAR, n_render), found)
         for p in range(GEOMETRY + 3):
             raw_ref[p, here, :] = found[p]
         return 0
 
-    lax.fori_loop(0, groups, fetch, 0)
+    lax.fori_loop(0, groups, complete, 0)
 
     def cam_rows():
         return [jnp.broadcast_to(cam_ref[i : i + 1, :], (8, 128)) for i in range(15)]
@@ -329,7 +375,9 @@
     last = 128 // tiles - 1
 
     def expose(chunk, _):
-        alpha_ref[:, chunk_of(chunk)] = jnp.exp2(dot_plain(left, wide_ref[0:32, chunk_of(chunk)]))
+        alpha = jnp.exp2(dot_plain(left, wide_ref[0:32, chunk_of(chunk)]))
+        for k in range(CHUNK // 128):
+            alpha_ref[chunk * (CHUNK // 128) + k] = alpha[:, 128 * k : 128 * k + 128]
         return 0
 
     lax.fori_loop(0, chunks, expose, 0)
@@ -349,12 +397,11 @@
         passing = [jnp.ones((8, 128), F32) for _ in range(parts)]
         shown = [[None] * parts for _ in range(3)]
         for row in range(entry_rows):
-            cut = slice(128 * row, 128 * row + 128)
             colours = colour_rows(row)
             for part in range(parts):
-                weight = passing[part] * alpha_ref[strip_of(strip, part), cut]
+                weight = passing[part] * alpha_ref[row, strip_of(strip, part), :]
                 passing[part] = passing[part] - weight
-                weight_ref[strip_of(strip, part), cut] = weight
+                weight_ref[row, strip_of(strip, part), :] = weight
                 for ch in range(3):
                     term = weight * colours[ch]
                     shown[ch][part] = term if row == 0 else shown[ch][part] + term
@@ -416,7 +463,6 @@
         residual = [[shown_ref[ch, strip_of(strip, part), :] for part in range(parts)] for ch in range(3)]
         facing = right_ref[pl.ds(pl.multiple_of(strip * STRIP, STRIP), STRIP), 0:80]
         for row in reversed(range(entry_rows)):
-            cut = slice(128 * row, 128 * row + 128)
             if row % 2:
                 shade = dot_plain(facing, wide_ref[32:112, 128 * row - 128 : 128 * row + 128])
             side = slice(128 * (row % 2), 128 * (row % 2) + 128)
@@ -425,8 +471,8 @@
             for part in range(parts):
                 here = [residual[ch][part] for ch in range(3)]
                 gap = shade[8 * part : 8 * part + 8, side] - behind[part]
-                behind[part] = behind[part] + alpha_ref[strip_of(strip, part), cut] * gap
-                weight = weight_ref[strip_of(strip, part), cut] * enter[part]
+                behind[part] = behind[part] + alpha_ref[row, strip_of(strip, part), :] * gap
+                weight = weight_ref[row, strip_of(strip, part), :] * enter[part]
                 slope = weight * gap
                 for ch in range(3):
                     term = weight * here[ch]
@@ -554,22 +600,27 @@
                 outs[turn][:, first : first + 128] = total
 
 
-def collect_kernel(n_render, n_view, *refs):
-    blocks, refs = refs[:n_render], refs[n_render:]
-    index_ref, origin_ref, refs = refs[0], refs[1], refs[2:]
-    outs, (lhs_ref, hot_ref, acc_ref) = refs[:n_view], refs[n_view:]
+def collect_kernel(n_render, n_view, own, turns, *refs):
+    final = turns[-1] == n_render - 1
+    blocks, refs = refs[: len(turns)], refs[len(turns) :]
+    index_ref, refs = refs[0], refs[1:]
     rows, cap = blocks[0].shape
-    own = outs[0].shape[0] // rows * 128
-    gaussians = own * n_view
-    spans = gaussians // SPAN
+    spans = own * n_view // SPAN
+    if final:
+        origin_ref, before_ref, refs = refs[0], refs[1], refs[2:]
+        outs, (lhs_ref, hot_ref, acc_ref) = refs[:n_view], refs[n_view:]
+    else:
+        acc_ref, lhs_ref, hot_ref = refs
     column = lax.axis_index("view")
-    for turn, index in enumerate(partner_rows(index_ref, n_render)):
-        lanes = slice(turn * cap, (turn + 1) * cap)
+    order = partner_rows(index_ref, n_render)
+    for place, turn in enumerate(turns):
+        lanes = slice(place * cap, (place + 1) * cap)
+        index = order[turn]
         span, lane = index // SPAN, index & (SPAN - 1)
         hot = lax.broadcasted_iota(jnp.int32, (SPAN, cap), 0) == jnp.broadcast_to(lane, (SPAN, cap))
         hot_ref[:, lanes] = jnp.where(hot, 1.0, 0.0).astype(BF16)
         in_span = lax.broadcasted_iota(jnp.int32, (spans, cap), 0) == jnp.broadcast_to(span, (spans, cap))
-        high, low = high_low(blocks[turn][...])
+        high, low = high_low(blocks[place][...])
         for part, value in ((0, high), (1, low)):
             for p in range(rows):
                 at = (part * rows + p) * spans
@@ -578,7 +629,10 @@
     product = dot_lanes(lhs_ref[...], hot_ref[...])
     for half in range(2):
         at = slice(half * 2 * rows * spans, (half + 1) * 2 * rows * spans)
-        acc_ref[at, :] = product[:, 128 * half : 128 * half + 128]
+        piece = product[:, 128 * half : 128 * half + 128]
+        acc_ref[at, :] = piece + before_ref[at, :] if final else piece
+    if not final:
+        return
     strips = own // 128
     for turn in range(n_view):
         for strip in range(strips):
@@ -592,21 +646,33 @@
         outs[turn][GEOMETRY * strips : GEOMETRY * strips + 1, :] = origin_ref[...]
 
 
-def owner_kernel(n_view, views, *refs):
-    blocks, (own_ref, out_ref, sum_ref) = refs[:n_view], refs[n_view:]
-    strips = out_ref.shape[1] // 128
+def owner_kernel(views, n_blocks, final, *refs):
+    blocks, refs = refs[:n_blocks], refs[n_blocks:]
+    own_ref, refs = refs[0], refs[1:]
+    if final:
+        before_ref, out_ref, sum_ref = refs
+        strips = out_ref.shape[1] // 128
+    else:
+        (sum_ref,) = refs
+        strips = sum_ref.shape[0] // (GEOMETRY + 48)
 
     def of(ref, p):
         return ref[p * strips : (p + 1) * strips, :]
 
+    def known(p):
+        return of(before_ref, p) if final else None
+
+    def plus(total, term):
+        return term if total is None else total + term
+
     position = [of(own_ref, a) for a in range(3)]
-    levels = [[None] * 16 for _ in range(3)]
-    moved = [0.0, 0.0, 0.0]
+    levels = [[known(GEOMETRY + 16 * ch + b) for b in range(16)] for ch in range(3)]
+    moved = [known(a) for a in range(3)]
     for block in blocks:
         for w in range(views):
             away = []
             for a in range(3):
-                at = 3 * w + a
+                at = 32 * a + w
                 offset = block[GEOMETRY * strips : GEOMETRY * strips + 1, at : at + 1]
                 away.append(position[a] + jnp.broadcast_to(offset, (strips, 128)))
             inverse = lax.rsqrt(away[0] * away[0] + away[1] * away[1] + away[2] * away[2])
@@ -615,25 +681,27 @@
             tint = [of(block, COLOUR_ROW + ch * views + w) for ch in range(3)]
             for ch in range(3):
                 for b in range(16):
-                    term = tint[ch] * basis[b]
-                    levels[ch][b] = term if levels[ch][b] is None else levels[ch][b] + term
+                    levels[ch][b] = plus(levels[ch][b], tint[ch] * basis[b])
             given = [
                 sum(tint[ch] * of(own_ref, GEOMETRY + 16 * ch + b) for ch in range(3)) for b in range(16)
             ]
             turned = pull(given)
             along = sum(turned[a] * direction[a] for a in range(3))
             for a in range(3):
-                moved[a] = moved[a] + inverse * (turned[a] - direction[a] * along)
+                moved[a] = plus(moved[a], inverse * (turned[a] - direction[a] * along))
     for p in range(GEOMETRY):
-        total = sum(of(block, p) for block in blocks)
-        sum_ref[p * strips : (p + 1) * strips, :] = total + moved[p] if p < 3 else total
+        total = moved[p] if p < 3 else known(p)
+        for block in blocks:
+            total = plus(total, of(block, p))
+        sum_ref[p * strips : (p + 1) * strips, :] = total
     for ch in range(3):
         for b in range(16):
             p = GEOMETRY + 16 * ch + b
             sum_ref[p * strips : (p + 1) * strips, :] = levels[ch][b]
-    count = out_ref.shape[0]
-    for strip in range(strips):
-        out_ref[:, 128 * strip : 128 * strip + 128] = sum_ref[pl.ds(strip, count, stride=strips), :]
+    if final:
+        count = out_ref.shape[0]
+        for strip in range(strips):
+            out_ref[:, 128 * strip : 128 * strip + 128] = sum_ref[pl.ds(strip, count, stride=strips), :]
 
 
 def swap(blocks, axis):
@@ -654,28 +722,33 @@
     )(*args)
 
 
-def render(n_render, views, arrived, table, code, live, slot, wanted):
-    tiles, length = slot.shape
+def meet(arrived, cameras, code, live, lists):
+    views, (tiles, length) = cameras.shape[0], lists.shape
+    rows = [jnp.pad(cameras.T, ((0, 0), (0, 128 - views)))]
+    for ids in (code, live):
+        rows.append(jnp.pad(ids.astype(F32)[None], ((0, 0), (0, 128 - tiles))))
+    small = jnp.concatenate(rows + [jnp.zeros((7, 128), F32)], axis=0)
+    entry_rows = tiles * length // 128
+    return call(
+        partial(meet_kernel, views),
+        [
+            jax.ShapeDtypeStruct((entry_rows, 128), jnp.int32),
+            jax.ShapeDtypeStruct((24, 128), F32),
+            jax.ShapeDtypeStruct((GEOMETRY + 3, entry_rows, 128), F32),
+            jax.ShapeDtypeStruct((1, 128), F32),
+        ],
+        [],
+        pltpu.VMEM,
+        small,
+        lists,
+        *arrived[:NEAR],
+    )
+
+
+def render(n_render, views, arrived, slot_lanes, lane_table, part, wanted):
     rows, cap = arrived[0].shape
-    view = code // (CROP * CROP)
-    cell = code % (CROP * CROP)
-    tile_table = sum(
-        jnp.where((view == w)[:, None], table[w : w + 1, :13], 0.0) for w in range(views)
-    )
-    extra = jnp.stack(
-        [
-            (8 * CROP - 8 - 16 * (cell % CROP)).astype(F32),
-            (8 * CROP - 8 - 16 * (cell // CROP)).astype(F32),
-            view.astype(F32),
-            live.astype(F32),
-        ],
-        axis=1,
-    )
-    lane_table = jnp.concatenate([tile_table, extra, jnp.zeros((tiles, 7), F32)], axis=1).T
-    lane_table = jnp.tile(lane_table, (1, 128 // tiles))
-    slot_lanes = slot.reshape(tiles, 128 // tiles, -1).transpose(2, 1, 0).reshape(-1, 128)
-    entries = tiles * length
-    entry_rows = entries // 128
+    entry_rows = slot_lanes.shape[0]
+    entries = entry_rows * 128
     spans = n_render * cap // SPAN
     return call(
         partial(render_kernel, n_render, views),
@@ -685,8 +758,8 @@
             pltpu.VMEM((2 * (GEOMETRY + 3), entry_rows, 128), F32),
             pltpu.VMEM((16 * entry_rows, 128), F32),
             pltpu.VMEM((112, entries), BF16),
-            pltpu.VMEM((PIXELS, entries), F32),
-            pltpu.VMEM((PIXELS, entries), F32),
+            pltpu.VMEM((entry_rows, PIXELS, 128), F32),
+            pltpu.VMEM((entry_rows, PIXELS, 128), F32),
             pltpu.VMEM((3, PIXELS, 128), F32),
             pltpu.VMEM((PIXELS, 128), F32),
             pltpu.VMEM((PIXELS, 128), F32),
@@ -698,9 +771,10 @@
             pltpu.VMEM((4 * rows * spans, 128), F32),
         ],
         pltpu.VMEM,
-        *arrived,
+        *arrived[NEAR:],
         slot_lanes,
         lane_table,
+        part,
         wanted,
     )
 
@@ -729,18 +803,32 @@
 def collect(n_render, n_view, homed, index, origin, own):
     rows, cap = homed[0].shape
     spans = n_view * own // SPAN
+    total = jax.ShapeDtypeStruct((4 * rows * spans, 128), F32)
+
+    def scratch(turns):
+        return [
+            pltpu.VMEM((2 * rows * spans, len(turns) * cap), BF16),
+            pltpu.VMEM((SPAN, len(turns) * cap), BF16),
+        ]
+
+    near, far = tuple(range(2)), tuple(range(2, n_render))
+    (early,) = call(
+        partial(collect_kernel, n_render, n_view, own, near),
+        [total],
+        scratch(near),
+        pltpu.VMEM,
+        *homed[:2],
+        index,
+    )
     return call(
-        partial(collect_kernel, n_render, n_view),
+        partial(collect_kernel, n_render, n_view, own, far),
         [jax.ShapeDtypeStruct((rows * own // 128, 128), F32)] * n_view,
-        [
-            pltpu.VMEM((2 * rows * spans, n_render * cap), BF16),
-            pltpu.VMEM((SPAN, n_render * cap), BF16),
-            pltpu.VMEM((4 * rows * spans, 128), F32),
-        ],
+        scratch(far) + [pltpu.VMEM(total.shape, F32)],
         pltpu.VMEM,
-        *homed,
+        *homed[2:],
         index,
         origin,
+        early,
     )
 
 
@@ -748,30 +836,31 @@
     index = send_index[0, 0]
     views = cameras.shape[0]
     own = params.shape[1] // n_view
-    table = camera_table(cameras)
-    origin = jnp.pad(table[:, 13:16].reshape(1, 3 * views), ((0, 0), (0, 128 - 3 * views)))
     mine = lax.dynamic_slice_in_dim(params, lax.axis_index("view") * own, own, 1).reshape(-1, 128)
 
     arrived = swap(list(slab(n_render, params, cameras, index)), "render")
-    image, *returned = render(
-        n_render,
-        views,
-        arrived,
-        table,
-        tile_id[0, 0],
-        tile_count[0, 0],
-        tile_slot[0, 0],
-        targets[0, 0],
-    )
+    slot_lanes, lane_table, part, origin = meet(
+        arrived, cameras, tile_id[0, 0], tile_count[0, 0], tile_slot[0, 0]
+    )
+    image, *returned = render(n_render, views, arrived, slot_lanes, lane_table, part, targets[0, 0])
     homed = swap(returned, "render")
     owned = swap(list(collect(n_render, n_view, homed, index, origin, own)), "view")
+    (early,) = call(
+        partial(owner_kernel, views, 2, False),
+        [jax.ShapeDtypeStruct(mine.shape, F32)],
+        [],
+        pltpu.VMEM,
+        *owned[:2],
+        mine,
+    )
     (gradients,) = call(
-        partial(owner_kernel, n_view, views),
+        partial(owner_kernel, views, n_view - 2, True),
         [jax.ShapeDtypeStruct((params.shape[0], own), F32)],
-        [pltpu.VMEM((params.shape[0] * own // 128, 128), F32)],
+        [pltpu.VMEM(mine.shape, F32)],
         pltpu.VMEM,
-        *owned,
+        *owned[2:],
         mine,
+        early,
     )
     return (image[None, None], gradients)
 

time: 46.7 us -> 43.5 us (0.931)
  local copies, waits for them, and re-layouts: 5.8 us -> 3.87 us
  waiting for transfers between devices: 9.76 us -> 7.94 us
    ppermute x9, waiting for transfers between devices: 9.76 us -> 7.94 us  [swap(): lax.ppermute(blocks[turn], axis, [(i, i ^ turn) for i in range(n)])]
    unnamed x16 -> x9, local copies, waits for them, and re-layouts: 3.86 us -> 2.78 us
    convert_element_type x4 -> x1, other arithmetic: 0.03 us -> 0.67 us  [meet(): rows.append(jnp.pad(ids.astype(F32)[None], ((0, 0), (0, 128 - tiles))))]
    pallas_call x4 -> x7, Pallas kernels: 20.1 us -> 20.2 us  [call(): pl.pallas_call(kernel, out_shape=out_shape, in_specs=[pl.BlockSpec(memory...]
  transfers between devices with their start and end apart: 9 -> 9, of which waited for: 4 -> 3; matrix products, arithmetic and copies ran while one was open for 6% -> 9% of each run, Pallas kernels for 0% -> 6%
where the time goes in v4:
time: 43.5 us; the launch traced here: 43.2 us
  Pallas kernels  20.2 us (46%)
  starting transfers between devices  9.64 us (22%)
  waiting for transfers between devices  7.94 us (18%)
  local copies, waits for them, and re-layouts  3.87 us (9%)
  other arithmetic  0.75 us (2%)
  between operations  0.75 us (2%)
    pallas_call x7, Pallas kernels, call(): pl.pallas_call(kernel, out_shape=out_shape, in_specs=[pl.BlockSpec(memory...  20.2 us
    ppermute x9, starting transfers between devices, swap(): lax.ppermute(blocks[turn], axis, [(i, i ^ turn) for i in range(n)])  9.64 us
    ppermute x9, waiting for transfers between devices, swap(): lax.ppermute(blocks[turn], axis, [(i, i ^ turn) for i in range(n)])  7.94 us
    unnamed x9, local copies, waits for them, and re-layouts  2.78 us
    dynamic_slice x1, local copies, waits for them, and re-layouts, body(): lax.dynamic_slice_in_dim(params, lax.axis_index('view') * own, own, 1)  0.97 us
  transfers between devices with their start and end apart: 9, of which 3 were waited for; matrix products, arithmetic and copies ran while one was open for 9% of the time, Pallas kernels for 6%

profile of v4, /device:TPU:0, one launch (start us, length us, event | category | flops | bytes accessed | tf_op | source)
XLA Modules:
  0.0 43.2 jit_solution(13065379461582048166)
XLA Ops:
  0.6 4.6 %shard_map.86 = (f32[24,512]{1,0:T(8,128)}, f32[24,512]{1,0:T(8,128)}, f32[24,512]{1,0:T(8,128)}, f32[24,512]{1,0:T(8,128)}) custom-call(f32[59,4096]{1,0:T(8,128)} %params_hbm.1, f32[4,7]{1,0:T(4,128)} %cameras_hbm.1, s32[4,512]{1,0:T(4,128)} %bitcast.12), custom_call_target="tpu_custom_call" | custom-call | tf_op jit(solution)/shard_map/pallas_call | solution.py:715
  5.2 0.0 copy-start.1
  5.3 3.0 %collective-permute-start = (f32[24,512]{1,0:T(8,128)}, f32[24,512]{1,0:T(8,128)S(1)}, u32[]{:S(2)}, u32[]{:S(2)}) collective-permute-start(f32[24,512]{1,0:T(8,128)} %get-tuple-element.19), channel_id=1, source_target_pairs={{0,8},{4,12},{8,0},{12,4},{1,9},{5,13},{9,1},{13,5},{2,10},{6,14},... | collective-permute-start | bytes 147464 | tf_op jit(solution)/shard_map/ppermute | solution.py:710
  8.3 0.0 collective-permute-start.1
  8.3 0.2 collective-permute-start.2
  8.5 0.8 %copy.9 = f32[4,7]{0,1:T(8,128)S(1)} copy(f32[4,7]{1,0:T(4,128)} %cameras_hbm.1) | data formatting | bytes 224 | tf_op args[1]
  9.3 0.7 %convert_bitcast_fusion = (f32[1,8]{1,0:T(1,128)S(1)}, f32[1,8]{1,0:T(1,128)S(1)}) fusion(s32[1,1,8]{2,1,0:T(1,128)} %param.11, s32[1,1,8]{2,1,0:T(1,128)} %param.10), kind=kLoop, calls=%fused_computation.11 | loop fusion | flops 16 | bytes 128 | tf_op jit(solution)/shard_map/convert_element_type | solution.py:729
  9.9 0.1 pad.17.clone
  10.0 0.1 fusion.small_ref
  10.1 0.0 copy-start.2
  10.1 0.8 %copy.13 = f32[1,1,8,3,256]{4,3,2,1,0:T(4,128)S(1)} copy(f32[1,1,8,3,256]{4,2,3,1,0:T(8,128)} %param.13) | data formatting | bytes 49152 | tf_op args[6]
  10.8 0.0 collective-permute-done.2.refs_1_
  10.9 0.0 copy-done.1
  10.9 0.0 copy-done.2
  10.9 1.4 %shard_map.87 = (s32[32,128]{1,0:T(8,128)S(1)}, f32[24,128]{1,0:T(8,128)S(1)}, f32[14,32,128]{2,1,0:T(8,128)S(1)}, f32[1,128]{1,0:T(1,128)S(1)}) custom-call(f32[16,128]{1,0:T(8,128)S(1)} %fusion.small_ref, s32[8,512]{1,0:T(8,128)S(1)} %bitcast.16, f32[24,512]{1,0:T(8,128)S(1)} %copy-done.1, f32[24,512]{1,0:T(8,128)S(1)} %collective-permute-done.2.refs_1_), custom_call_target="tpu_custom_call" | custom-call | tf_op jit(solution)/shard_map/pallas_call | solution.py:715
  12.3 0.0 collective-permute-done.refs_0_
  12.3 0.0 collective-permute-done.1.refs_1_
  12.3 11.0 %shard_map.88 = (f32[8,3,256]{2,1,0:T(4,128)S(1)}, f32[24,512]{1,0:T(8,128)S(1)}, f32[24,512]{1,0:T(8,128)S(1)}, f32[24,512]{1,0:T(8,128)S(1)}, f32[24,512]{1,0:T(8,128)S(1)}) custom-call(f32[24,512]{1,0:T(8,128)S(1)} %collective-permute-done.refs_0_, f32[24,512]{1,0:T(8,128)S(1)} %collective-permute-done.1.refs_1_, ...), custom_call_target="tpu_custom_call" | custom-call | tf_op jit(solution)/shard_map/pallas_call | solution.py:715
  23.3 0.4 collective-permute-start.5
  23.7 1.7 %collective-permute-start.3 = (f32[24,512]{1,0:T(8,128)S(1)}, f32[24,512]{1,0:T(8,128)S(1)}, u32[]{:S(2)}, u32[]{:S(2)}) collective-permute-start(f32[24,512]{1,0:T(8,128)S(1)} %get-tuple-element.27), channel_id=1, source_target_pairs={{0,8},{4,12},{8,0},{12,4},{1,9},{5,13},{9,1},{13,5},{2,10},{6,14},... | collective-permute-start | bytes 147464 | tf_op jit(solution)/shard_map/ppermute | solution.py:710
  25.4 0.0 copy-start
  25.4 0.1 collective-permute-start.4
  25.5 0.0 collective-permute-done.5.refs_1_
  25.5 0.6 %copy-done = s32[1,1,4,512]{3,2,1,0:T(4,128)S(1)} copy-done((s32[1,1,4,512]{3,2,1,0:T(4,128)S(1)}, s32[1,1,4,512]{3,2,1,0:T(4,128)}, u32[]{:S(2)}) %copy-start) | copy-done | bytes 8216
  26.1 0.6 %shard_map.89.refs_4_ = f32[1536,128]{1,0:T(8,128)S(1)} custom-call(f32[24,512]{1,0:T(8,128)S(1)} %get-tuple-element.30.refs_0_, f32[24,512]{1,0:T(8,128)S(1)} %collective-permute-done.5.refs_1_, s32[4,512]{1,0:T(4,128)S(1)} %bitcast.13), custom_call_target="tpu_custom_call" | custom-call | tf_op jit(solution)/shard_map/pallas_call | solution.py:715
  26.7 1.1 %collective-permute-done.3.refs_0_ = f32[24,512]{1,0:T(8,128)S(1)} collective-permute-done((f32[24,512]{1,0:T(8,128)S(1)}, f32[24,512]{1,0:T(8,128)S(1)}, u32[]{:S(2)}, u32[]{:S(2)}) %collective-permute-start.3) | collective-permute-done | bytes 49184 | tf_op jit(solution)/shard_map/ppermute | solution.py:710
  27.8 1.3 %collective-permute-done.4.refs_1_ = f32[24,512]{1,0:T(8,128)S(1)} collective-permute-done((f32[24,512]{1,0:T(8,128)S(1)}, f32[24,512]{1,0:T(8,128)S(1)}, u32[]{:S(2)}, u32[]{:S(2)}) %collective-permute-start.4) | collective-permute-done | bytes 49184 | tf_op jit(solution)/shard_map/ppermute | solution.py:710
  29.1 0.9 %shard_map.90 = (f32[192,128]{1,0:T(8,128)S(1)}, f32[192,128]{1,0:T(8,128)S(1)}, f32[192,128]{1,0:T(8,128)S(1)}, f32[192,128]{1,0:T(8,128)S(1)}) custom-call(f32[24,512]{1,0:T(8,128)S(1)} %collective-permute-done.3.refs_0_, f32[24,512]{1,0:T(8,128)S(1)} %collective-permute-done.4.refs_1_, s32[4,512]{1,0:T(4,128)S(1)} %bitcast.14, ...), custom_call_target="tpu_custom_call" | custom-call | tf_op jit(solution)/shard_map/pallas_call | solution.py:715
  30.0 2.7 %collective-permute-start.6 = (f32[192,128]{1,0:T(8,128)S(1)}, f32[192,128]{1,0:T(8,128)S(1)}, u32[]{:S(2)}, u32[]{:S(2)}) collective-permute-start(f32[192,128]{1,0:T(8,128)S(1)} %get-tuple-element.32), channel_id=1, source_target_pairs={{0,2},{1,3},{2,0},{3,1},{4,6},{5,7},{6,4},{7,5},{8,10},{9,11},{10,... | collective-permute-start | bytes 294920 | tf_op jit(solution)/shard_map/ppermute | solution.py:710
  32.7 1.3 %collective-permute-start.7 = (f32[192,128]{1,0:T(8,128)S(1)}, f32[192,128]{1,0:T(8,128)S(1)}, u32[]{:S(2)}, u32[]{:S(2)}) collective-permute-start(f32[192,128]{1,0:T(8,128)S(1)} %get-tuple-element.33), channel_id=1, source_target_pairs={{0,3},{1,2},{2,1},{3,0},{4,7},{5,6},{6,5},{7,4},{8,11},{9,10},{10,... | collective-permute-start | bytes 294920 | tf_op jit(solution)/shard_map/ppermute | solution.py:710
  34.0 0.2 collective-permute-start.8
  34.2 1.0 %constant_dynamic-slice_fusion = f32[59,1024]{1,0:T(8,128)S(1)} fusion(f32[59,4096]{1,0:T(8,128)} %params_hbm.1, s32[]{:T(128)S(6)} %select_n.3), kind=kLoop, calls=%fused_computation.13 | loop fusion | bytes 483332 | tf_op jit(solution)/shard_map/dynamic_slice | solution.py:839
  35.3 0.6 %copy.11 = f32[1,1,8,3,256]{4,2,3,1,0:T(8,128)} copy(f32[1,1,8,3,256]{4,3,2,1,0:T(4,128)S(1)} %bitcast.15) | data formatting | bytes 49152
  35.9 5.6 %collective-permute-done.8.refs_1_ = f32[192,128]{1,0:T(8,128)S(1)} collective-permute-done((f32[192,128]{1,0:T(8,128)S(1)}, f32[192,128]{1,0:T(8,128)S(1)}, u32[]{:S(2)}, u32[]{:S(2)}) %collective-permute-start.8) | collective-permute-done | bytes 98336 | tf_op jit(solution)/shard_map/ppermute | solution.py:710
  41.4 0.5 %shard_map.91.refs_3_ = f32[472,128]{1,0:T(8,128)S(1)} custom-call(f32[192,128]{1,0:T(8,128)S(1)} %get-tuple-element.34.refs_0_, f32[192,128]{1,0:T(8,128)S(1)} %collective-permute-done.8.refs_1_, f32[472,128]{1,0:T(8,128)S(1)} %reshape.29.refs_2_), custom_call_target="tpu_custom_call" | custom-call | tf_op jit(solution)/shard_map/pallas_call | solution.py:715
  41.9 0.0 collective-permute-done.6.refs_0_
  41.9 0.0 collective-permute-done.7.refs_1_
  41.9 1.2 %shard_map.92 = f32[59,1024]{1,0:T(8,128)} custom-call(f32[192,128]{1,0:T(8,128)S(1)} %collective-permute-done.6.refs_0_, f32[192,128]{1,0:T(8,128)S(1)} %collective-permute-done.7.refs_1_, f32[472,128]{1,0:T(8,128)S(1)} %reshape.29.refs_2_, f32[472,128]{1,0:T(8,128)S(1)} %shard_map.91.refs_3_), custom_call_target="tpu_custom_call" | custom-call | tf_op jit(solution)/shard_map/pallas_call | solution.py:715
  (2 shorter events, 0.0 us)
Async XLA Ops:
  5.2 5.6 %copy-start.1 = (f32[24,512]{1,0:T(8,128)S(1)}, f32[24,512]{1,0:T(8,128)}, u32[]{:S(2)}) copy-start(f32[24,512]{1,0:T(8,128)} %get-tuple-element.21.refs_0_) | copy-start | bytes 147460
  5.3 7.1 %collective-permute-start = (f32[24,512]{1,0:T(8,128)}, f32[24,512]{1,0:T(8,128)S(1)}, u32[]{:S(2)}, u32[]{:S(2)}) collective-permute-start(f32[24,512]{1,0:T(8,128)} %get-tuple-element.19), channel_id=1, source_target_pairs={{0,8},{4,12},{8,0},{12,4},{1,9},{5,13},{9,1},{13,5},{2,10},{6,14},... | collective-permute-start | bytes 147464 | tf_op jit(solution)/shard_map/ppermute | solution.py:710
  8.3 4.0 %collective-permute-start.1 = (f32[24,512]{1,0:T(8,128)}, f32[24,512]{1,0:T(8,128)S(1)}, u32[]{:S(2)}, u32[]{:S(2)}) collective-permute-start(f32[24,512]{1,0:T(8,128)} %get-tuple-element.20), channel_id=1, source_target_pairs={{0,12},{4,8},{8,4},{12,0},{1,13},{5,9},{9,5},{13,1},{2,14},{6,10},... | collective-permute-start | bytes 147464 | tf_op jit(solution)/shard_map/ppermute | solution.py:710
  8.3 2.6 %collective-permute-start.2 = (f32[24,512]{1,0:T(8,128)}, f32[24,512]{1,0:T(8,128)S(1)}, u32[]{:S(2)}, u32[]{:S(2)}) collective-permute-start(f32[24,512]{1,0:T(8,128)} %get-tuple-element.22), channel_id=1, source_target_pairs={{0,4},{4,0},{8,12},{12,8},{1,5},{5,1},{9,13},{13,9},{2,6},{6,2},{1... | collective-permute-start | bytes 147464 | tf_op jit(solution)/shard_map/ppermute | solution.py:710
  10.1 0.8 %copy-start.2 = (s32[1,1,8,512]{3,2,1,0:T(8,128)S(1)}, s32[1,1,8,512]{3,2,1,0:T(8,128)}, u32[]{:S(2)}) copy-start(s32[1,1,8,512]{3,2,1,0:T(8,128)} %param.12) | copy-start | bytes 49156
  23.3 2.2 %collective-permute-start.5 = (f32[24,512]{1,0:T(8,128)S(1)}, f32[24,512]{1,0:T(8,128)S(1)}, u32[]{:S(2)}, u32[]{:S(2)}) collective-permute-start(f32[24,512]{1,0:T(8,128)S(1)} %get-tuple-element.31), channel_id=1, source_target_pairs={{0,4},{4,0},{8,12},{12,8},{1,5},{5,1},{9,13},{13,9},{2,6},{6,2},{1... | collective-permute-start | bytes 147464 | tf_op jit(solution)/shard_map/ppermute | solution.py:710
  23.7 4.1 %collective-permute-start.3 = (f32[24,512]{1,0:T(8,128)S(1)}, f32[24,512]{1,0:T(8,128)S(1)}, u32[]{:S(2)}, u32[]{:S(2)}) collective-permute-start(f32[24,512]{1,0:T(8,128)S(1)} %get-tuple-element.27), channel_id=1, source_target_pairs={{0,8},{4,12},{8,0},{12,4},{1,9},{5,13},{9,1},{13,5},{2,10},{6,14},... | collective-permute-start | bytes 147464 | tf_op jit(solution)/shard_map/ppermute | solution.py:710
  25.4 0.7 %copy-start = (s32[1,1,4,512]{3,2,1,0:T(4,128)S(1)}, s32[1,1,4,512]{3,2,1,0:T(4,128)}, u32[]{:S(2)}) copy-start(s32[1,1,4,512]{3,2,1,0:T(4,128)} %param.9) | copy-start | bytes 24580
  25.4 3.7 %collective-permute-start.4 = (f32[24,512]{1,0:T(8,128)S(1)}, f32[24,512]{1,0:T(8,128)S(1)}, u32[]{:S(2)}, u32[]{:S(2)}) collective-permute-start(f32[24,512]{1,0:T(8,128)S(1)} %get-tuple-element.28), channel_id=1, source_target_pairs={{0,12},{4,8},{8,4},{12,0},{1,13},{5,9},{9,5},{13,1},{2,14},{6,10},... | collective-permute-start | bytes 147464 | tf_op jit(solution)/shard_map/ppermute | solution.py:710
  30.0 11.9 %collective-permute-start.6 = (f32[192,128]{1,0:T(8,128)S(1)}, f32[192,128]{1,0:T(8,128)S(1)}, u32[]{:S(2)}, u32[]{:S(2)}) collective-permute-start(f32[192,128]{1,0:T(8,128)S(1)} %get-tuple-element.32), channel_id=1, source_target_pairs={{0,2},{1,3},{2,0},{3,1},{4,6},{5,7},{6,4},{7,5},{8,10},{9,11},{10,... | collective-permute-start | bytes 294920 | tf_op jit(solution)/shard_map/ppermute | solution.py:710
  32.7 9.3 %collective-permute-start.7 = (f32[192,128]{1,0:T(8,128)S(1)}, f32[192,128]{1,0:T(8,128)S(1)}, u32[]{:S(2)}, u32[]{:S(2)}) collective-permute-start(f32[192,128]{1,0:T(8,128)S(1)} %get-tuple-element.33), channel_id=1, source_target_pairs={{0,3},{1,2},{2,1},{3,0},{4,7},{5,6},{6,5},{7,4},{8,11},{9,10},{10,... | collective-permute-start | bytes 294920 | tf_op jit(solution)/shard_map/ppermute | solution.py:710
  34.0 7.4 %collective-permute-start.8 = (f32[192,128]{1,0:T(8,128)S(1)}, f32[192,128]{1,0:T(8,128)S(1)}, u32[]{:S(2)}, u32[]{:S(2)}) collective-permute-start(f32[192,128]{1,0:T(8,128)S(1)} %get-tuple-element.35), channel_id=1, source_target_pairs={{0,1},{1,0},{2,3},{3,2},{4,5},{5,4},{6,7},{7,6},{8,9},{9,8},{10,11... | collective-permute-start | bytes 294920 | tf_op jit(solution)/shard_map/ppermute | solution.py:710

commit v5 on v4

--- a/solution.py
+++ b/solution.py
@@ -11,6 +11,7 @@
 PIXELS = 256
 GEOMETRY = 11
 COLOUR_ROW = 12
+TURN_ROW = 6
 SPAN = 256
 CHUNK = 2048
 STRIP = 256
@@ -248,7 +249,7 @@
     return found
 
 
-def meet_kernel(views, small_ref, list_ref, *refs):
+def meet_kernel(camera_ref, code_ref, live_ref, list_ref, *refs):
     blocks, (slot_ref, cam_ref, part_ref, origin_ref) = refs[:NEAR], refs[NEAR:]
     tiles, length = list_ref.shape
     segments = 128 // tiles
@@ -261,26 +262,35 @@
         turned.append(pltpu.roll(base, 128 - begin % 128, 1) if begin % 128 else base)
     slot_ref[...] = jnp.concatenate(turned, axis=0).T[0:steps, :].astype(jnp.int32)
 
-    def small(row):
-        return jnp.broadcast_to(small_ref[row : row + 1, :], (8, 128))
-
+    views = camera_ref.shape[0]
     lane = lax.broadcasted_iota(jnp.int32, (8, 128), 1)
-    tile = lane & (tiles - 1)
-    code = lane_pick(small(7), tile).astype(jnp.int32)
+    by_tile = lax.broadcasted_iota(jnp.int32, (8, 128), 0) < 4
+    code, live = jnp.zeros((8, 128), jnp.int32), jnp.zeros((8, 128), jnp.int32)
+    for t in range(tiles):
+        here = (lane & (tiles - 1)) == t
+        code = jnp.where(here, code_ref[0, t], code)
+        live = jnp.where(here, live_ref[0, t], live)
     view = code // (CROP * CROP)
     cell = code - view * (CROP * CROP)
     down = cell // CROP
-    parts = camera_parts([small(a) for a in range(3)], [small(a) for a in (3, 4, 5)], small(6))
+    place = jnp.where(by_tile, view, lane)
+    cameras = []
+    for c in range(7):
+        value = jnp.full((8, 128), camera_ref[0, c])
+        for w in range(1, views):
+            value = jnp.where(place == w, camera_ref[w, c], value)
+        cameras.append(value)
+    parts = camera_parts(cameras[0:3], cameras[3:6], cameras[6])
     for c in range(13):
-        cam_ref[c : c + 1, :] = lane_pick(parts[c], view)[0:1, :]
+        cam_ref[c : c + 1, :] = parts[c][0:1, :]
     cam_ref[13:14, :] = (8 * CROP - 8 - 16 * (cell - down * CROP)).astype(F32)[0:1, :]
     cam_ref[14:15, :] = (8 * CROP - 8 - 16 * down).astype(F32)[0:1, :]
     cam_ref[15:16, :] = view.astype(F32)[0:1, :]
-    cam_ref[16:17, :] = lane_pick(small(8), tile)[0:1, :]
+    cam_ref[16:17, :] = live.astype(F32)[0:1, :]
     row = jnp.where(lane < 32, parts[13], 0.0)
     for a in (1, 2):
         row = row + pltpu.roll(jnp.where(lane < 32, parts[13 + a], 0.0), 32 * a, 1)
-    origin_ref[...] = row[0:1, :]
+    origin_ref[...] = row[4:5, :]
 
     def group_work(group, _):
         here = pl.ds(pl.multiple_of(group * 8, 8), 8)
@@ -638,12 +648,13 @@
         for strip in range(strips):
             span = (column ^ turn) * (own // SPAN) + strip // 2
             first = (strip % 2) * 2 * rows * spans
-            total = (
-                acc_ref[pl.ds(first + span, rows, stride=spans), :]
-                + acc_ref[pl.ds(first + rows * spans + span, rows, stride=spans), :]
-            )
-            outs[turn][pl.ds(strip, rows, stride=strips), :] = total
-        outs[turn][GEOMETRY * strips : GEOMETRY * strips + 1, :] = origin_ref[...]
+            for p, count, to in ((0, GEOMETRY, 0), (COLOUR_ROW, rows - COLOUR_ROW, GEOMETRY)):
+                begin = first + p * spans + span
+                outs[turn][pl.ds(to * strips + strip, count, stride=strips), :] = (
+                    acc_ref[pl.ds(begin, count, stride=spans), :]
+                    + acc_ref[pl.ds(begin + rows * spans, count, stride=spans), :]
+                )
+        outs[turn][TURN_ROW * strips : TURN_ROW * strips + 1, :] = origin_ref[...]
 
 
 def owner_kernel(views, n_blocks, final, *refs):
@@ -673,12 +684,12 @@
             away = []
             for a in range(3):
                 at = 32 * a + w
-                offset = block[GEOMETRY * strips : GEOMETRY * strips + 1, at : at + 1]
+                offset = block[TURN_ROW * strips : TURN_ROW * strips + 1, at : at + 1]
                 away.append(position[a] + jnp.broadcast_to(offset, (strips, 128)))
             inverse = lax.rsqrt(away[0] * away[0] + away[1] * away[1] + away[2] * away[2])
             direction = [part * inverse for part in away]
             basis, pull = jax.vjp(harmonic_basis, *direction)
-            tint = [of(block, COLOUR_ROW + ch * views + w) for ch in range(3)]
+            tint = [of(block, GEOMETRY + ch * views + w) for ch in range(3)]
             for ch in range(3):
                 for b in range(16):
                     levels[ch][b] = plus(levels[ch][b], tint[ch] * basis[b])
@@ -689,11 +700,14 @@
             along = sum(turned[a] * direction[a] for a in range(3))
             for a in range(3):
                 moved[a] = plus(moved[a], inverse * (turned[a] - direction[a] * along))
+    totals = [moved[p] if p < 3 else known(p) for p in range(GEOMETRY)]
     for p in range(GEOMETRY):
-        total = moved[p] if p < 3 else known(p)
         for block in blocks:
-            total = plus(total, of(block, p))
-        sum_ref[p * strips : (p + 1) * strips, :] = total
+            totals[p] = plus(totals[p], of(block, p))
+    along = sum(totals[TURN_ROW + a] * of(own_ref, TURN_ROW + a) for a in (1, 2, 3))
+    totals[TURN_ROW] = -along / of(own_ref, TURN_ROW)
+    for p in range(GEOMETRY):
+        sum_ref[p * strips : (p + 1) * strips, :] = totals[p]
     for ch in range(3):
         for b in range(16):
             p = GEOMETRY + 16 * ch + b
@@ -715,7 +729,10 @@
     return pl.pallas_call(
         kernel,
         out_shape=out_shape,
-        in_specs=[pl.BlockSpec(memory_space=space)] * len(args),
+        in_specs=[
+            pl.BlockSpec(memory_space=space[i] if isinstance(space, list) else space)
+            for i in range(len(args))
+        ],
         out_specs=[pl.BlockSpec(memory_space=pltpu.VMEM)] * len(out_shape),
         scratch_shapes=scratch,
         compiler_params=pltpu.CompilerParams(vmem_limit_bytes=(64 if space == pl.ANY else 48) * 1024 * 1024),
@@ -723,14 +740,10 @@
 
 
 def meet(arrived, cameras, code, live, lists):
-    views, (tiles, length) = cameras.shape[0], lists.shape
-    rows = [jnp.pad(cameras.T, ((0, 0), (0, 128 - views)))]
-    for ids in (code, live):
-        rows.append(jnp.pad(ids.astype(F32)[None], ((0, 0), (0, 128 - tiles))))
-    small = jnp.concatenate(rows + [jnp.zeros((7, 128), F32)], axis=0)
+    tiles, length = lists.shape
     entry_rows = tiles * length // 128
     return call(
-        partial(meet_kernel, views),
+        meet_kernel,
         [
             jax.ShapeDtypeStruct((entry_rows, 128), jnp.int32),
             jax.ShapeDtypeStruct((24, 128), F32),
@@ -738,8 +751,10 @@
             jax.ShapeDtypeStruct((1, 128), F32),
         ],
         [],
-        pltpu.VMEM,
-        small,
+        [pltpu.SMEM] * 3 + [pltpu.VMEM] * (1 + NEAR),
+        cameras,
+        code,
+        live,
         lists,
         *arrived[:NEAR],
     )
@@ -822,7 +837,7 @@
     )
     return call(
         partial(collect_kernel, n_render, n_view, own, far),
-        [jax.ShapeDtypeStruct((rows * own // 128, 128), F32)] * n_view,
+        [jax.ShapeDtypeStruct(((rows - 1) * own // 128, 128), F32)] * n_view,
         scratch(far) + [pltpu.VMEM(total.shape, F32)],
         pltpu.VMEM,
         *homed[2:],
@@ -840,7 +855,7 @@
 
     arrived = swap(list(slab(n_render, params, cameras, index)), "render")
     slot_lanes, lane_table, part, origin = meet(
-        arrived, cameras, tile_id[0, 0], tile_count[0, 0], tile_slot[0, 0]
+        arrived, cameras, tile_id[0], tile_count[0], tile_slot[0, 0]
     )
     image, *returned = render(n_render, views, arrived, slot_lanes, lane_table, part, targets[0, 0])
     homed = swap(returned, "render")

time: 43.5 us -> 43.1 us (level)
  other arithmetic: 0.75 us -> 0 us
  Pallas kernels: 20.2 us -> 20.8 us
  waiting for transfers between devices: 7.94 us -> 8.44 us
    convert_element_type x1 -> x0, other arithmetic: 0.67 us -> none  [meet(): rows.append(jnp.pad(ids.astype(F32)[None], ((0, 0), (0, 128 - tiles))))]
    pallas_call x7, Pallas kernels: 20.2 us -> 20.8 us  [call(): pl.pallas_call(kernel, out_shape=out_shape, in_specs=[pl.BlockSpec(memory...]
    ppermute x9, waiting for transfers between devices: 7.94 us -> 8.44 us  [swap(): lax.ppermute(blocks[turn], axis, [(i, i ^ turn) for i in range(n)])]
    unnamed x9 -> x14, local copies, waits for them, and re-layouts: 2.78 us -> 2.52 us
  transfers between devices with their start and end apart: 9 -> 9, of which waited for: 3 -> 4; matrix products, arithmetic and copies ran while one was open for 9% -> 6% of each run, Pallas kernels for 6% -> 7%
where the time goes in v5:
time: 43.1 us; the launch traced here: 42.8 us
  Pallas kernels  20.8 us (48%)
  starting transfers between devices  9.3 us (22%)
  waiting for transfers between devices  8.44 us (20%)
  local copies, waits for them, and re-layouts  3.53 us (8%)
  between operations  0.77 us (2%)
    pallas_call x7, Pallas kernels, call(): pl.pallas_call(kernel, out_shape=out_shape, in_specs=[pl.BlockSpec(memory...  20.8 us
    ppermute x9, starting transfers between devices, swap(): lax.ppermute(blocks[turn], axis, [(i, i ^ turn) for i in range(n)])  9.3 us
    ppermute x9, waiting for transfers between devices, swap(): lax.ppermute(blocks[turn], axis, [(i, i ^ turn) for i in range(n)])  8.44 us
    unnamed x14, local copies, waits for them, and re-layouts  2.52 us
    dynamic_slice x1, local copies, waits for them, and re-layouts, body(): lax.dynamic_slice_in_dim(params, lax.axis_index('view') * own, own, 1)  0.97 us
  transfers between devices with their start and end apart: 9, of which 4 were waited for; matrix products, arithmetic and copies ran while one was open for 6% of the time, Pallas kernels for 7%

profile of v5, /device:TPU:0, one launch (start us, length us, event | category | flops | bytes accessed | tf_op | source)
XLA Modules:
  0.0 42.8 jit_solution(4320626404462127974)
XLA Ops:
  0.6 4.6 %shard_map.86 = (f32[24,512]{1,0:T(8,128)}, f32[24,512]{1,0:T(8,128)}, f32[24,512]{1,0:T(8,128)}, f32[24,512]{1,0:T(8,128)}) custom-call(f32[59,4096]{1,0:T(8,128)} %params_hbm.1, f32[4,7]{1,0:T(4,128)} %camera_ref.1, s32[4,512]{1,0:T(4,128)} %bitcast.9), custom_call_target="tpu_custom_call" | custom-call | tf_op jit(solution)/shard_map/pallas_call | solution.py:729
  5.3 0.0 copy-start.1
  5.3 0.5 %collective-permute-start.2 = (f32[24,512]{1,0:T(8,128)}, f32[24,512]{1,0:T(8,128)S(1)}, u32[]{:S(2)}, u32[]{:S(2)}) collective-permute-start(f32[24,512]{1,0:T(8,128)} %get-tuple-element.22), channel_id=1, source_target_pairs={{0,4},{4,0},{8,12},{12,8},{1,5},{5,1},{9,13},{13,9},{2,6},{6,2},{1... | collective-permute-start | bytes 147464 | tf_op jit(solution)/shard_map/ppermute | solution.py:724
  5.8 2.6 %collective-permute-start = (f32[24,512]{1,0:T(8,128)}, f32[24,512]{1,0:T(8,128)S(1)}, u32[]{:S(2)}, u32[]{:S(2)}) collective-permute-start(f32[24,512]{1,0:T(8,128)} %get-tuple-element.19), channel_id=1, source_target_pairs={{0,8},{4,12},{8,0},{12,4},{1,9},{5,13},{9,1},{13,5},{2,10},{6,14},... | collective-permute-start | bytes 147464 | tf_op jit(solution)/shard_map/ppermute | solution.py:724
  8.4 0.1 collective-permute-start.1
  8.5 0.0 copy-start.2
  8.5 0.8 %copy.12 = f32[1,1,8,3,256]{4,3,2,1,0:T(4,128)S(1)} copy(f32[1,1,8,3,256]{4,2,3,1,0:T(8,128)} %param.13) | data formatting | bytes 49152 | tf_op args[6]
  9.2 0.0 collective-permute-done.2.refs_1_
  9.2 0.0 copy-start.3
  9.2 0.0 copy-start.4
  9.3 0.0 copy-start.5
  9.3 0.0 copy-done.1
  9.3 0.0 copy-done.2
  9.3 0.6 %copy-done.3 = f32[4,7]{1,0:T(4,128)S(1)} copy-done((f32[4,7]{1,0:T(4,128)S(1)}, f32[4,7]{1,0:T(4,128)}, u32[]{:S(2)}) %copy-start.3) | copy-done | bytes 136
  9.9 0.0 copy-done.4
  9.9 0.0 copy-done.5
  9.9 2.0 %shard_map.87 = (s32[32,128]{1,0:T(8,128)S(1)}, f32[24,128]{1,0:T(8,128)S(1)}, f32[14,32,128]{2,1,0:T(8,128)S(1)}, f32[1,128]{1,0:T(1,128)S(1)}) custom-call(f32[4,7]{1,0:T(4,128)S(1)} %copy-done.3, s32[1,8]{1,0:T(1,128)S(1)} %bitcast.14, s32[1,8]{1,0:T(1,128)S(1)} %bitcast.15, s32[8,512]{1,0:T(8,128)S(1)} %bitcast.13, f32[24,512]{1,0:T(8,128)S(1)} %copy-done.1, ...), custom_call_target="tpu_custom_call" | custom-call | tf_op jit(solution)/shard_map/pallas_call | solution.py:729
  11.9 0.0 collective-permute-done.refs_0_
  11.9 0.5 %collective-permute-done.1.refs_1_ = f32[24,512]{1,0:T(8,128)S(1)} collective-permute-done((f32[24,512]{1,0:T(8,128)}, f32[24,512]{1,0:T(8,128)S(1)}, u32[]{:S(2)}, u32[]{:S(2)}) %collective-permute-start.1) | collective-permute-done | bytes 49184 | tf_op jit(solution)/shard_map/ppermute | solution.py:724
  12.4 11.0 %shard_map.88 = (f32[8,3,256]{2,1,0:T(4,128)S(1)}, f32[24,512]{1,0:T(8,128)S(1)}, f32[24,512]{1,0:T(8,128)S(1)}, f32[24,512]{1,0:T(8,128)S(1)}, f32[24,512]{1,0:T(8,128)S(1)}) custom-call(f32[24,512]{1,0:T(8,128)S(1)} %collective-permute-done.refs_0_, f32[24,512]{1,0:T(8,128)S(1)} %collective-permute-done.1.refs_1_, ...), custom_call_target="tpu_custom_call" | custom-call | tf_op jit(solution)/shard_map/pallas_call | solution.py:729
  23.4 0.2 collective-permute-start.5
  23.6 1.5 %collective-permute-start.3 = (f32[24,512]{1,0:T(8,128)S(1)}, f32[24,512]{1,0:T(8,128)S(1)}, u32[]{:S(2)}, u32[]{:S(2)}) collective-permute-start(f32[24,512]{1,0:T(8,128)S(1)} %get-tuple-element.27), channel_id=1, source_target_pairs={{0,8},{4,12},{8,0},{12,4},{1,9},{5,13},{9,1},{13,5},{2,10},{6,14},... | collective-permute-start | bytes 147464 | tf_op jit(solution)/shard_map/ppermute | solution.py:724
  25.1 0.0 copy-start
  25.1 0.2 collective-permute-start.4
  25.3 0.0 collective-permute-done.5.refs_1_
  25.3 0.5 %copy-done = s32[1,1,4,512]{3,2,1,0:T(4,128)S(1)} copy-done((s32[1,1,4,512]{3,2,1,0:T(4,128)S(1)}, s32[1,1,4,512]{3,2,1,0:T(4,128)}, u32[]{:S(2)}) %copy-start) | copy-done | bytes 8216
  25.8 0.6 %shard_map.89.refs_4_ = f32[1536,128]{1,0:T(8,128)S(1)} custom-call(f32[24,512]{1,0:T(8,128)S(1)} %get-tuple-element.30.refs_0_, f32[24,512]{1,0:T(8,128)S(1)} %collective-permute-done.5.refs_1_, s32[4,512]{1,0:T(4,128)S(1)} %bitcast.10), custom_call_target="tpu_custom_call" | custom-call | tf_op jit(solution)/shard_map/pallas_call | solution.py:729
  26.4 1.3 %collective-permute-done.3.refs_0_ = f32[24,512]{1,0:T(8,128)S(1)} collective-permute-done((f32[24,512]{1,0:T(8,128)S(1)}, f32[24,512]{1,0:T(8,128)S(1)}, u32[]{:S(2)}, u32[]{:S(2)}) %collective-permute-start.3) | collective-permute-done | bytes 49184 | tf_op jit(solution)/shard_map/ppermute | solution.py:724
  27.7 1.4 %collective-permute-done.4.refs_1_ = f32[24,512]{1,0:T(8,128)S(1)} collective-permute-done((f32[24,512]{1,0:T(8,128)S(1)}, f32[24,512]{1,0:T(8,128)S(1)}, u32[]{:S(2)}, u32[]{:S(2)}) %collective-permute-start.4) | collective-permute-done | bytes 49184 | tf_op jit(solution)/shard_map/ppermute | solution.py:724
  29.1 0.9 %shard_map.90 = (f32[184,128]{1,0:T(8,128)S(1)}, f32[184,128]{1,0:T(8,128)S(1)}, f32[184,128]{1,0:T(8,128)S(1)}, f32[184,128]{1,0:T(8,128)S(1)}) custom-call(f32[24,512]{1,0:T(8,128)S(1)} %collective-permute-done.3.refs_0_, f32[24,512]{1,0:T(8,128)S(1)} %collective-permute-done.4.refs_1_, s32[4,512]{1,0:T(4,128)S(1)} %bitcast.11, ...), custom_call_target="tpu_custom_call" | custom-call | tf_op jit(solution)/shard_map/pallas_call | solution.py:729
  29.9 2.6 %collective-permute-start.6 = (f32[184,128]{1,0:T(8,128)S(1)}, f32[184,128]{1,0:T(8,128)S(1)}, u32[]{:S(2)}, u32[]{:S(2)}) collective-permute-start(f32[184,128]{1,0:T(8,128)S(1)} %get-tuple-element.32), channel_id=1, source_target_pairs={{0,2},{1,3},{2,0},{3,1},{4,6},{5,7},{6,4},{7,5},{8,10},{9,11},{10,... | collective-permute-start | bytes 282632 | tf_op jit(solution)/shard_map/ppermute | solution.py:724
  32.6 1.3 %collective-permute-start.7 = (f32[184,128]{1,0:T(8,128)S(1)}, f32[184,128]{1,0:T(8,128)S(1)}, u32[]{:S(2)}, u32[]{:S(2)}) collective-permute-start(f32[184,128]{1,0:T(8,128)S(1)} %get-tuple-element.33), channel_id=1, source_target_pairs={{0,3},{1,2},{2,1},{3,0},{4,7},{5,6},{6,5},{7,4},{8,11},{9,10},{10,... | collective-permute-start | bytes 282632 | tf_op jit(solution)/shard_map/ppermute | solution.py:724
  33.9 0.2 collective-permute-start.8
  34.1 1.0 %constant_dynamic-slice_fusion = f32[59,1024]{1,0:T(8,128)S(1)} fusion(f32[59,4096]{1,0:T(8,128)} %params_hbm.1, s32[]{:T(128)S(6)} %select_n.3), kind=kLoop, calls=%fused_computation.1 | loop fusion | bytes 483332 | tf_op jit(solution)/shard_map/dynamic_slice | solution.py:854
  35.2 0.6 %copy.10 = f32[1,1,8,3,256]{4,2,3,1,0:T(8,128)} copy(f32[1,1,8,3,256]{4,3,2,1,0:T(4,128)S(1)} %bitcast.12) | data formatting | bytes 49152
  35.8 5.3 %collective-permute-done.8.refs_1_ = f32[184,128]{1,0:T(8,128)S(1)} collective-permute-done((f32[184,128]{1,0:T(8,128)S(1)}, f32[184,128]{1,0:T(8,128)S(1)}, u32[]{:S(2)}, u32[]{:S(2)}) %collective-permute-start.8) | collective-permute-done | bytes 94240 | tf_op jit(solution)/shard_map/ppermute | solution.py:724
  41.1 0.5 %shard_map.91.refs_3_ = f32[472,128]{1,0:T(8,128)S(1)} custom-call(f32[184,128]{1,0:T(8,128)S(1)} %get-tuple-element.34.refs_0_, f32[184,128]{1,0:T(8,128)S(1)} %collective-permute-done.8.refs_1_, f32[472,128]{1,0:T(8,128)S(1)} %reshape.7.refs_2_), custom_call_target="tpu_custom_call" | custom-call | tf_op jit(solution)/shard_map/pallas_call | solution.py:729
  41.6 0.0 collective-permute-done.6.refs_0_
  41.6 0.0 collective-permute-done.7.refs_1_
  41.6 1.2 %shard_map.92 = f32[59,1024]{1,0:T(8,128)} custom-call(f32[184,128]{1,0:T(8,128)S(1)} %collective-permute-done.6.refs_0_, f32[184,128]{1,0:T(8,128)S(1)} %collective-permute-done.7.refs_1_, f32[472,128]{1,0:T(8,128)S(1)} %reshape.7.refs_2_, f32[472,128]{1,0:T(8,128)S(1)} %shard_map.91.refs_3_), custom_call_target="tpu_custom_call" | custom-call | tf_op jit(solution)/shard_map/pallas_call | solution.py:729
  (1 shorter events, 0.0 us)
Async XLA Ops:
  5.3 4.0 %copy-start.1 = (f32[24,512]{1,0:T(8,128)S(1)}, f32[24,512]{1,0:T(8,128)}, u32[]{:S(2)}) copy-start(f32[24,512]{1,0:T(8,128)} %get-tuple-element.21.refs_0_) | copy-start | bytes 147460
  5.3 4.0 %collective-permute-start.2 = (f32[24,512]{1,0:T(8,128)}, f32[24,512]{1,0:T(8,128)S(1)}, u32[]{:S(2)}, u32[]{:S(2)}) collective-permute-start(f32[24,512]{1,0:T(8,128)} %get-tuple-element.22), channel_id=1, source_target_pairs={{0,4},{4,0},{8,12},{12,8},{1,5},{5,1},{9,13},{13,9},{2,6},{6,2},{1... | collective-permute-start | bytes 147464 | tf_op jit(solution)/shard_map/ppermute | solution.py:724
  5.8 6.1 %collective-permute-start = (f32[24,512]{1,0:T(8,128)}, f32[24,512]{1,0:T(8,128)S(1)}, u32[]{:S(2)}, u32[]{:S(2)}) collective-permute-start(f32[24,512]{1,0:T(8,128)} %get-tuple-element.19), channel_id=1, source_target_pairs={{0,8},{4,12},{8,0},{12,4},{1,9},{5,13},{9,1},{13,5},{2,10},{6,14},... | collective-permute-start | bytes 147464 | tf_op jit(solution)/shard_map/ppermute | solution.py:724
  8.4 4.0 %collective-permute-start.1 = (f32[24,512]{1,0:T(8,128)}, f32[24,512]{1,0:T(8,128)S(1)}, u32[]{:S(2)}, u32[]{:S(2)}) collective-permute-start(f32[24,512]{1,0:T(8,128)} %get-tuple-element.20), channel_id=1, source_target_pairs={{0,12},{4,8},{8,4},{12,0},{1,13},{5,9},{9,5},{13,1},{2,14},{6,10},... | collective-permute-start | bytes 147464 | tf_op jit(solution)/shard_map/ppermute | solution.py:724
  8.5 0.8 %copy-start.2 = (s32[1,1,8,512]{3,2,1,0:T(8,128)S(1)}, s32[1,1,8,512]{3,2,1,0:T(8,128)}, u32[]{:S(2)}) copy-start(s32[1,1,8,512]{3,2,1,0:T(8,128)} %param.12) | copy-start | bytes 49156
  9.2 0.7 %copy-start.3 = (f32[4,7]{1,0:T(4,128)S(1)}, f32[4,7]{1,0:T(4,128)}, u32[]{:S(2)}) copy-start(f32[4,7]{1,0:T(4,128)} %camera_ref.1) | copy-start | bytes 340
  9.2 0.7 %copy-start.4 = (s32[1,1,8]{2,1,0:T(1,128)S(1)}, s32[1,1,8]{2,1,0:T(1,128)}, u32[]{:S(2)}) copy-start(s32[1,1,8]{2,1,0:T(1,128)} %param.10) | copy-start | bytes 100
  9.3 0.7 %copy-start.5 = (s32[1,1,8]{2,1,0:T(1,128)S(1)}, s32[1,1,8]{2,1,0:T(1,128)}, u32[]{:S(2)}) copy-start(s32[1,1,8]{2,1,0:T(1,128)} %param.11) | copy-start | bytes 100
  23.4 1.9 %collective-permute-start.5 = (f32[24,512]{1,0:T(8,128)S(1)}, f32[24,512]{1,0:T(8,128)S(1)}, u32[]{:S(2)}, u32[]{:S(2)}) collective-permute-start(f32[24,512]{1,0:T(8,128)S(1)} %get-tuple-element.31), channel_id=1, source_target_pairs={{0,4},{4,0},{8,12},{12,8},{1,5},{5,1},{9,13},{13,9},{2,6},{6,2},{1... | collective-permute-start | bytes 147464 | tf_op jit(solution)/shard_map/ppermute | solution.py:724
  23.6 4.1 %collective-permute-start.3 = (f32[24,512]{1,0:T(8,128)S(1)}, f32[24,512]{1,0:T(8,128)S(1)}, u32[]{:S(2)}, u32[]{:S(2)}) collective-permute-start(f32[24,512]{1,0:T(8,128)S(1)} %get-tuple-element.27), channel_id=1, source_target_pairs={{0,8},{4,12},{8,0},{12,4},{1,9},{5,13},{9,1},{13,5},{2,10},{6,14},... | collective-permute-start | bytes 147464 | tf_op jit(solution)/shard_map/ppermute | solution.py:724
  25.1 0.7 %copy-start = (s32[1,1,4,512]{3,2,1,0:T(4,128)S(1)}, s32[1,1,4,512]{3,2,1,0:T(4,128)}, u32[]{:S(2)}) copy-start(s32[1,1,4,512]{3,2,1,0:T(4,128)} %param.9) | copy-start | bytes 24580
  25.1 4.0 %collective-permute-start.4 = (f32[24,512]{1,0:T(8,128)S(1)}, f32[24,512]{1,0:T(8,128)S(1)}, u32[]{:S(2)}, u32[]{:S(2)}) collective-permute-start(f32[24,512]{1,0:T(8,128)S(1)} %get-tuple-element.28), channel_id=1, source_target_pairs={{0,12},{4,8},{8,4},{12,0},{1,13},{5,9},{9,5},{13,1},{2,14},{6,10},... | collective-permute-start | bytes 147464 | tf_op jit(solution)/shard_map/ppermute | solution.py:724
  29.9 11.6 %collective-permute-start.6 = (f32[184,128]{1,0:T(8,128)S(1)}, f32[184,128]{1,0:T(8,128)S(1)}, u32[]{:S(2)}, u32[]{:S(2)}) collective-permute-start(f32[184,128]{1,0:T(8,128)S(1)} %get-tuple-element.32), channel_id=1, source_target_pairs={{0,2},{1,3},{2,0},{3,1},{4,6},{5,7},{6,4},{7,5},{8,10},{9,11},{10,... | collective-permute-start | bytes 282632 | tf_op jit(solution)/shard_map/ppermute | solution.py:724
  32.6 9.0 %collective-permute-start.7 = (f32[184,128]{1,0:T(8,128)S(1)}, f32[184,128]{1,0:T(8,128)S(1)}, u32[]{:S(2)}, u32[]{:S(2)}) collective-permute-start(f32[184,128]{1,0:T(8,128)S(1)} %get-tuple-element.33), channel_id=1, source_target_pairs={{0,3},{1,2},{2,1},{3,0},{4,7},{5,6},{6,5},{7,4},{8,11},{9,10},{10,... | collective-permute-start | bytes 282632 | tf_op jit(solution)/shard_map/ppermute | solution.py:724
  33.9 7.2 %collective-permute-start.8 = (f32[184,128]{1,0:T(8,128)S(1)}, f32[184,128]{1,0:T(8,128)S(1)}, u32[]{:S(2)}, u32[]{:S(2)}) collective-permute-start(f32[184,128]{1,0:T(8,128)S(1)} %get-tuple-element.35), channel_id=1, source_target_pairs={{0,1},{1,0},{2,3},{3,2},{4,5},{5,4},{6,7},{7,6},{8,9},{9,8},{10,11... | collective-permute-start | bytes 282632 | tf_op jit(solution)/shard_map/ppermute | solution.py:724

commit v6 on v5

--- a/solution.py
+++ b/solution.py
@@ -13,7 +13,7 @@
 COLOUR_ROW = 12
 TURN_ROW = 6
 SPAN = 256
-CHUNK = 2048
+CHUNK = 4096
 STRIP = 256
 NEAR = 2
 LOG2_E = 1.4426950408889634
@@ -588,11 +588,11 @@
                 lhs_ref[at : at + views * spans, at_lanes] = value.astype(BF16)
 
     def spread_rows(step, _):
-        for i in range(4):
-            spread_out(step * 4 + i, 0)
-        return 0
-
-    lax.fori_loop(0, entry_rows // 4, spread_rows, 0)
+        for i in range(8):
+            spread_out(step * 8 + i, 0)
+        return 0
+
+    lax.fori_loop(0, entry_rows // 8, spread_rows, 0)
     product = dot_lanes(lhs_ref[...], hot_ref[...])
     for half in range(SPAN // 128):
         at = slice(half * 2 * half_rows, (half + 1) * 2 * half_rows)
@@ -771,7 +771,7 @@
         + [jax.ShapeDtypeStruct((rows, cap), F32)] * n_render,
         [
             pltpu.VMEM((2 * (GEOMETRY + 3), entry_rows, 128), F32),
-            pltpu.VMEM((16 * entry_rows, 128), F32),
+            pltpu.VMEM((17 * entry_rows, 128), F32),
             pltpu.VMEM((112, entries), BF16),
             pltpu.VMEM((entry_rows, PIXELS, 128), F32),
             pltpu.VMEM((entry_rows, PIXELS, 128), F32),
@@ -783,7 +783,7 @@
             pltpu.VMEM((9 * PIXELS // STRIP * 8 * entry_rows, 128), F32),
             pltpu.VMEM((2 * rows * spans, entries), BF16),
             pltpu.VMEM((SPAN, entries), BF16),
-            pltpu.VMEM((4 * rows * spans, 128), F32),
+            pltpu.VMEM((4 * rows * spans + spans, 128), F32),
         ],
         pltpu.VMEM,
         *arrived[NEAR:],

time: 43.1 us -> 42.7 us (level)
  no operation moved by 1% of the time
where the time goes in v6:
time: 42.7 us; the launch traced here: 42.5 us
  Pallas kernels  20.5 us (48%)
  starting transfers between devices  9.34 us (22%)
  waiting for transfers between devices  8.38 us (20%)
  local copies, waits for them, and re-layouts  3.51 us (8%)
  between operations  0.77 us (2%)
    pallas_call x7, Pallas kernels, call(): pl.pallas_call(kernel, out_shape=out_shape, in_specs=[pl.BlockSpec(memory...  20.5 us
    ppermute x9, starting transfers between devices, swap(): lax.ppermute(blocks[turn], axis, [(i, i ^ turn) for i in range(n)])  9.34 us
    ppermute x9, waiting for transfers between devices, swap(): lax.ppermute(blocks[turn], axis, [(i, i ^ turn) for i in range(n)])  8.38 us
    unnamed x14, local copies, waits for them, and re-layouts  2.5 us
    dynamic_slice x1, local copies, waits for them, and re-layouts, body(): lax.dynamic_slice_in_dim(params, lax.axis_index('view') * own, own, 1)  0.97 us
  transfers between devices with their start and end apart: 9, of which 4 were waited for; matrix products, arithmetic and copies ran while one was open for 6% of the time, Pallas kernels for 7%

profile of v6, /device:TPU:0, one launch (start us, length us, event | category | flops | bytes accessed | tf_op | source)
XLA Modules:
  0.0 42.5 jit_solution(16813407688289000477)
XLA Ops:
  0.6 4.6 %shard_map.86 = (f32[24,512]{1,0:T(8,128)}, f32[24,512]{1,0:T(8,128)}, f32[24,512]{1,0:T(8,128)}, f32[24,512]{1,0:T(8,128)}) custom-call(f32[59,4096]{1,0:T(8,128)} %params_hbm.1, f32[4,7]{1,0:T(4,128)} %camera_ref.1, s32[4,512]{1,0:T(4,128)} %bitcast.9), custom_call_target="tpu_custom_call" | custom-call | tf_op jit(solution)/shard_map/pallas_call | solution.py:729
  5.3 0.0 copy-start.1
  5.3 0.5 %collective-permute-start.2 = (f32[24,512]{1,0:T(8,128)}, f32[24,512]{1,0:T(8,128)S(1)}, u32[]{:S(2)}, u32[]{:S(2)}) collective-permute-start(f32[24,512]{1,0:T(8,128)} %get-tuple-element.22), channel_id=1, source_target_pairs={{0,4},{4,0},{8,12},{12,8},{1,5},{5,1},{9,13},{13,9},{2,6},{6,2},{1... | collective-permute-start | bytes 147464 | tf_op jit(solution)/shard_map/ppermute | solution.py:724
  5.8 2.6 %collective-permute-start = (f32[24,512]{1,0:T(8,128)}, f32[24,512]{1,0:T(8,128)S(1)}, u32[]{:S(2)}, u32[]{:S(2)}) collective-permute-start(f32[24,512]{1,0:T(8,128)} %get-tuple-element.19), channel_id=1, source_target_pairs={{0,8},{4,12},{8,0},{12,4},{1,9},{5,13},{9,1},{13,5},{2,10},{6,14},... | collective-permute-start | bytes 147464 | tf_op jit(solution)/shard_map/ppermute | solution.py:724
  8.4 0.1 collective-permute-start.1
  8.5 0.0 copy-start.2
  8.5 0.8 %copy.12 = f32[1,1,8,3,256]{4,3,2,1,0:T(4,128)S(1)} copy(f32[1,1,8,3,256]{4,2,3,1,0:T(8,128)} %param.13) | data formatting | bytes 49152 | tf_op args[6]
  9.2 0.0 collective-permute-done.2.refs_1_
  9.2 0.0 copy-start.3
  9.2 0.0 copy-start.4
  9.3 0.0 copy-start.5
  9.3 0.0 copy-done.1
  9.3 0.0 copy-done.2
  9.3 0.6 %copy-done.3 = f32[4,7]{1,0:T(4,128)S(1)} copy-done((f32[4,7]{1,0:T(4,128)S(1)}, f32[4,7]{1,0:T(4,128)}, u32[]{:S(2)}) %copy-start.3) | copy-done | bytes 136
  9.9 0.0 copy-done.4
  9.9 0.0 copy-done.5
  9.9 2.0 %shard_map.87 = (s32[32,128]{1,0:T(8,128)S(1)}, f32[24,128]{1,0:T(8,128)S(1)}, f32[14,32,128]{2,1,0:T(8,128)S(1)}, f32[1,128]{1,0:T(1,128)S(1)}) custom-call(f32[4,7]{1,0:T(4,128)S(1)} %copy-done.3, s32[1,8]{1,0:T(1,128)S(1)} %bitcast.14, s32[1,8]{1,0:T(1,128)S(1)} %bitcast.15, s32[8,512]{1,0:T(8,128)S(1)} %bitcast.13, f32[24,512]{1,0:T(8,128)S(1)} %copy-done.1, ...), custom_call_target="tpu_custom_call" | custom-call | tf_op jit(solution)/shard_map/pallas_call | solution.py:729
  11.9 0.0 collective-permute-done.refs_0_
  11.9 0.5 %collective-permute-done.1.refs_1_ = f32[24,512]{1,0:T(8,128)S(1)} collective-permute-done((f32[24,512]{1,0:T(8,128)}, f32[24,512]{1,0:T(8,128)S(1)}, u32[]{:S(2)}, u32[]{:S(2)}) %collective-permute-start.1) | collective-permute-done | bytes 49184 | tf_op jit(solution)/shard_map/ppermute | solution.py:724
  12.4 10.6 %shard_map.88 = (f32[8,3,256]{2,1,0:T(4,128)S(1)}, f32[24,512]{1,0:T(8,128)S(1)}, f32[24,512]{1,0:T(8,128)S(1)}, f32[24,512]{1,0:T(8,128)S(1)}, f32[24,512]{1,0:T(8,128)S(1)}) custom-call(f32[24,512]{1,0:T(8,128)S(1)} %collective-permute-done.refs_0_, f32[24,512]{1,0:T(8,128)S(1)} %collective-permute-done.1.refs_1_, ...), custom_call_target="tpu_custom_call" | custom-call | tf_op jit(solution)/shard_map/pallas_call | solution.py:729
  23.0 0.2 collective-permute-start.5
  23.2 1.5 %collective-permute-start.3 = (f32[24,512]{1,0:T(8,128)S(1)}, f32[24,512]{1,0:T(8,128)S(1)}, u32[]{:S(2)}, u32[]{:S(2)}) collective-permute-start(f32[24,512]{1,0:T(8,128)S(1)} %get-tuple-element.27), channel_id=1, source_target_pairs={{0,8},{4,12},{8,0},{12,4},{1,9},{5,13},{9,1},{13,5},{2,10},{6,14},... | collective-permute-start | bytes 147464 | tf_op jit(solution)/shard_map/ppermute | solution.py:724
  24.7 0.0 copy-start
  24.7 0.2 collective-permute-start.4
  25.0 0.0 collective-permute-done.5.refs_1_
  25.0 0.5 %copy-done = s32[1,1,4,512]{3,2,1,0:T(4,128)S(1)} copy-done((s32[1,1,4,512]{3,2,1,0:T(4,128)S(1)}, s32[1,1,4,512]{3,2,1,0:T(4,128)}, u32[]{:S(2)}) %copy-start) | copy-done | bytes 8216
  25.4 0.6 %shard_map.89.refs_4_ = f32[1536,128]{1,0:T(8,128)S(1)} custom-call(f32[24,512]{1,0:T(8,128)S(1)} %get-tuple-element.30.refs_0_, f32[24,512]{1,0:T(8,128)S(1)} %collective-permute-done.5.refs_1_, s32[4,512]{1,0:T(4,128)S(1)} %bitcast.10), custom_call_target="tpu_custom_call" | custom-call | tf_op jit(solution)/shard_map/pallas_call | solution.py:729
  26.1 1.3 %collective-permute-done.3.refs_0_ = f32[24,512]{1,0:T(8,128)S(1)} collective-permute-done((f32[24,512]{1,0:T(8,128)S(1)}, f32[24,512]{1,0:T(8,128)S(1)}, u32[]{:S(2)}, u32[]{:S(2)}) %collective-permute-start.3) | collective-permute-done | bytes 49184 | tf_op jit(solution)/shard_map/ppermute | solution.py:724
  27.3 1.4 %collective-permute-done.4.refs_1_ = f32[24,512]{1,0:T(8,128)S(1)} collective-permute-done((f32[24,512]{1,0:T(8,128)S(1)}, f32[24,512]{1,0:T(8,128)S(1)}, u32[]{:S(2)}, u32[]{:S(2)}) %collective-permute-start.4) | collective-permute-done | bytes 49184 | tf_op jit(solution)/shard_map/ppermute | solution.py:724
  28.7 0.9 %shard_map.90 = (f32[184,128]{1,0:T(8,128)S(1)}, f32[184,128]{1,0:T(8,128)S(1)}, f32[184,128]{1,0:T(8,128)S(1)}, f32[184,128]{1,0:T(8,128)S(1)}) custom-call(f32[24,512]{1,0:T(8,128)S(1)} %collective-permute-done.3.refs_0_, f32[24,512]{1,0:T(8,128)S(1)} %collective-permute-done.4.refs_1_, s32[4,512]{1,0:T(4,128)S(1)} %bitcast.11, ...), custom_call_target="tpu_custom_call" | custom-call | tf_op jit(solution)/shard_map/pallas_call | solution.py:729
  29.6 2.7 %collective-permute-start.6 = (f32[184,128]{1,0:T(8,128)S(1)}, f32[184,128]{1,0:T(8,128)S(1)}, u32[]{:S(2)}, u32[]{:S(2)}) collective-permute-start(f32[184,128]{1,0:T(8,128)S(1)} %get-tuple-element.32), channel_id=1, source_target_pairs={{0,2},{1,3},{2,0},{3,1},{4,6},{5,7},{6,4},{7,5},{8,10},{9,11},{10,... | collective-permute-start | bytes 282632 | tf_op jit(solution)/shard_map/ppermute | solution.py:724
  32.2 1.3 %collective-permute-start.7 = (f32[184,128]{1,0:T(8,128)S(1)}, f32[184,128]{1,0:T(8,128)S(1)}, u32[]{:S(2)}, u32[]{:S(2)}) collective-permute-start(f32[184,128]{1,0:T(8,128)S(1)} %get-tuple-element.33), channel_id=1, source_target_pairs={{0,3},{1,2},{2,1},{3,0},{4,7},{5,6},{6,5},{7,4},{8,11},{9,10},{10,... | collective-permute-start | bytes 282632 | tf_op jit(solution)/shard_map/ppermute | solution.py:724
  33.6 0.2 collective-permute-start.8
  33.8 1.0 %constant_dynamic-slice_fusion = f32[59,1024]{1,0:T(8,128)S(1)} fusion(f32[59,4096]{1,0:T(8,128)} %params_hbm.1, s32[]{:T(128)S(6)} %select_n.3), kind=kLoop, calls=%fused_computation.1 | loop fusion | bytes 483332 | tf_op jit(solution)/shard_map/dynamic_slice | solution.py:854
  34.8 0.6 %copy.10 = f32[1,1,8,3,256]{4,2,3,1,0:T(8,128)} copy(f32[1,1,8,3,256]{4,3,2,1,0:T(4,128)S(1)} %bitcast.12) | data formatting | bytes 49152
  35.5 5.3 %collective-permute-done.8.refs_1_ = f32[184,128]{1,0:T(8,128)S(1)} collective-permute-done((f32[184,128]{1,0:T(8,128)S(1)}, f32[184,128]{1,0:T(8,128)S(1)}, u32[]{:S(2)}, u32[]{:S(2)}) %collective-permute-start.8) | collective-permute-done | bytes 94240 | tf_op jit(solution)/shard_map/ppermute | solution.py:724
  40.7 0.5 %shard_map.91.refs_3_ = f32[472,128]{1,0:T(8,128)S(1)} custom-call(f32[184,128]{1,0:T(8,128)S(1)} %get-tuple-element.34.refs_0_, f32[184,128]{1,0:T(8,128)S(1)} %collective-permute-done.8.refs_1_, f32[472,128]{1,0:T(8,128)S(1)} %reshape.7.refs_2_), custom_call_target="tpu_custom_call" | custom-call | tf_op jit(solution)/shard_map/pallas_call | solution.py:729
  41.2 0.0 collective-permute-done.6.refs_0_
  41.2 0.0 collective-permute-done.7.refs_1_
  41.2 1.2 %shard_map.92 = f32[59,1024]{1,0:T(8,128)} custom-call(f32[184,128]{1,0:T(8,128)S(1)} %collective-permute-done.6.refs_0_, f32[184,128]{1,0:T(8,128)S(1)} %collective-permute-done.7.refs_1_, f32[472,128]{1,0:T(8,128)S(1)} %reshape.7.refs_2_, f32[472,128]{1,0:T(8,128)S(1)} %shard_map.91.refs_3_), custom_call_target="tpu_custom_call" | custom-call | tf_op jit(solution)/shard_map/pallas_call | solution.py:729
  (1 shorter events, 0.0 us)
Async XLA Ops:
  5.3 4.0 %copy-start.1 = (f32[24,512]{1,0:T(8,128)S(1)}, f32[24,512]{1,0:T(8,128)}, u32[]{:S(2)}) copy-start(f32[24,512]{1,0:T(8,128)} %get-tuple-element.21.refs_0_) | copy-start | bytes 147460
  5.3 4.0 %collective-permute-start.2 = (f32[24,512]{1,0:T(8,128)}, f32[24,512]{1,0:T(8,128)S(1)}, u32[]{:S(2)}, u32[]{:S(2)}) collective-permute-start(f32[24,512]{1,0:T(8,128)} %get-tuple-element.22), channel_id=1, source_target_pairs={{0,4},{4,0},{8,12},{12,8},{1,5},{5,1},{9,13},{13,9},{2,6},{6,2},{1... | collective-permute-start | bytes 147464 | tf_op jit(solution)/shard_map/ppermute | solution.py:724
  5.8 6.1 %collective-permute-start = (f32[24,512]{1,0:T(8,128)}, f32[24,512]{1,0:T(8,128)S(1)}, u32[]{:S(2)}, u32[]{:S(2)}) collective-permute-start(f32[24,512]{1,0:T(8,128)} %get-tuple-element.19), channel_id=1, source_target_pairs={{0,8},{4,12},{8,0},{12,4},{1,9},{5,13},{9,1},{13,5},{2,10},{6,14},... | collective-permute-start | bytes 147464 | tf_op jit(solution)/shard_map/ppermute | solution.py:724
  8.4 4.0 %collective-permute-start.1 = (f32[24,512]{1,0:T(8,128)}, f32[24,512]{1,0:T(8,128)S(1)}, u32[]{:S(2)}, u32[]{:S(2)}) collective-permute-start(f32[24,512]{1,0:T(8,128)} %get-tuple-element.20), channel_id=1, source_target_pairs={{0,12},{4,8},{8,4},{12,0},{1,13},{5,9},{9,5},{13,1},{2,14},{6,10},... | collective-permute-start | bytes 147464 | tf_op jit(solution)/shard_map/ppermute | solution.py:724
  8.5 0.8 %copy-start.2 = (s32[1,1,8,512]{3,2,1,0:T(8,128)S(1)}, s32[1,1,8,512]{3,2,1,0:T(8,128)}, u32[]{:S(2)}) copy-start(s32[1,1,8,512]{3,2,1,0:T(8,128)} %param.12) | copy-start | bytes 49156
  9.2 0.7 %copy-start.3 = (f32[4,7]{1,0:T(4,128)S(1)}, f32[4,7]{1,0:T(4,128)}, u32[]{:S(2)}) copy-start(f32[4,7]{1,0:T(4,128)} %camera_ref.1) | copy-start | bytes 340
  9.2 0.7 %copy-start.4 = (s32[1,1,8]{2,1,0:T(1,128)S(1)}, s32[1,1,8]{2,1,0:T(1,128)}, u32[]{:S(2)}) copy-start(s32[1,1,8]{2,1,0:T(1,128)} %param.10) | copy-start | bytes 100
  9.3 0.7 %copy-start.5 = (s32[1,1,8]{2,1,0:T(1,128)S(1)}, s32[1,1,8]{2,1,0:T(1,128)}, u32[]{:S(2)}) copy-start(s32[1,1,8]{2,1,0:T(1,128)} %param.11) | copy-start | bytes 100
  23.0 1.9 %collective-permute-start.5 = (f32[24,512]{1,0:T(8,128)S(1)}, f32[24,512]{1,0:T(8,128)S(1)}, u32[]{:S(2)}, u32[]{:S(2)}) collective-permute-start(f32[24,512]{1,0:T(8,128)S(1)} %get-tuple-element.31), channel_id=1, source_target_pairs={{0,4},{4,0},{8,12},{12,8},{1,5},{5,1},{9,13},{13,9},{2,6},{6,2},{1... | collective-permute-start | bytes 147464 | tf_op jit(solution)/shard_map/ppermute | solution.py:724
  23.2 4.1 %collective-permute-start.3 = (f32[24,512]{1,0:T(8,128)S(1)}, f32[24,512]{1,0:T(8,128)S(1)}, u32[]{:S(2)}, u32[]{:S(2)}) collective-permute-start(f32[24,512]{1,0:T(8,128)S(1)} %get-tuple-element.27), channel_id=1, source_target_pairs={{0,8},{4,12},{8,0},{12,4},{1,9},{5,13},{9,1},{13,5},{2,10},{6,14},... | collective-permute-start | bytes 147464 | tf_op jit(solution)/shard_map/ppermute | solution.py:724
  24.7 0.7 %copy-start = (s32[1,1,4,512]{3,2,1,0:T(4,128)S(1)}, s32[1,1,4,512]{3,2,1,0:T(4,128)}, u32[]{:S(2)}) copy-start(s32[1,1,4,512]{3,2,1,0:T(4,128)} %param.9) | copy-start | bytes 24580
  24.7 4.0 %collective-permute-start.4 = (f32[24,512]{1,0:T(8,128)S(1)}, f32[24,512]{1,0:T(8,128)S(1)}, u32[]{:S(2)}, u32[]{:S(2)}) collective-permute-start(f32[24,512]{1,0:T(8,128)S(1)} %get-tuple-element.28), channel_id=1, source_target_pairs={{0,12},{4,8},{8,4},{12,0},{1,13},{5,9},{9,5},{13,1},{2,14},{6,10},... | collective-permute-start | bytes 147464 | tf_op jit(solution)/shard_map/ppermute | solution.py:724
  29.6 11.6 %collective-permute-start.6 = (f32[184,128]{1,0:T(8,128)S(1)}, f32[184,128]{1,0:T(8,128)S(1)}, u32[]{:S(2)}, u32[]{:S(2)}) collective-permute-start(f32[184,128]{1,0:T(8,128)S(1)} %get-tuple-element.32), channel_id=1, source_target_pairs={{0,2},{1,3},{2,0},{3,1},{4,6},{5,7},{6,4},{7,5},{8,10},{9,11},{10,... | collective-permute-start | bytes 282632 | tf_op jit(solution)/shard_map/ppermute | solution.py:724
  32.2 9.0 %collective-permute-start.7 = (f32[184,128]{1,0:T(8,128)S(1)}, f32[184,128]{1,0:T(8,128)S(1)}, u32[]{:S(2)}, u32[]{:S(2)}) collective-permute-start(f32[184,128]{1,0:T(8,128)S(1)} %get-tuple-element.33), channel_id=1, source_target_pairs={{0,3},{1,2},{2,1},{3,0},{4,7},{5,6},{6,5},{7,4},{8,11},{9,10},{10,... | collective-permute-start | bytes 282632 | tf_op jit(solution)/shard_map/ppermute | solution.py:724
  33.6 7.1 %collective-permute-start.8 = (f32[184,128]{1,0:T(8,128)S(1)}, f32[184,128]{1,0:T(8,128)S(1)}, u32[]{:S(2)}, u32[]{:S(2)}) collective-permute-start(f32[184,128]{1,0:T(8,128)S(1)} %get-tuple-element.35), channel_id=1, source_target_pairs={{0,1},{1,0},{2,3},{3,2},{4,5},{5,4},{6,7},{7,6},{8,9},{9,8},{10,11... | collective-permute-start | bytes 282632 | tf_op jit(solution)/shard_map/ppermute | solution.py:724
